TPU v7x, 512 devices: a whole 4x8x8 slice. The times are simulated.
512 devices in a mesh: face: 8 (over z_hi, x), row: 8 (over z_lo, core), col: 8 (over y).
Axes of the slice: x: 4, y: 8, z: 8 (z_hi: 2, z_lo: 4; z = z_hi * 4 + z_lo), core: 2. Of those that a mesh axis runs over, the one named last changes fastest.
Arguments:
- state: bfloat16 [8, 128, 128, 1024], P('face', None, 'row', 'col'), may hold values from -6 to 6
- conv_in: bfloat16 [5, 256, 128], replicated, may hold values from -0.1875 to 0.1875
- bias_in: float32 [256], replicated, may hold values from -3 to 3
- conv_out: bfloat16 [5, 128, 256], replicated, may hold values from -0.125 to 0.125
- bias_out: float32 [128], replicated, may hold values from -3 to 3
- land: int32 [8, 64], P('face'), may hold values from 0 to 1, as said below
- owner: int32 [8, 64], P('face'), may hold values from 0 to 31, as said below
Outputs:
- new_state: bfloat16 [8, 128, 128, 1024], P('face', None, 'row', 'col')
- ocean: bfloat16 [8, 64, 2, 4, 16, 128], P('face', ('row', 'col'))
Inputs may be any that keep to these rules, and one draw needn't show every extreme that they name: `land`: in every face the tiles owned by ocean device 0 are wet. `owner`: within a face each value 0 to 31 owns exactly two tiles, so no device owns more than 2 wet tiles, and device 0 of every face owns exactly 2; devices with index 32 or more own none.
All inputs are finite; a program needn't handle non-finite values.
Results may differ from a plain program's by a relative error of at most 0.0034.
Values may be sent and summed in bfloat16 or wider, within the bound.
No kernel may reach another device: no remote copies, remote signals or barrier semaphores. Data moves between devices by JAX's collectives and lax.ppermute only.
A program may use at most 64 MiB of HBM per device.

v0:
```python
import jax
import jax.numpy as jnp
from jax import lax
from jax.sharding import PartitionSpec as P

OC = 4
CAP = 2


OFFSETS = (
    (0, 0, 0),
    (0, 1, 1),
    (0, -1, 1),
    (1, 0, 2),
    (-1, 0, 2),
    (1, 1, 3),
    (-1, -1, 3),
    (1, -1, 4),
    (-1, 1, 4),
)


def swapped(array, axis, apart):
    return lax.ppermute(array, axis, [(i, i ^ 1 << apart) for i in range(lax.axis_size(axis))])


def extended(cells, sides, width):
    for axis, dim in sides:
        count = lax.axis_size(axis)
        ends = count - 1
        head = lax.slice_in_dim(cells, 0, width, axis=dim)
        tail = lax.slice_in_dim(cells, cells.shape[dim] - width, cells.shape[dim], axis=dim)
        cells = jnp.concatenate(
            [
                lax.ppermute(tail, axis, [(i, (i + 1) % count) for i in range(ends)]),
                cells,
                lax.ppermute(head, axis, [((i + 1) % count, i) for i in range(ends)]),
            ],
            axis=dim,
        )
    return cells


def conv_block(padded, weights):
    row_count = padded.shape[1] - 2
    col_count = padded.shape[2] - 2
    summed = jnp.zeros((weights.shape[1], row_count, col_count), jnp.float32)
    for row_step, col_step, tap_index in OFFSETS:
        shifted = padded[
            :, 1 + row_step : 1 + row_step + row_count, 1 + col_step : 1 + col_step + col_count
        ]
        summed = summed + jnp.einsum(
            "oi,irc->orc", weights[tap_index], shifted, preferred_element_type=jnp.float32
        )
    return summed


def extend(values, width):
    col_count = values.shape[2]
    east_strip = values[:, ::-1, col_count - width :][:, :, ::-1]
    west_strip = values[:, ::-1, :width][:, :, ::-1]
    for bit_number in range(lax.axis_size("row").bit_length() - 1):
        east_strip, west_strip = swapped((east_strip, west_strip), "row", bit_number)
    east_strip = swapped(east_strip, "face", 0)
    west_strip = swapped(west_strip, "face", 1)
    column = lax.axis_index("col")
    last_col = lax.axis_size("col") - 1
    widened = extended(values, (("col", 2),), width)
    widened = widened.at[:, :, col_count + width :].set(
        jnp.where(column == last_col, east_strip, widened[:, :, col_count + width :])
    )
    widened = widened.at[:, :, :width].set(
        jnp.where(column == 0, west_strip, widened[:, :, :width])
    )
    return extended(widened, (("row", 1),), width)


def local(state, conv_in, bias_in, conv_out, bias_out, land, owner):
    anchor = state[0]
    hidden = jax.nn.gelu(conv_block(extend(anchor, 1), conv_in) + bias_in[:, None, None]).astype(
        jnp.bfloat16
    )
    grown = extend(hidden, 1)
    new_state = (
        anchor.astype(jnp.float32) + conv_block(grown, conv_out) + bias_out[:, None, None]
    ).astype(jnp.bfloat16)
    wet_face = 1 - land[0]
    own_face = owner[0]
    tile_count = own_face.shape[0]
    order = jnp.arange(tile_count, dtype=jnp.int32)
    earlier = order[None, :] < order[:, None]
    same = (own_face[:, None] == own_face[None, :]) & (wet_face[None, :] == 1) & earlier
    slot_face = jnp.sum(same.astype(jnp.int32), axis=1)
    myself = lax.axis_index(("row", "col"))
    slot_ids = jnp.arange(CAP, dtype=jnp.int32)
    sea = new_state[:OC][None]
    chosen = (
        (wet_face[None, :] == 1)
        & (own_face[None, :] == myself)
        & (slot_face[None, :] == slot_ids[:, None])
    )
    chosen = chosen.astype(jnp.bfloat16)
    ocean = jnp.einsum(
        "sj,jabc->sabc",
        chosen,
        lax.all_gather(sea, ("row", "col"), axis=0, tiled=True),
        preferred_element_type=jnp.float32,
    )
    return (new_state[None], ocean.astype(jnp.bfloat16)[None, None])


def solution(mesh):
    in_specs = (P("face", None, "row", "col"), P(), P(), P(), P(), P("face", None), P("face", None))
    out_specs = (P("face", None, "row", "col"), P("face", ("row", "col"), None, None, None, None))
    return jax.shard_map(local, mesh=mesh, in_specs=in_specs, out_specs=out_specs, check_vma=False)
```

profile of v0, /device:TPU:1, one launch (start us, length us, event | category | flops | bytes accessed | tf_op | source)
XLA Modules:
  0.0 303.4 jit_solution(408178514764240853)
XLA Ops:
  7.2 0.0 all-gather.3.cloned.1.call-start
  7.2 1.5 copy.77
  8.8 8.8 %collective-permute-start.2 = (bf16[128,16,1]{0,2,1:T(2,128)(2,1)S(1)}, bf16[128,16,1]{0,2,1:T(2,128)(2,1)S(1)}, u32[]{:S(2)}, u32[]{:S(2)}) collective-permute-start(bf16[128,16,1]{0,2,1:T(2,128)(2,1)S(1)} %rev.12), channel_id=1, source_target_pairs={{0,8},{8,0},{16,24},{24,16},{32,40},{40,32},{48,56},{56,48},{1,9},... | collective-permute-start | bytes 12296 | tf_op jit(solution)/shard_map/ppermute | solution.py:24
  17.6 1.9 collective-permute-start.6
  19.5 1.9 collective-permute-start.3
  21.5 3.4 %collective-permute-start.7 = (bf16[128,16,1]{0,2,1:T(2,128)(2,1)S(1)}, bf16[128,16,1]{0,2,1:T(2,128)(2,1)S(1)}, u32[]{:S(2)}, u32[]{:S(2)}) collective-permute-start(bf16[128,16,1]{0,2,1:T(2,128)(2,1)S(1)} %collective-permute-done.6), channel_id=1, source_target_pairs={{0,16},{8,24},{16,0},{24,8},{32,48},{40,56},{48,32},{56,40},{1,17}... | collective-permute-start | bytes 12296 | tf_op jit(solution)/shard_map/ppermute | solution.py:24
  24.8 1.9 collective-permute-start.4
  26.8 2.4 collective-permute-start
  29.1 1.3 collective-permute-start.1
  30.4 3.2 %collective-permute-start.8 = (bf16[128,16,1]{0,2,1:T(2,128)(2,1)S(1)}, bf16[128,16,1]{0,2,1:T(2,128)(2,1)S(1)}, u32[]{:S(2)}, u32[]{:S(2)}) collective-permute-start(bf16[128,16,1]{0,2,1:T(2,128)(2,1)S(1)} %collective-permute-done.7), channel_id=1, source_target_pairs={{0,32},{8,40},{16,48},{24,56},{32,0},{40,8},{48,16},{56,24},{1,33}... | collective-permute-start | bytes 12296 | tf_op jit(solution)/shard_map/ppermute | solution.py:24
  33.7 1.9 collective-permute-start.5
  35.6 0.2 pad_maximum_fusion.5
  35.8 4.6 %collective-permute-start.9 = (bf16[128,16,1]{0,2,1:T(2,128)(2,1)S(1)}, bf16[128,16,1]{0,2,1:T(2,128)(2,1)S(1)}, u32[]{:S(2)}, u32[]{:S(2)}) collective-permute-start(bf16[128,16,1]{0,2,1:T(2,128)(2,1)S(1)} %collective-permute-done.8), channel_id=1, source_target_pairs={{0,128},{64,192},{128,0},{192,64},{256,384},{320,448},{384,256},{4... | collective-permute-start | bytes 12296 | tf_op jit(solution)/shard_map/ppermute | solution.py:24
  40.4 0.1 scatter.14
  40.5 1.2 collective-permute-done.9
  41.7 0.1 scatter.15
  41.8 7.1 %collective-permute-start.11 = (bf16[128,1,130]{0,2,1:T(8,128)(2,1)S(1)}, bf16[128,1,130]{0,2,1:T(8,128)(2,1)S(1)}, u32[]{:S(2)}, u32[]{:S(2)}) collective-permute-start(bf16[128,1,130]{0,2,1:T(8,128)(2,1)S(1)} %get-tuple-element.63), channel_id=1, source_target_pairs={{0,8},{8,16},{16,24},{24,32},{32,40},{40,48},{48,56},{1,9},{9,17},... | collective-permute-start | bytes 99848 | tf_op jit(solution)/shard_map/ppermute | solution.py:35
  48.9 0.4 fusion.62
  49.3 0.4 fusion.64
  49.8 1.9 collective-permute-start.10
  51.7 0.4 fusion.46
  52.2 0.4 fusion.54
  52.6 0.4 fusion.43
  53.0 2.0 collective-permute-done.10
  55.0 0.4 fusion.52
  55.5 0.0 copy-start.3
  55.5 0.4 fusion.56
  55.9 0.4 fusion.49
  56.4 1.5 fusion.7
  57.9 2.1 collective-permute-start.14
  60.0 2.4 collective-permute-start.18
  62.4 2.2 collective-permute-start.15
  64.7 3.1 %collective-permute-start.19 = (bf16[256,16,1]{0,2,1:T(2,128)(2,1)S(1)}, bf16[256,16,1]{0,2,1:T(2,128)(2,1)S(1)}, u32[]{:S(2)}, u32[]{:S(2)}) collective-permute-start(bf16[256,16,1]{0,2,1:T(2,128)(2,1)S(1)} %collective-permute-done.18), channel_id=1, source_target_pairs={{0,16},{8,24},{16,0},{24,8},{32,48},{40,56},{48,32},{56,40},{1,17}... | collective-permute-start | bytes 24584 | tf_op jit(solution)/shard_map/ppermute | solution.py:24
  67.8 3.7 %collective-permute-start.16 = (bf16[256,16,1]{0,2,1:T(2,128)(2,1)S(1)}, bf16[256,16,1]{0,2,1:T(2,128)(2,1)S(1)}, u32[]{:S(2)}, u32[]{:S(2)}) collective-permute-start(bf16[256,16,1]{0,2,1:T(2,128)(2,1)S(1)} %collective-permute-done.15), channel_id=1, source_target_pairs={{0,32},{8,40},{16,48},{24,56},{32,0},{40,8},{48,16},{56,24},{1,33}... | collective-permute-start | bytes 24584 | tf_op jit(solution)/shard_map/ppermute | solution.py:24
  71.4 4.2 %collective-permute-start.12 = (bf16[256,16,1]{0,2,1:T(2,128)(2,1)S(1)}, bf16[256,16,1]{0,2,1:T(2,128)(2,1)S(1)}, u32[]{:S(2)}, u32[]{:S(2)}) collective-permute-start(bf16[256,16,1]{0,2,1:T(2,128)(2,1)S(1)} %get-tuple-element.60), channel_id=1, source_target_pairs={{0,1},{1,2},{2,3},{3,4},{4,5},{5,6},{6,7},{8,9},{9,10},{10,11},{11... | collective-permute-start | bytes 24584 | tf_op jit(solution)/shard_map/ppermute | solution.py:35
  75.7 1.3 collective-permute-start.13
  77.0 2.5 collective-permute-start.20
  79.5 3.1 %collective-permute-start.17 = (bf16[256,16,1]{0,2,1:T(2,128)(2,1)S(1)}, bf16[256,16,1]{0,2,1:T(2,128)(2,1)S(1)}, u32[]{:S(2)}, u32[]{:S(2)}) collective-permute-start(bf16[256,16,1]{0,2,1:T(2,128)(2,1)S(1)} %collective-permute-done.16), channel_id=1, source_target_pairs={{0,64},{64,0},{128,192},{192,128},{256,320},{320,256},{384,448},{4... | collective-permute-start | bytes 24584 | tf_op jit(solution)/shard_map/ppermute | solution.py:24
  82.7 0.6 pad_maximum_fusion
  83.3 4.4 %collective-permute-start.21 = (bf16[256,16,1]{0,2,1:T(2,128)(2,1)S(1)}, bf16[256,16,1]{0,2,1:T(2,128)(2,1)S(1)}, u32[]{:S(2)}, u32[]{:S(2)}) collective-permute-start(bf16[256,16,1]{0,2,1:T(2,128)(2,1)S(1)} %collective-permute-done.20), channel_id=1, source_target_pairs={{0,128},{64,192},{128,0},{192,64},{256,384},{320,448},{384,256},{4... | collective-permute-start | bytes 24584 | tf_op jit(solution)/shard_map/ppermute | solution.py:24
  87.7 0.1 scatter.16
  87.8 1.5 collective-permute-done.21
  89.3 0.1 scatter.19
  89.4 4.7 %collective-permute-start.23 = (bf16[256,1,130]{0,2,1:T(8,128)(2,1)S(1)}, bf16[256,1,130]{0,2,1:T(8,128)(2,1)S(1)}, u32[]{:S(2)}, u32[]{:S(2)}) collective-permute-start(bf16[256,1,130]{0,2,1:T(8,128)(2,1)S(1)} %get-tuple-element.59), channel_id=1, source_target_pairs={{0,8},{8,16},{16,24},{24,32},{32,40},{40,48},{48,56},{1,9},{9,17},... | collective-permute-start | bytes 199688 | tf_op jit(solution)/shard_map/ppermute | solution.py:35
  94.2 0.4 fusion.36
  94.6 0.4 fusion.38
  95.1 2.1 collective-permute-start.22
  97.2 0.5 fusion.24
  97.7 0.4 fusion.32
  98.1 0.4 fusion.21
  98.5 2.1 collective-permute-done.22
  100.7 0.5 fusion.30
  101.2 0.0 copy-start.5
  101.2 0.4 fusion.34
  101.6 0.5 fusion.27
  102.1 0.0 copy-start.2
  102.1 0.8 fusion.18
  102.9 0.8 copy.96
  103.8 0.0 all-gather.3.cloned.1.call-update
  103.8 0.2 convert_reduce_fusion
  104.0 1.2 copy.98
  105.2 188.8 %all-gather.3.cloned.1.call-done = bf16[256,16,128]{2,1,0:T(8,128)(2,1)} async-done(((bf16[4,16,128]{2,1,0:T(8,128)(2,1)}), bf16[256,16,128]{2,1,0:T(8,128)(2,1)}) %all-gather.3.cloned.1.call-update) | async-done | bytes 1048592 | tf_op jit(solution)/shard_map/all_gather | solution.py:106
  294.0 1.9 fusion.19
  295.9 0.6 copy.99
  (42 shorter events, 0.3 us)
Async XLA Ops:
  7.2 41.7 %copy-start = (bf16[5,256,128]{2,1,0:T(8,128)(2,1)S(1)}, bf16[5,256,128]{2,1,0:T(8,128)(2,1)}, u32[]{:S(2)}) copy-start(bf16[5,256,128]{2,1,0:T(8,128)(2,1)} %param.16) | copy-start | bytes 983044
  7.2 286.8 %all-gather.3.cloned.1.call-start = ((), (), s32[]{:S(2)}) async-start(), calls=%async_computation | async-start | bytes 1064960 | tf_op jit(solution)/shard_map/all_gather | solution.py:106
  8.8 10.7 %collective-permute-start.2 = (bf16[128,16,1]{0,2,1:T(2,128)(2,1)S(1)}, bf16[128,16,1]{0,2,1:T(2,128)(2,1)S(1)}, u32[]{:S(2)}, u32[]{:S(2)}) collective-permute-start(bf16[128,16,1]{0,2,1:T(2,128)(2,1)S(1)} %rev.12), channel_id=1, source_target_pairs={{0,8},{8,0},{16,24},{24,16},{32,40},{40,32},{48,56},{56,48},{1,9},... | collective-permute-start | bytes 12296 | tf_op jit(solution)/shard_map/ppermute | solution.py:24
  17.6 3.9 %collective-permute-start.6 = (bf16[128,16,1]{0,2,1:T(2,128)(2,1)S(1)}, bf16[128,16,1]{0,2,1:T(2,128)(2,1)S(1)}, u32[]{:S(2)}, u32[]{:S(2)}) collective-permute-start(bf16[128,16,1]{0,2,1:T(2,128)(2,1)S(1)} %rev.13), channel_id=1, source_target_pairs={{0,8},{8,0},{16,24},{24,16},{32,40},{40,32},{48,56},{56,48},{1,9},... | collective-permute-start | bytes 12296 | tf_op jit(solution)/shard_map/ppermute | solution.py:24
  19.5 5.3 %collective-permute-start.3 = (bf16[128,16,1]{0,2,1:T(2,128)(2,1)S(1)}, bf16[128,16,1]{0,2,1:T(2,128)(2,1)S(1)}, u32[]{:S(2)}, u32[]{:S(2)}) collective-permute-start(bf16[128,16,1]{0,2,1:T(2,128)(2,1)S(1)} %collective-permute-done.2), channel_id=1, source_target_pairs={{0,16},{8,24},{16,0},{24,8},{32,48},{40,56},{48,32},{56,40},{1,17}... | collective-permute-start | bytes 12296 | tf_op jit(solution)/shard_map/ppermute | solution.py:24
  21.5 9.0 %collective-permute-start.7 = (bf16[128,16,1]{0,2,1:T(2,128)(2,1)S(1)}, bf16[128,16,1]{0,2,1:T(2,128)(2,1)S(1)}, u32[]{:S(2)}, u32[]{:S(2)}) collective-permute-start(bf16[128,16,1]{0,2,1:T(2,128)(2,1)S(1)} %collective-permute-done.6), channel_id=1, source_target_pairs={{0,16},{8,24},{16,0},{24,8},{32,48},{40,56},{48,32},{56,40},{1,17}... | collective-permute-start | bytes 12296 | tf_op jit(solution)/shard_map/ppermute | solution.py:24
  24.8 8.8 %collective-permute-start.4 = (bf16[128,16,1]{0,2,1:T(2,128)(2,1)S(1)}, bf16[128,16,1]{0,2,1:T(2,128)(2,1)S(1)}, u32[]{:S(2)}, u32[]{:S(2)}) collective-permute-start(bf16[128,16,1]{0,2,1:T(2,128)(2,1)S(1)} %collective-permute-done.3), channel_id=1, source_target_pairs={{0,32},{8,40},{16,48},{24,56},{32,0},{40,8},{48,16},{56,24},{1,33}... | collective-permute-start | bytes 12296 | tf_op jit(solution)/shard_map/ppermute | solution.py:24
  26.8 8.8 %collective-permute-start = (bf16[128,16,1]{0,2,1:T(2,128)(2,1)S(1)}, bf16[128,16,1]{0,2,1:T(2,128)(2,1)S(1)}, u32[]{:S(2)}, u32[]{:S(2)}) collective-permute-start(bf16[128,16,1]{0,2,1:T(2,128)(2,1)S(1)} %get-tuple-element.64), channel_id=1, source_target_pairs={{0,1},{1,2},{2,3},{3,4},{4,5},{5,6},{6,7},{8,9},{9,10},{10,11},{11... | collective-permute-start | bytes 12296 | tf_op jit(solution)/shard_map/ppermute | solution.py:35
  29.1 6.5 %collective-permute-start.1 = (bf16[128,16,1]{0,2,1:T(2,128)(2,1)S(1)}, bf16[128,16,1]{0,2,1:T(2,128)(2,1)S(1)}, u32[]{:S(2)}, u32[]{:S(2)}) collective-permute-start(bf16[128,16,1]{0,2,1:T(2,128)(2,1)S(1)} %get-tuple-element.65), channel_id=1, source_target_pairs={{1,0},{2,1},{3,2},{4,3},{5,4},{6,5},{7,6},{9,8},{10,9},{11,10},{12... | collective-permute-start | bytes 12296 | tf_op jit(solution)/shard_map/ppermute | solution.py:37
  30.4 5.3 %collective-permute-start.8 = (bf16[128,16,1]{0,2,1:T(2,128)(2,1)S(1)}, bf16[128,16,1]{0,2,1:T(2,128)(2,1)S(1)}, u32[]{:S(2)}, u32[]{:S(2)}) collective-permute-start(bf16[128,16,1]{0,2,1:T(2,128)(2,1)S(1)} %collective-permute-done.7), channel_id=1, source_target_pairs={{0,32},{8,40},{16,48},{24,56},{32,0},{40,8},{48,16},{56,24},{1,33}... | collective-permute-start | bytes 12296 | tf_op jit(solution)/shard_map/ppermute | solution.py:24
  33.7 6.7 %collective-permute-start.5 = (bf16[128,16,1]{0,2,1:T(2,128)(2,1)S(1)}, bf16[128,16,1]{0,2,1:T(2,128)(2,1)S(1)}, u32[]{:S(2)}, u32[]{:S(2)}) collective-permute-start(bf16[128,16,1]{0,2,1:T(2,128)(2,1)S(1)} %collective-permute-done.4), channel_id=1, source_target_pairs={{0,64},{64,0},{128,192},{192,128},{256,320},{320,256},{384,448},{4... | collective-permute-start | bytes 12296 | tf_op jit(solution)/shard_map/ppermute | solution.py:24
  35.8 5.9 %collective-permute-start.9 = (bf16[128,16,1]{0,2,1:T(2,128)(2,1)S(1)}, bf16[128,16,1]{0,2,1:T(2,128)(2,1)S(1)}, u32[]{:S(2)}, u32[]{:S(2)}) collective-permute-start(bf16[128,16,1]{0,2,1:T(2,128)(2,1)S(1)} %collective-permute-done.8), channel_id=1, source_target_pairs={{0,128},{64,192},{128,0},{192,64},{256,384},{320,448},{384,256},{4... | collective-permute-start | bytes 12296 | tf_op jit(solution)/shard_map/ppermute | solution.py:24
  41.8 9.9 %collective-permute-start.11 = (bf16[128,1,130]{0,2,1:T(8,128)(2,1)S(1)}, bf16[128,1,130]{0,2,1:T(8,128)(2,1)S(1)}, u32[]{:S(2)}, u32[]{:S(2)}) collective-permute-start(bf16[128,1,130]{0,2,1:T(8,128)(2,1)S(1)} %get-tuple-element.63), channel_id=1, source_target_pairs={{0,8},{8,16},{16,24},{24,32},{32,40},{40,48},{48,56},{1,9},{9,17},... | collective-permute-start | bytes 99848 | tf_op jit(solution)/shard_map/ppermute | solution.py:35
  49.8 5.3 %collective-permute-start.10 = (bf16[128,1,130]{0,2,1:T(8,128)(2,1)S(1)}, bf16[128,1,130]{0,2,1:T(8,128)(2,1)S(1)}, u32[]{:S(2)}, u32[]{:S(2)}) collective-permute-start(bf16[128,1,130]{0,2,1:T(8,128)(2,1)S(1)} %get-tuple-element.62), channel_id=1, source_target_pairs={{8,0},{16,8},{24,16},{32,24},{40,32},{48,40},{56,48},{9,1},{17,9},... | collective-permute-start | bytes 99848 | tf_op jit(solution)/shard_map/ppermute | solution.py:37
  55.5 0.9 copy-start.3
  57.9 36.3 %copy-start.1 = (bf16[5,128,256]{2,1,0:T(8,128)(2,1)S(1)}, bf16[5,128,256]{2,1,0:T(8,128)(2,1)}, u32[]{:S(2)}) copy-start(bf16[5,128,256]{2,1,0:T(8,128)(2,1)} %param.18) | copy-start | bytes 983044
  57.9 4.5 %collective-permute-start.14 = (bf16[256,16,1]{0,2,1:T(2,128)(2,1)S(1)}, bf16[256,16,1]{0,2,1:T(2,128)(2,1)S(1)}, u32[]{:S(2)}, u32[]{:S(2)}) collective-permute-start(bf16[256,16,1]{0,2,1:T(2,128)(2,1)S(1)} %rev.14), channel_id=1, source_target_pairs={{0,8},{8,0},{16,24},{24,16},{32,40},{40,32},{48,56},{56,48},{1,9},... | collective-permute-start | bytes 24584 | tf_op jit(solution)/shard_map/ppermute | solution.py:24
  60.0 4.6 %collective-permute-start.18 = (bf16[256,16,1]{0,2,1:T(2,128)(2,1)S(1)}, bf16[256,16,1]{0,2,1:T(2,128)(2,1)S(1)}, u32[]{:S(2)}, u32[]{:S(2)}) collective-permute-start(bf16[256,16,1]{0,2,1:T(2,128)(2,1)S(1)} %rev.15), channel_id=1, source_target_pairs={{0,8},{8,0},{16,24},{24,16},{32,40},{40,32},{48,56},{56,48},{1,9},... | collective-permute-start | bytes 24584 | tf_op jit(solution)/shard_map/ppermute | solution.py:24
  62.4 5.3 %collective-permute-start.15 = (bf16[256,16,1]{0,2,1:T(2,128)(2,1)S(1)}, bf16[256,16,1]{0,2,1:T(2,128)(2,1)S(1)}, u32[]{:S(2)}, u32[]{:S(2)}) collective-permute-start(bf16[256,16,1]{0,2,1:T(2,128)(2,1)S(1)} %collective-permute-done.14), channel_id=1, source_target_pairs={{0,16},{8,24},{16,0},{24,8},{32,48},{40,56},{48,32},{56,40},{1,17}... | collective-permute-start | bytes 24584 | tf_op jit(solution)/shard_map/ppermute | solution.py:24
  64.7 12.3 %collective-permute-start.19 = (bf16[256,16,1]{0,2,1:T(2,128)(2,1)S(1)}, bf16[256,16,1]{0,2,1:T(2,128)(2,1)S(1)}, u32[]{:S(2)}, u32[]{:S(2)}) collective-permute-start(bf16[256,16,1]{0,2,1:T(2,128)(2,1)S(1)} %collective-permute-done.18), channel_id=1, source_target_pairs={{0,16},{8,24},{16,0},{24,8},{32,48},{40,56},{48,32},{56,40},{1,17}... | collective-permute-start | bytes 24584 | tf_op jit(solution)/shard_map/ppermute | solution.py:24
  67.8 11.8 %collective-permute-start.16 = (bf16[256,16,1]{0,2,1:T(2,128)(2,1)S(1)}, bf16[256,16,1]{0,2,1:T(2,128)(2,1)S(1)}, u32[]{:S(2)}, u32[]{:S(2)}) collective-permute-start(bf16[256,16,1]{0,2,1:T(2,128)(2,1)S(1)} %collective-permute-done.15), channel_id=1, source_target_pairs={{0,32},{8,40},{16,48},{24,56},{32,0},{40,8},{48,16},{56,24},{1,33}... | collective-permute-start | bytes 24584 | tf_op jit(solution)/shard_map/ppermute | solution.py:24
  71.4 11.3 %collective-permute-start.12 = (bf16[256,16,1]{0,2,1:T(2,128)(2,1)S(1)}, bf16[256,16,1]{0,2,1:T(2,128)(2,1)S(1)}, u32[]{:S(2)}, u32[]{:S(2)}) collective-permute-start(bf16[256,16,1]{0,2,1:T(2,128)(2,1)S(1)} %get-tuple-element.60), channel_id=1, source_target_pairs={{0,1},{1,2},{2,3},{3,4},{4,5},{5,6},{6,7},{8,9},{9,10},{10,11},{11... | collective-permute-start | bytes 24584 | tf_op jit(solution)/shard_map/ppermute | solution.py:35
  75.7 7.0 %collective-permute-start.13 = (bf16[256,16,1]{0,2,1:T(2,128)(2,1)S(1)}, bf16[256,16,1]{0,2,1:T(2,128)(2,1)S(1)}, u32[]{:S(2)}, u32[]{:S(2)}) collective-permute-start(bf16[256,16,1]{0,2,1:T(2,128)(2,1)S(1)} %get-tuple-element.61), channel_id=1, source_target_pairs={{1,0},{2,1},{3,2},{4,3},{5,4},{6,5},{7,6},{9,8},{10,9},{11,10},{12... | collective-permute-start | bytes 24584 | tf_op jit(solution)/shard_map/ppermute | solution.py:37
  77.0 6.3 %collective-permute-start.20 = (bf16[256,16,1]{0,2,1:T(2,128)(2,1)S(1)}, bf16[256,16,1]{0,2,1:T(2,128)(2,1)S(1)}, u32[]{:S(2)}, u32[]{:S(2)}) collective-permute-start(bf16[256,16,1]{0,2,1:T(2,128)(2,1)S(1)} %collective-permute-done.19), channel_id=1, source_target_pairs={{0,32},{8,40},{16,48},{24,56},{32,0},{40,8},{48,16},{56,24},{1,33}... | collective-permute-start | bytes 24584 | tf_op jit(solution)/shard_map/ppermute | solution.py:24
  79.5 8.1 %collective-permute-start.17 = (bf16[256,16,1]{0,2,1:T(2,128)(2,1)S(1)}, bf16[256,16,1]{0,2,1:T(2,128)(2,1)S(1)}, u32[]{:S(2)}, u32[]{:S(2)}) collective-permute-start(bf16[256,16,1]{0,2,1:T(2,128)(2,1)S(1)} %collective-permute-done.16), channel_id=1, source_target_pairs={{0,64},{64,0},{128,192},{192,128},{256,320},{320,256},{384,448},{4... | collective-permute-start | bytes 24584 | tf_op jit(solution)/shard_map/ppermute | solution.py:24
  83.3 6.0 %collective-permute-start.21 = (bf16[256,16,1]{0,2,1:T(2,128)(2,1)S(1)}, bf16[256,16,1]{0,2,1:T(2,128)(2,1)S(1)}, u32[]{:S(2)}, u32[]{:S(2)}) collective-permute-start(bf16[256,16,1]{0,2,1:T(2,128)(2,1)S(1)} %collective-permute-done.20), channel_id=1, source_target_pairs={{0,128},{64,192},{128,0},{192,64},{256,384},{320,448},{384,256},{4... | collective-permute-start | bytes 24584 | tf_op jit(solution)/shard_map/ppermute | solution.py:24
  89.4 7.7 %collective-permute-start.23 = (bf16[256,1,130]{0,2,1:T(8,128)(2,1)S(1)}, bf16[256,1,130]{0,2,1:T(8,128)(2,1)S(1)}, u32[]{:S(2)}, u32[]{:S(2)}) collective-permute-start(bf16[256,1,130]{0,2,1:T(8,128)(2,1)S(1)} %get-tuple-element.59), channel_id=1, source_target_pairs={{0,8},{8,16},{16,24},{24,32},{32,40},{40,48},{48,56},{1,9},{9,17},... | collective-permute-start | bytes 199688 | tf_op jit(solution)/shard_map/ppermute | solution.py:35
  95.1 5.6 %collective-permute-start.22 = (bf16[256,1,130]{0,2,1:T(8,128)(2,1)S(1)}, bf16[256,1,130]{0,2,1:T(8,128)(2,1)S(1)}, u32[]{:S(2)}, u32[]{:S(2)}) collective-permute-start(bf16[256,1,130]{0,2,1:T(8,128)(2,1)S(1)} %get-tuple-element.58), channel_id=1, source_target_pairs={{8,0},{16,8},{24,16},{32,24},{40,32},{48,40},{56,48},{9,1},{17,9},... | collective-permute-start | bytes 199688 | tf_op jit(solution)/shard_map/ppermute | solution.py:37
  101.2 0.9 copy-start.5
  102.1 1.7 copy-start.2
  102.1 1.7 copy-start.4
Sparse Core Ops, SparseCore 0:
  103.9 190.0 all-gather.2
where the time goes:
time: 306 us; the launch traced here: 303 us
  waiting for transfers between devices  196 us (64%)
  starting transfers between devices  76.1 us (25%)
  between operations  14.7 us (5%)
  matrix products  11.2 us (4%)
  local copies, waits for them, and re-layouts  4.58 us (1%)
    all_gather x1, waiting for transfers between devices, local(): lax.all_gather(sea, ('row', 'col'), axis=0, tiled=True)  189 us
    ppermute x16, starting transfers between devices, swapped(): lax.ppermute(array, axis, [(i, i ^ 1 << apart) for i in range(lax.axis_si...  51 us
    ppermute x4, starting transfers between devices, extended(): lax.ppermute(tail, axis, [(i, (i + 1) % count) for i in range(ends)])  18.4 us
    dot_general x18, matrix products, conv_block(): jnp.einsum('oi,irc->orc', weights[tap_index], shifted, preferred_element_...  9.34 us
    ppermute x4, starting transfers between devices, extended(): lax.ppermute(head, axis, [((i + 1) % count, i) for i in range(ends)])  6.61 us
  transfers between devices with their start and end apart: 25, of which 5 were waited for; matrix products, arithmetic and copies ran while one was open for 2% of the time, Pallas kernels for 0%

commit v1 on v0

v1 whole, which is shorter than its diff:
```python
import jax
import jax.numpy as jnp
from jax import lax
from jax.sharding import PartitionSpec as P

OC = 4
CAP = 2
ALL = ("face", "row", "col")
CLASSES = ((3, 2, 4), (1, 0, 1), (4, 2, 3))


def exchange(values, partner):
    shape = tuple(lax.axis_size(a) for a in ALL)
    number = lambda f, r, c: (f * shape[1] + r) * shape[2] + c
    pairs = []
    for f in range(shape[0]):
        for r in range(shape[1]):
            for c in range(shape[2]):
                other = partner(f, r, c, shape)
                if other is not None:
                    pairs.append((number(f, r, c), number(*other)))
    return lax.ppermute(values, ALL, pairs)


def col_near(f, r, c, shape):
    return (f, r, c ^ 1)


def col_far(f, r, c, shape):
    if c == 0:
        return (f ^ 2, shape[1] - 1 - r, c)
    if c == shape[2] - 1:
        return (f ^ 1, shape[1] - 1 - r, c)
    return (f, r, ((c + 1) ^ 1) - 1)


def row_near(f, r, c, shape):
    return (f, r ^ 1, c)


def row_far(f, r, c, shape):
    return None if r in (0, shape[1] - 1) else (f, ((r + 1) ^ 1) - 1, c)


def extend(values, width):
    r, c = lax.axis_index("row"), lax.axis_index("col")
    east, west = values[:, :, -width:], values[:, :, :width]
    odd = c % 2 == 1
    flip = lambda v: v[:, ::-1, ::-1]
    far = jnp.where(odd, east, west)
    at_seam = (c == 0) | (c == lax.axis_size("col") - 1)
    far = jnp.where(at_seam, flip(far), far)
    got_far = exchange(far, col_far)
    got_near = exchange(jnp.where(odd, west, east), col_near)
    wide = jnp.concatenate(
        [jnp.where(odd, got_near, got_far), values, jnp.where(odd, got_far, got_near)], axis=2
    )
    top, bottom = wide[:, :width], wide[:, -width:]
    odd = r % 2 == 1
    got_far = exchange(jnp.where(odd, bottom, top), row_far)
    got_near = exchange(jnp.where(odd, top, bottom), row_near)
    return jnp.concatenate(
        [jnp.where(odd, got_near, got_far), wide, jnp.where(odd, got_far, got_near)], axis=1
    )


def conv(padded, weights):
    kernel = jnp.stack([jnp.stack([weights[t] for t in row], axis=-1) for row in CLASSES], axis=-2)
    return lax.conv_general_dilated(
        padded[None],
        kernel,
        (1, 1),
        "VALID",
        dimension_numbers=("NCHW", "OIHW", "NCHW"),
        preferred_element_type=jnp.float32,
    )[0]


def relay(sea, land, owner):
    rows, cols = lax.axis_size("row"), lax.axis_size("col")
    r, c = lax.axis_index("row"), lax.axis_index("col")
    wet = land[0] == 0
    owner = owner[0]
    order = jnp.arange(owner.shape[0], dtype=jnp.int32)
    same = (owner[:, None] == owner[None, :]) & wet[None, :] & (order[None, :] < order[:, None])
    slot = jnp.sum(same.astype(jnp.int32), axis=1)
    mine = r * cols + c
    to_col = wet[mine] & (owner[mine] % cols == jnp.arange(cols))
    sent = jnp.where(to_col[:, None, None, None], sea[None], jnp.zeros_like(sea)[None])
    held = lax.all_to_all(sent, "col", 0, 0, tiled=True)
    row_owner = lax.dynamic_slice_in_dim(owner, r * cols, cols)
    row_wet = lax.dynamic_slice_in_dim(wet, r * cols, cols)
    row_slot = lax.dynamic_slice_in_dim(slot, r * cols, cols)
    place = jnp.where(row_wet & (row_owner % cols == c), row_owner // cols * CAP + row_slot, -1)
    chosen = (place[None, :] == jnp.arange(rows * CAP)[:, None]).astype(jnp.bfloat16)
    sent = jnp.einsum("pj,jabc->pabc", chosen, held, preferred_element_type=jnp.float32)
    sent = sent.astype(jnp.bfloat16).reshape((rows, CAP) + sea.shape)
    got = lax.all_to_all(sent, "row", 0, 0, tiled=True)
    return jnp.sum(got.astype(jnp.float32), axis=0).astype(jnp.bfloat16)


def local(state, conv_in, bias_in, conv_out, bias_out, land, owner):
    anchor = state[0]
    r = lax.axis_index("row")
    hidden = jax.nn.gelu(conv(extend(anchor, 2), conv_in) + bias_in[:, None, None])
    height = hidden.shape[1]
    index = jnp.arange(height)
    inside = ((r > 0) | (index > 0)) & ((r < lax.axis_size("row") - 1) | (index < height - 1))
    hidden = jnp.where(inside[None, :, None], hidden, 0).astype(jnp.bfloat16)
    new_state = anchor.astype(jnp.float32) + conv(hidden, conv_out) + bias_out[:, None, None]
    new_state = new_state.astype(jnp.bfloat16)
    return (new_state[None], relay(new_state[:OC], land, owner)[None, None])


def solution(mesh):
    in_specs = (P("face", None, "row", "col"), P(), P(), P(), P(), P("face", None), P("face", None))
    out_specs = (P("face", None, "row", "col"), P("face", ("row", "col"), None, None, None, None))
    return jax.shard_map(local, mesh=mesh, in_specs=in_specs, out_specs=out_specs, check_vma=False)
```

time: 306 us -> 63.4 us (0.21)
  waiting for transfers between devices: 196 us -> 17.5 us
  starting transfers between devices: 76.1 us -> 25.1 us
  between operations: 14.7 us -> 2.93 us
  matrix products: 11.2 us -> 5.77 us
  local copies, waits for them, and re-layouts: 4.58 us -> 8.71 us
    all_gather x1 -> x0, waiting for transfers between devices: 189 us -> none  [local(): lax.all_gather(sea, ('row', 'col'), axis=0, tiled=True)]
    ppermute x24 -> x4, starting transfers between devices: 76.1 us -> 17.2 us  [exchange(): return lax.ppermute(values, ALL, pairs)]
    all_to_all x0 -> x2, waiting for transfers between devices: none -> 16.4 us  [the longest x1 9.28 us: relay(): held = lax.all_to_all(sent, 'col', 0, 0, tiled=True)]
    dot_general x19 -> x1, matrix products: 11.2 us -> 0.34 us  [relay(): jnp.einsum('pj,jabc->pabc', chosen, held, preferred_element_type=jnp.floa...]
    all_to_all x0 -> x2, starting transfers between devices: none -> 7.88 us  [the longest x1 4.1 us: relay(): held = lax.all_to_all(sent, 'col', 0, 0, tiled=True)]
    ppermute x24 -> x4, waiting for transfers between devices: 6.91 us -> 1.1 us  [exchange(): return lax.ppermute(values, ALL, pairs)]
    conv_general_dilated x0 -> x2, matrix products: none -> 5.42 us  [conv(): lax.conv_general_dilated(padded[None], kernel, (1, 1), 'VALID', dimension...]
  transfers between devices with their start and end apart: 25 -> 6, of which waited for: 5 -> 3; matrix products, arithmetic and copies ran while one was open for 2% -> 6% of each run, Pallas kernels for 0% -> 0%
where the time goes in v1:
time: 63.4 us; the launch traced here: 63 us
  starting transfers between devices  25.1 us (40%)
  waiting for transfers between devices  17.5 us (28%)
  local copies, waits for them, and re-layouts  8.71 us (14%)
  matrix products  5.77 us (9%)
  other arithmetic  2.99 us (5%)
  between operations  2.93 us (5%)
    ppermute x4, starting transfers between devices, exchange(): return lax.ppermute(values, ALL, pairs)  17.2 us
    all_to_all x1, waiting for transfers between devices, relay(): held = lax.all_to_all(sent, 'col', 0, 0, tiled=True)  9.28 us
    all_to_all x1, waiting for transfers between devices, relay(): got = lax.all_to_all(sent, 'row', 0, 0, tiled=True)  7.08 us
    unnamed x17, local copies, waits for them, and re-layouts  5.49 us
    conv_general_dilated x2, matrix products, conv(): lax.conv_general_dilated(padded[None], kernel, (1, 1), 'VALID', dimension...  5.42 us
    all_to_all x1, starting transfers between devices, relay(): held = lax.all_to_all(sent, 'col', 0, 0, tiled=True)  4.1 us
    all_to_all x1, starting transfers between devices, relay(): got = lax.all_to_all(sent, 'row', 0, 0, tiled=True)  3.78 us
  transfers between devices with their start and end apart: 6, of which 3 were waited for; matrix products, arithmetic and copies ran while one was open for 6% of the time, Pallas kernels for 0%

profile of v1, /device:TPU:1, one launch (start us, length us, event | category | flops | bytes accessed | tf_op | source)
XLA Modules:
  0.0 63.0 jit_solution(5336455374934631021)
XLA Ops:
  0.6 0.0 copy-start
  0.6 0.0 copy-start.1
  0.7 0.0 copy-start.5
  0.7 1.8 %copy.27 = bf16[1,128,16,128]{1,2,3,0:T(8,128)(2,1)S(1)} copy(bf16[1,128,16,128]{3,2,1,0:T(8,128)(2,1)} %param.7) | data formatting | bytes 1048576 | tf_op args[0]
  2.5 11.5 %collective-permute-start.1 = (bf16[128,16,2]{0,1,2:T(8,128)(2,1)S(1)}, bf16[128,16,2]{0,1,2:T(8,128)(2,1)S(1)}, u32[]{:S(2)}, u32[]{:S(2)}) collective-permute-start(bf16[128,16,2]{0,1,2:T(8,128)(2,1)S(1)} %broadcast_select_fusion.5), channel_id=1, source_target_pairs={{0,184},{1,2},{2,1},{3,4},{4,3},{5,6},{6,5},{7,127},{8,176},{9,10}... | collective-permute-start | bytes 24584 | tf_op jit(solution)/shard_map/ppermute | solution.py:22
  14.0 1.9 %collective-permute-start = (bf16[128,16,2]{0,1,2:T(8,128)(2,1)S(1)}, bf16[128,16,2]{0,1,2:T(8,128)(2,1)S(1)}, u32[]{:S(2)}, u32[]{:S(2)}) collective-permute-start(bf16[128,16,2]{0,1,2:T(8,128)(2,1)S(1)} %get-tuple-element.11), channel_id=1, source_target_pairs={{0,1},{1,0},{2,3},{3,2},{4,5},{5,4},{6,7},{7,6},{8,9},{9,8},{10,11... | collective-permute-start | bytes 24584 | tf_op jit(solution)/shard_map/ppermute | solution.py:22
  15.9 0.0 copy-done
  16.0 0.0 copy-done.1
  16.0 0.0 copy-start.2
  16.0 0.0 copy-done.5
  16.1 0.1 fusion.47
  16.1 0.1 fusion.43
  16.2 0.4 copy-done.2
  16.6 0.6 constant_dynamic-slice_fusion
  19.2 0.6 constant_dynamic-slice_fusion.1
  19.8 0.0 collective-permute-done.1
  19.8 0.0 collective-permute-done
  19.8 0.1 broadcast_select_fusion.3
  20.0 1.9 %collective-permute-start.3 = (bf16[128,2,132]{0,1,2:T(2,128)(2,1)S(1)}, bf16[128,2,132]{0,1,2:T(2,128)(2,1)S(1)}, u32[]{:S(2)}, u32[]{:S(2)}) collective-permute-start(bf16[128,2,132]{0,1,2:T(2,128)(2,1)S(1)} %bitcast.95), channel_id=1, source_target_pairs={{8,16},{9,17},{10,18},{11,19},{12,20},{13,21},{14,22},{15,23},{16,... | collective-permute-start | bytes 202760 | tf_op jit(solution)/shard_map/ppermute | solution.py:22
  21.9 1.9 %collective-permute-start.2 = (bf16[128,2,132]{0,1,2:T(2,128)(2,1)S(1)}, bf16[128,2,132]{0,1,2:T(2,128)(2,1)S(1)}, u32[]{:S(2)}, u32[]{:S(2)}) collective-permute-start(bf16[128,2,132]{0,1,2:T(2,128)(2,1)S(1)} %get-tuple-element.8), channel_id=1, source_target_pairs={{0,8},{1,9},{2,10},{3,11},{4,12},{5,13},{6,14},{7,15},{8,0},{9,1},... | collective-permute-start | bytes 202760 | tf_op jit(solution)/shard_map/ppermute | solution.py:22
  23.8 0.7 %compare_and_fusion = pred[8]{0:T(512)(128)(4,1)S(1)} fusion(pred[]{:T(512)} %bitcast.30, s32[]{:T(128)S(6)} %select_n.114), kind=kLoop, calls=%fused_computation.94 | loop fusion | flops 16 | bytes 13 | tf_op jit(solution)/shard_map/and | solution.py:88
  24.5 1.1 %collective-permute-done.3 = bf16[128,2,132]{0,1,2:T(2,128)(2,1)S(1)} collective-permute-done((bf16[128,2,132]{0,1,2:T(2,128)(2,1)S(1)}, bf16[128,2,132]{0,1,2:T(2,128)(2,1)S(1)}, u32[]{:S(2)}, u32[]{:S(2)}) %collective-permute-start.3) | collective-permute-done | bytes 67616 | tf_op jit(solution)/shard_map/ppermute | solution.py:22
  25.6 0.0 collective-permute-done.2
  25.6 0.5 maximum_bitcast_fusion
  26.1 0.2 pad
  26.3 0.0 copy-start.4
  26.3 0.0 copy-start.6
  26.3 0.1 copy.30
  26.4 0.5 copy-done.4
  26.9 0.0 copy-done.6
  27.0 2.5 %fusion.19 = bf16[18,1,8,17,256]{4,2,3,0,1:T(8,128)(2,1)S(1)} fusion(f32[256]{0:T(256)S(1)} %copy-done.4, pred[18]{0:T(512)(128)(4,1)S(1)} %or_and_fusion, pred[8,17]{0,1:T(8,128)(4,1)S(1)} %copy-done.6, bf16[128,20,1,7,2]{0,3,4,1,2:T(8,128)(2,1)S(1)} %slice.73, bf16[128,20,1,8,17]{0,3,4,1,2:T(8,128)(2,1)S(1)} %copy.30, ...), kind=kOutput, calls=%fused_computation.21 | convolution fusion | flops 1454960640 | bytes 2612378 | tf_op jit(solution)/shard_map/conv_general_dilated | solution.py:69
  29.5 2.9 %fusion.13 = f32[16,8,17,128]{3,1,2,0:T(8,128)S(1)} fusion(bf16[18,1,7,2,256]{4,2,3,0,1:T(8,128)(2,1)S(1)} %slice.74, bf16[18,1,8,17,256]{4,2,3,0,1:T(8,128)(2,1)S(1)} %fusion.19, bf16[128,256,1,3]{1,0,3,2:T(8,128)(2,1)S(1)} %get-tuple-element.24, bf16[128,256,1,3]{1,0,3,2:T(8,128)(2,1)S(1)} %get-tuple-element.34, ...), kind=kOutput, calls=%fused_computation.16 | convolution fusion | flops 1288249344 | bytes 3086336 | tf_op jit(solution)/shard_map/conv_general_dilated | solution.py:69
  32.4 0.2 copy.31
  32.7 0.0 copy-start.3
  32.7 0.1 slice_bitcast_fusion
  32.8 0.6 copy-done.3
  33.3 0.1 fusion.21
  33.5 0.5 copy.32
  33.9 0.7 %broadcast_select_fusion.4 = bf16[8,4,16,128]{3,2,1,0:T(8,128)(2,1)} fusion(pred[8]{0:T(512)(128)(4,1)S(1)} %compare_and_fusion, bf16[4,16,128]{2,1,0:T(8,128)(2,1)S(1)} %copy.32), kind=kLoop, calls=%fused_computation.67 | loop fusion | flops 65536 | bytes 147464 | tf_op jit(solution)/shard_map/jit(_where)/select_n | solution.py:89
  34.7 4.1 %all-to-all-start = ((bf16[8,4,16,128]{3,2,1,0:T(8,128)(2,1)}), bf16[8,4,16,128]{3,2,1,0:T(8,128)(2,1)S(1)}, u32[]{:S(2)}, u32[]{:S(2)}) async-start(bf16[8,4,16,128]{3,2,1,0:T(8,128)(2,1)} %broadcast_select_fusion.4), calls=%async_computation | async-start | bytes 262144 | tf_op jit(solution)/shard_map/all_to_all | solution.py:90
  38.8 0.2 convert_reduce_fusion
  38.9 0.1 fusion.55
  39.0 9.3 %all-to-all-done = bf16[8,4,16,128]{3,2,1,0:T(8,128)(2,1)S(1)} async-done(((bf16[8,4,16,128]{3,2,1,0:T(8,128)(2,1)}), bf16[8,4,16,128]{3,2,1,0:T(8,128)(2,1)S(1)}, u32[]{:S(2)}, u32[]{:S(2)}) %all-to-all-start) | async-done | bytes 131104 | tf_op jit(solution)/shard_map/all_to_all | solution.py:90
  48.3 0.3 convolution_convert_fusion
  48.7 0.9 %copy.34 = bf16[8,2,4,16,128]{4,1,3,2,0:T(2,128)(2,1)} copy(bf16[8,2,4,16,128]{4,1,0,3,2:T(2,128)(2,1)S(1)} %bitcast.89) | data formatting | bytes 524288 | tf_op jit(solution)/shard_map/reshape | solution.py:97
  49.6 3.8 %all-to-all-start.1 = ((bf16[8,2,4,16,128]{4,1,3,2,0:T(2,128)(2,1)}), bf16[8,2,4,16,128]{4,1,3,2,0:T(2,128)(2,1)S(1)}, u32[]{:S(2)}, u32[]{:S(2)}) async-start(bf16[8,2,4,16,128]{4,1,3,2,0:T(2,128)(2,1)} %copy.34), calls=%async_computation.1 | async-start | bytes 524288 | tf_op jit(solution)/shard_map/all_to_all | solution.py:98
  53.4 0.1 fusion.23
  53.5 1.5 %copy.36 = bf16[1,128,16,128]{3,2,1,0:T(8,128)(2,1)} copy(bf16[1,128,16,128]{1,2,3,0:T(8,128)(2,1)S(1)} %fusion.23) | data formatting | bytes 1048576
  55.0 7.1 %all-to-all-done.1 = bf16[8,2,4,16,128]{4,1,3,2,0:T(2,128)(2,1)S(1)} async-done(((bf16[8,2,4,16,128]{4,1,3,2,0:T(2,128)(2,1)}), bf16[8,2,4,16,128]{4,1,3,2,0:T(2,128)(2,1)S(1)}, u32[]{:S(2)}, u32[]{:S(2)}) %all-to-all-start.1) | async-done | bytes 262176 | tf_op jit(solution)/shard_map/all_to_all | solution.py:98
  62.1 0.2 reduce_sum.22
  62.3 0.6 copy.37
  (12 shorter events, 0.2 us)
Async XLA Ops:
  0.6 15.3 %copy-start = (bf16[5,256,128]{2,1,0:T(8,128)(2,1)S(1)}, bf16[5,256,128]{2,1,0:T(8,128)(2,1)}, u32[]{:S(2)}) copy-start(bf16[5,256,128]{2,1,0:T(8,128)(2,1)} %param.8) | copy-start | bytes 983044
  0.6 15.3 %copy-start.1 = (bf16[5,128,256]{2,1,0:T(8,128)(2,1)S(1)}, bf16[5,128,256]{2,1,0:T(8,128)(2,1)}, u32[]{:S(2)}) copy-start(bf16[5,128,256]{2,1,0:T(8,128)(2,1)} %param.10) | copy-start | bytes 983044
  0.7 15.4 %copy-start.5 = (s32[1,64]{1,0:T(1,128)S(1)}, s32[1,64]{1,0:T(1,128)}, u32[]{:S(2)}) copy-start(s32[1,64]{1,0:T(1,128)} %param.12) | copy-start | bytes 772
  2.5 17.3 %collective-permute-start.1 = (bf16[128,16,2]{0,1,2:T(8,128)(2,1)S(1)}, bf16[128,16,2]{0,1,2:T(8,128)(2,1)S(1)}, u32[]{:S(2)}, u32[]{:S(2)}) collective-permute-start(bf16[128,16,2]{0,1,2:T(8,128)(2,1)S(1)} %broadcast_select_fusion.5), channel_id=1, source_target_pairs={{0,184},{1,2},{2,1},{3,4},{4,3},{5,6},{6,5},{7,127},{8,176},{9,10}... | collective-permute-start | bytes 24584 | tf_op jit(solution)/shard_map/ppermute | solution.py:22
  14.0 5.8 %collective-permute-start = (bf16[128,16,2]{0,1,2:T(8,128)(2,1)S(1)}, bf16[128,16,2]{0,1,2:T(8,128)(2,1)S(1)}, u32[]{:S(2)}, u32[]{:S(2)}) collective-permute-start(bf16[128,16,2]{0,1,2:T(8,128)(2,1)S(1)} %get-tuple-element.11), channel_id=1, source_target_pairs={{0,1},{1,0},{2,3},{3,2},{4,5},{5,4},{6,7},{7,6},{8,9},{9,8},{10,11... | collective-permute-start | bytes 24584 | tf_op jit(solution)/shard_map/ppermute | solution.py:22
  16.0 0.7 %copy-start.2 = (s32[1,64]{1,0:T(1,128)S(1)}, s32[1,64]{1,0:T(1,128)}, u32[]{:S(2)}) copy-start(s32[1,64]{1,0:T(1,128)} %param.13) | copy-start | bytes 772
  20.0 5.6 %collective-permute-start.3 = (bf16[128,2,132]{0,1,2:T(2,128)(2,1)S(1)}, bf16[128,2,132]{0,1,2:T(2,128)(2,1)S(1)}, u32[]{:S(2)}, u32[]{:S(2)}) collective-permute-start(bf16[128,2,132]{0,1,2:T(2,128)(2,1)S(1)} %bitcast.95), channel_id=1, source_target_pairs={{8,16},{9,17},{10,18},{11,19},{12,20},{13,21},{14,22},{15,23},{16,... | collective-permute-start | bytes 202760 | tf_op jit(solution)/shard_map/ppermute | solution.py:22
  21.9 3.7 %collective-permute-start.2 = (bf16[128,2,132]{0,1,2:T(2,128)(2,1)S(1)}, bf16[128,2,132]{0,1,2:T(2,128)(2,1)S(1)}, u32[]{:S(2)}, u32[]{:S(2)}) collective-permute-start(bf16[128,2,132]{0,1,2:T(2,128)(2,1)S(1)} %get-tuple-element.8), channel_id=1, source_target_pairs={{0,8},{1,9},{2,10},{3,11},{4,12},{5,13},{6,14},{7,15},{8,0},{9,1},... | collective-permute-start | bytes 202760 | tf_op jit(solution)/shard_map/ppermute | solution.py:22
  26.3 0.7 %copy-start.4 = (f32[256]{0:T(256)S(1)}, f32[256]{0:T(256)}, u32[]{:S(2)}) copy-start(f32[256]{0:T(256)} %param.9) | copy-start | bytes 3076
  26.3 0.7 %copy-start.6 = (pred[8,17]{0,1:T(8,128)(4,1)S(1)}, pred[8,17]{0,1:T(8,128)(4,1)}, u32[]{:S(2)}) copy-start(pred[8,17]{0,1:T(8,128)(4,1)} %constant.93) | copy-start | bytes 412
  32.7 0.7 %copy-start.3 = (f32[128]{0:T(128)S(1)}, f32[128]{0:T(128)}, u32[]{:S(2)}) copy-start(f32[128]{0:T(128)} %param.11) | copy-start | bytes 1540
  34.7 13.7 %all-to-all-start = ((bf16[8,4,16,128]{3,2,1,0:T(8,128)(2,1)}), bf16[8,4,16,128]{3,2,1,0:T(8,128)(2,1)S(1)}, u32[]{:S(2)}, u32[]{:S(2)}) async-start(bf16[8,4,16,128]{3,2,1,0:T(8,128)(2,1)} %broadcast_select_fusion.4), calls=%async_computation | async-start | bytes 262144 | tf_op jit(solution)/shard_map/all_to_all | solution.py:90
  49.6 12.5 %all-to-all-start.1 = ((bf16[8,2,4,16,128]{4,1,3,2,0:T(2,128)(2,1)}), bf16[8,2,4,16,128]{4,1,3,2,0:T(2,128)(2,1)S(1)}, u32[]{:S(2)}, u32[]{:S(2)}) async-start(bf16[8,2,4,16,128]{4,1,3,2,0:T(2,128)(2,1)} %copy.34), calls=%async_computation.1 | async-start | bytes 524288 | tf_op jit(solution)/shard_map/all_to_all | solution.py:98

commit v2 on v1

v2 whole, which is shorter than its diff:
```python
import jax
import jax.numpy as jnp
from jax import lax
from jax.experimental import pallas as pl
from jax.experimental.pallas import tpu as pltpu
from jax.sharding import PartitionSpec as P

OC = 4
CAP = 2
ALL = ("face", "row", "col")
BORDER = 2

PITCH = 144
TAPS = (3, 2, 4, 1, 0, 1, 4, 2, 3)
NT = (((1,), (1,)), ((), ()))
VM = pl.BlockSpec(memory_space=pltpu.VMEM)
SM = pl.BlockSpec(memory_space=pltpu.SMEM)
PARAMS = pltpu.CompilerParams(vmem_limit_bytes=28 * 2**20)


def turn_kernel(state, cells, edges, flat, turned):
    chans, rows, cols = state.shape
    flat[...] = state[...].reshape(chans * rows, cols).astype(jnp.float32)
    for r in range(rows):
        turned[r] = flat[pl.ds(r, chans, stride=rows), :].T
        cells[r] = turned[r].astype(jnp.bfloat16)
    for k, w in enumerate((0, 1, cols - 2, cols - 1)):
        edges[k] = turned.reshape(rows * cols, chans)[pl.ds(w, rows, stride=cols), :].astype(jnp.bfloat16)


def turn(state):
    chans, rows, cols = state.shape
    return pl.pallas_call(
        turn_kernel,
        out_shape=[jax.ShapeDtypeStruct((rows, cols, chans), jnp.bfloat16), jax.ShapeDtypeStruct((4, rows, chans), jnp.bfloat16)],
        in_specs=[VM], out_specs=[VM, VM],
        scratch_shapes=[pltpu.VMEM((chans * rows, cols), jnp.float32), pltpu.VMEM((rows, cols, chans), jnp.float32)],
        compiler_params=PARAMS,
    )(state)


def hidden_kernel(flags, cells, sides, above, below, conv_in, bias_in, conv_out, bias_sea, state, hidden, blocks, field, taps):
    rows, cols, chans = cells.shape
    hid = bias_in.shape[1]
    f32 = jnp.float32
    for r in range(rows):
        field[2 + r, 8 : 8 + cols] = cells[r].astype(f32)
    side = sides[...].astype(f32)
    for k, s in enumerate((6, 7, 8 + cols, 9 + cols)):
        for r in range(rows):
            field[2 + r, s : s + 1] = side[k, r : r + 1]
    for start, strip in ((0, above), (2 + rows, below)):
        v = strip[...].astype(f32)
        for j in range(2):
            field[start + j, 8 : 8 + cols] = v[j * cols : (j + 1) * cols]
            for k, s in enumerate((6, 7, 8 + cols, 9 + cols)):
                at = 2 * cols + 4 * j + k
                field[start + j, s : s + 1] = v[at : at + 1]
    for r in range(rows + 4):
        for k in range(3):
            taps[r, :, k * chans : (k + 1) * chans] = field[r, 6 + k : 6 + k + PITCH].astype(jnp.bfloat16)
    weights = jnp.concatenate([conv_in[t] for t in TAPS], axis=1)
    step = 3
    for j in range(0, rows + 2, step):
        data = jnp.concatenate([taps[j + d : j + d + step].reshape(step * PITCH, 3 * chans) for d in range(3)], axis=1)
        x = lax.dot_general(data, weights, NT, preferred_element_type=f32) + bias_in[...]
        x = jax.nn.gelu(x).reshape(step, PITCH, hid)
        for d in range(step):
            y = x[d]
            if j + d == 0:
                y = jnp.where(flags[0] == 0, 0.0, y)
            if j + d == rows + 1:
                y = jnp.where(flags[1] == 0, 0.0, y)
            hidden[j + d] = y.astype(jnp.bfloat16)
    sea_weights = conv_out[:, 0:16].reshape(5 * 16, hid)
    z = []
    for j in range(0, rows + 2, 2):
        two = lax.dot_general(sea_weights, hidden[j : j + 2].reshape(2 * PITCH, hid), NT, preferred_element_type=f32)
        z += [two[:, :PITCH], two[:, PITCH:]]
    cut = lambda j, t: z[j][16 * t : 16 * t + 8]
    count = blocks.shape[1]
    for r in range(rows):
        j = r + 1
        mid = cut(j, 0) + cut(j - 1, 2) + cut(j + 1, 2)
        plus = cut(j, 1) + cut(j + 1, 3) + cut(j - 1, 4)
        minus = cut(j, 1) + cut(j - 1, 3) + cut(j + 1, 4)
        total = mid[:, 1 : 1 + cols] + plus[:, 2 : 2 + cols] + minus[:, :cols] + bias_sea[...]
        field[0:8, r] = total
    for o in range(count):
        v = field[o, 0:rows] [:, :cols] + state[o].astype(f32)
        v = v.astype(jnp.bfloat16)
        for b in range(blocks.shape[0]):
            blocks[b, o] = jnp.where(flags[2] == b, v, jnp.zeros_like(v))


def first_half(flags, cells, sides, above, below, conv_in, bias_in, conv_out, bias_sea, state, n_blocks, n_sea):
    rows, cols, chans = cells.shape
    hid = conv_in.shape[1]
    return pl.pallas_call(
        hidden_kernel,
        out_shape=[
            jax.ShapeDtypeStruct((rows + 2, PITCH, hid), jnp.bfloat16),
            jax.ShapeDtypeStruct((n_blocks, n_sea, rows, cols), jnp.bfloat16),
        ],
        in_specs=[SM] + [VM] * 9,
        out_specs=[VM, VM],
        scratch_shapes=[
            pltpu.VMEM((rows + 4, PITCH + 8, chans), jnp.float32),
            pltpu.VMEM((rows + 4, PITCH, 3 * chans), jnp.bfloat16),
        ],
        compiler_params=PARAMS,
        cost_estimate=pl.CostEstimate(flops=2 * 2592 * 1152 * 256, bytes_accessed=3_000_000, transcendentals=2592 * 256),
    )(flags, cells, sides, above, below, conv_in, bias_in, conv_out, bias_sea, state)


def out_kernel(hidden, cells, conv_out, bias_out, new_state, z, flat):
    rows, cols, chans = cells.shape
    hid = hidden.shape[2]
    f32 = jnp.float32
    weights = conv_out[...].reshape(5 * chans, hid)
    step = 3
    for j in range(0, rows + 2, step):
        data = hidden[j : j + step].reshape(step * PITCH, hid)
        z[j : j + step] = lax.dot_general(data, weights, NT, preferred_element_type=f32).reshape(step, PITCH, 5 * chans)
    cut = lambda j, t, s: z[j, s : s + cols, t * chans : (t + 1) * chans]
    for r in range(rows):
        j = r + 1
        total = cut(j, 0, 1) + cut(j - 1, 2, 1) + cut(j + 1, 2, 1)
        total += cut(j, 1, 2) + cut(j + 1, 3, 2) + cut(j - 1, 4, 2)
        total += cut(j, 1, 0) + cut(j - 1, 3, 0) + cut(j + 1, 4, 0)
        total += bias_out[...] + cells[r].astype(f32)
        flat[pl.ds(r, chans, stride=rows), :] = total.T
    new_state[...] = flat[...].reshape(chans, rows, cols).astype(jnp.bfloat16)


def second_half(hidden, cells, conv_out, bias_out):
    rows, cols, chans = cells.shape
    return pl.pallas_call(
        out_kernel,
        out_shape=jax.ShapeDtypeStruct((chans, rows, cols), jnp.bfloat16),
        in_specs=[VM] * 4,
        out_specs=VM,
        scratch_shapes=[pltpu.VMEM((rows + 2, PITCH, 5 * chans), jnp.float32), pltpu.VMEM((chans * rows, cols), jnp.float32)],
        compiler_params=PARAMS,
        cost_estimate=pl.CostEstimate(flops=2 * 2592 * 640 * 256, bytes_accessed=2_500_000, transcendentals=0),
    )(hidden, cells, conv_out, bias_out)


def exchange(values, partner):
    shape = tuple(lax.axis_size(a) for a in ALL)
    number = lambda f, r, c: (f * shape[1] + r) * shape[2] + c
    pairs = []
    for f in range(shape[0]):
        for r in range(shape[1]):
            for c in range(shape[2]):
                other = partner(f, r, c, shape)
                if other is not None:
                    pairs.append((number(f, r, c), number(*other)))
    return lax.ppermute(values, ALL, pairs)


def col_near(f, r, c, shape):
    return (f, r, c ^ 1)


def col_far(f, r, c, shape):
    if c == 0:
        return (f ^ 2, shape[1] - 1 - r, c)
    if c == shape[2] - 1:
        return (f ^ 1, shape[1] - 1 - r, c)
    return (f, r, ((c + 1) ^ 1) - 1)


def row_near(f, r, c, shape):
    return (f, r ^ 1, c)


def row_far(f, r, c, shape):
    return None if r in (0, shape[1] - 1) else (f, ((r + 1) ^ 1) - 1, c)


def sort_kernel(place, held, sent):
    sent[...] = jnp.zeros_like(sent)
    for k in range(held.shape[0]):

        @pl.when(place[k] >= 0)
        def _():
            sent[pl.ds(place[k], 1)] = held[k][None]


def sort_tiles(place, held, count):
    return pl.pallas_call(
        sort_kernel,
        out_shape=jax.ShapeDtypeStruct((count,) + held.shape[1:], held.dtype),
        in_specs=[SM, VM],
        out_specs=VM,
        compiler_params=PARAMS,
    )(place, held)


def merge_kernel(got, ocean):
    total = got[0].astype(jnp.float32)
    for k in range(1, got.shape[0]):
        total += got[k].astype(jnp.float32)
    ocean[...] = total.astype(ocean.dtype)


def merge(got):
    return pl.pallas_call(
        merge_kernel,
        out_shape=jax.ShapeDtypeStruct(got.shape[1:], got.dtype),
        in_specs=[VM],
        out_specs=VM,
        compiler_params=PARAMS,
    )(got)


def routes(land, owner):
    rows, cols = lax.axis_size("row"), lax.axis_size("col")
    r, c = lax.axis_index("row"), lax.axis_index("col")
    wet = land[0] == 0
    owner = owner[0]
    order = jnp.arange(owner.shape[0], dtype=jnp.int32)
    same = (owner[:, None] == owner[None, :]) & wet[None, :] & (order[None, :] < order[:, None])
    slot = jnp.sum(same.astype(jnp.int32), axis=1)
    mine = (order == r * cols + c) & wet
    to_col = jnp.sum(jnp.where(mine, owner % cols + 1, 0)) - 1
    place = jnp.where(wet & (owner % cols == c), owner // cols * CAP + slot, -1)
    place = lax.dynamic_slice_in_dim(place, r * cols, cols)
    return to_col, jnp.where(place < rows * CAP, place, -1)


def local(state, conv_in, bias_in, conv_out, bias_out, land, owner):
    state = state[0]
    chans, height, width = state.shape
    rows, cols = lax.axis_size("row"), lax.axis_size("col")
    r, c = lax.axis_index("row"), lax.axis_index("col")
    cells, edges = turn(state)

    odd = c % 2 == 1
    west, east = edges[:BORDER], edges[BORDER:]
    flip = lambda v: v[::-1, ::-1]
    far = jnp.where(odd, east, west)
    far = jnp.where((c == 0) | (c == cols - 1), flip(far), far)
    got_far = exchange(far, col_far)
    got_near = exchange(jnp.where(odd, west, east), col_near)
    sides = jnp.concatenate([jnp.where(odd, got_near, got_far), jnp.where(odd, got_far, got_near)])

    odd = r % 2 == 1

    def strip(start):
        corners = sides[:, start : start + BORDER].transpose(1, 0, 2)
        body = cells[start : start + BORDER].reshape(BORDER * width, chans)
        return jnp.concatenate([body, corners.reshape(2 * BORDER * BORDER, chans)])

    top, bottom = strip(0), strip(height - BORDER)
    got_far = exchange(jnp.where(odd, bottom, top), row_far)
    got_near = exchange(jnp.where(odd, top, bottom), row_near)
    above, below = jnp.where(odd, got_near, got_far), jnp.where(odd, got_far, got_near)

    to_col, place = routes(land, owner)
    flags = jnp.stack([r > 0, r < rows - 1, to_col]).astype(jnp.int32)
    hidden, blocks = first_half(
        flags, cells, sides, above, below, conv_in, bias_in[None], conv_out, bias_out[:8, None], state, cols, OC
    )
    held = lax.all_to_all(blocks, "col", 0, 0, tiled=True)
    new_state = second_half(hidden, cells, conv_out, bias_out[None])
    sent = sort_tiles(place, held, rows * CAP).reshape((rows, CAP, OC, height, width))
    got = lax.all_to_all(sent, "row", 0, 0, tiled=True)
    return (new_state[None], merge(got)[None, None])


def solution(mesh):
    in_specs = (P("face", None, "row", "col"), P(), P(), P(), P(), P("face", None), P("face", None))
    out_specs = (P("face", None, "row", "col"), P("face", ("row", "col"), None, None, None, None))
    return jax.shard_map(local, mesh=mesh, in_specs=in_specs, out_specs=out_specs, check_vma=False)
```

time: 63.4 us -> 59.1 us (0.932)
  Pallas kernels: 0 us -> 9.55 us
  local copies, waits for them, and re-layouts: 8.71 us -> 1.84 us
  matrix products: 5.77 us -> 0 us
  between operations: 2.93 us -> 1.47 us
    pallas_call x0 -> x5, Pallas kernels: none -> 9.55 us  [the longest x1 4.75 us: first_half(): pl.pallas_call(hidden_kernel, out_shape=[jax.ShapeDtypeStruct((rows + 2,...]
    conv_general_dilated x2 -> x0, matrix products: 5.42 us -> none  [conv(): lax.conv_general_dilated(padded[None], kernel, (1, 1), 'VALID', dimension...]
    unnamed x17 -> x12, local copies, waits for them, and re-layouts: 5.49 us -> 1.06 us
    dynamic_slice x2 -> x0, local copies, waits for them, and re-layouts: 1.17 us -> none  [relay(): to_col = wet[mine] & (owner[mine] % cols == jnp.arange(cols))]
    reshape x1 -> x0, local copies, waits for them, and re-layouts: 0.92 us -> none  [relay(): sent = sent.astype(jnp.bfloat16).reshape((rows, CAP) + sea.shape)]
    and x3 -> x0, other arithmetic: 0.67 us -> none  [the longest x1 0.65 us: relay(): to_col = wet[mine] & (owner[mine] % cols == jnp.arange(cols))]
    eq x0 -> x1, other arithmetic: none -> 0.66 us  [routes(): wet = land[0] == 0]
    ppermute x4, waiting for transfers between devices: 1.1 us -> 1.74 us  [exchange(): return lax.ppermute(values, ALL, pairs)]
  transfers between devices with their start and end apart: 6 -> 6, of which waited for: 3 -> 3; matrix products, arithmetic and copies ran while one was open for 6% -> 6% of each run, Pallas kernels for 0% -> 4%
where the time goes in v2:
time: 59.1 us; the launch traced here: 58.7 us
  starting transfers between devices  25.1 us (42%)
  waiting for transfers between devices  17.6 us (30%)
  Pallas kernels  9.55 us (16%)
  other arithmetic  3.15 us (5%)
  local copies, waits for them, and re-layouts  1.84 us (3%)
  between operations  1.47 us (2%)
    ppermute x4, starting transfers between devices, exchange(): return lax.ppermute(values, ALL, pairs)  17.2 us
    all_to_all x1, waiting for transfers between devices, local(): held = lax.all_to_all(blocks, 'col', 0, 0, tiled=True)  9.49 us
    all_to_all x1, waiting for transfers between devices, local(): got = lax.all_to_all(sent, 'row', 0, 0, tiled=True)  6.34 us
    pallas_call x1, Pallas kernels, first_half(): pl.pallas_call(hidden_kernel, out_shape=[jax.ShapeDtypeStruct((rows + 2,...  4.75 us
    all_to_all x1, starting transfers between devices, local(): held = lax.all_to_all(blocks, 'col', 0, 0, tiled=True)  4.11 us
    all_to_all x1, starting transfers between devices, local(): got = lax.all_to_all(sent, 'row', 0, 0, tiled=True)  3.77 us
    pallas_call x1, Pallas kernels, second_half(): pl.pallas_call(out_kernel, out_shape=jax.ShapeDtypeStruct((chans, rows, c...  2.39 us
    ppermute x4, waiting for transfers between devices, exchange(): return lax.ppermute(values, ALL, pairs)  1.74 us
  transfers between devices with their start and end apart: 6, of which 3 were waited for; matrix products, arithmetic and copies ran while one was open for 6% of the time, Pallas kernels for 4%

profile of v2, /device:TPU:1, one launch (start us, length us, event | category | flops | bytes accessed | tf_op | source)
XLA Modules:
  0.0 58.7 jit_solution(17920454627907916590)
XLA Ops:
  0.6 0.0 copy-start.4
  0.7 0.0 copy-start
  0.7 1.0 %copy-done = bf16[1,128,16,128]{3,2,1,0:T(8,128)(2,1)S(1)} copy-done((bf16[1,128,16,128]{3,2,1,0:T(8,128)(2,1)S(1)}, bf16[1,128,16,128]{3,2,1,0:T(8,128)(2,1)}, u32[]{:S(2)}) %copy-start) | copy-done | bytes 524312
  1.7 0.0 copy-start.1
  1.7 0.0 copy-start.2
  1.7 0.0 copy-start.3
  1.7 0.4 shard_map.86
  2.2 11.5 %collective-permute-start.1 = (bf16[2,16,128]{2,1,0:T(8,128)(2,1)S(1)}, bf16[2,16,128]{2,1,0:T(8,128)(2,1)S(1)}, u32[]{:S(2)}, u32[]{:S(2)}) collective-permute-start(bf16[2,16,128]{2,1,0:T(8,128)(2,1)S(1)} %broadcast_select_fusion.4), channel_id=1, source_target_pairs={{0,184},{1,2},{2,1},{3,4},{4,3},{5,6},{6,5},{7,127},{8,176},{9,10}... | collective-permute-start | bytes 24584 | tf_op jit(solution)/shard_map/ppermute | solution.py:159
  13.7 1.9 %collective-permute-start = (bf16[2,16,128]{2,1,0:T(8,128)(2,1)S(1)}, bf16[2,16,128]{2,1,0:T(8,128)(2,1)S(1)}, u32[]{:S(2)}, u32[]{:S(2)}) collective-permute-start(bf16[2,16,128]{2,1,0:T(8,128)(2,1)S(1)} %get-tuple-element.20), channel_id=1, source_target_pairs={{0,1},{1,0},{2,3},{3,2},{4,5},{5,4},{6,7},{7,6},{8,9},{9,8},{10,11... | collective-permute-start | bytes 24584 | tf_op jit(solution)/shard_map/ppermute | solution.py:159
  15.6 0.7 %slice_bitcast_fusion = f32[8,1]{0,1:T(1,128)S(1)} fusion(f32[128]{0:T(128)} %param.11), kind=kLoop, calls=%fused_computation.33 | loop fusion | bytes 64 | tf_op jit(solution)/shard_map/broadcast_in_dim | solution.py:264
  16.3 0.7 %compare_bitcast_fusion = pred[64]{0:T(512)(128)(4,1)S(1)} fusion(s32[1,64]{1,0:T(1,128)} %param.12), kind=kLoop, calls=%fused_computation.28 | loop fusion | flops 64 | bytes 320 | tf_op jit(solution)/shard_map/eq | solution.py:221
  16.9 0.9 %convert_reduce_fusion = s32[64]{0:T(128)S(1)} fusion(s32[64]{0:T(128)} %bitcast.41, pred[64]{0:T(512)(128)(4,1)S(1)} %compare_bitcast_fusion), kind=kLoop, calls=%fused_computation.6 | loop fusion | flops 24512 | bytes 576 | tf_op jit(solution)/shard_map/reduce_sum | solution.py:225
  17.9 1.3 %and_select_fusion.1 = (s32[64]{0:T(128)S(1)}, s32[]{:T(128)}) fusion(s32[64]{0:T(128)S(1)} %convert_reduce_fusion, s32[]{:T(128)S(6)} %axis_index.33, s32[1,64]{1,0:T(1,128)} %param.13, s32[1,64]{1,0:T(1,128)} %param.12, s32[]{:T(128)S(6)} %add.32), kind=kLoop, calls=%fused_computation.25 | loop fusion | flops 1919 | bytes 1036 | tf_op jit(solution)/shard_map/jit(_where)/select_n | solution.py:228
  19.8 0.1 pad_add_fusion.flags
  19.9 0.1 copy.14.bias_sea
  20.0 0.0 collective-permute-done.1
  20.0 0.0 collective-permute-done
  20.1 1.9 %collective-permute-start.3 = (bf16[264,128]{1,0:T(8,128)(2,1)S(1)}, bf16[264,128]{1,0:T(8,128)(2,1)S(1)}, u32[]{:S(2)}, u32[]{:S(2)}) collective-permute-start(bf16[264,128]{1,0:T(8,128)(2,1)S(1)} %get-tuple-element.14), channel_id=1, source_target_pairs={{8,16},{9,17},{10,18},{11,19},{12,20},{13,21},{14,22},{15,23},{16,... | collective-permute-start | bytes 202760 | tf_op jit(solution)/shard_map/ppermute | solution.py:159
  22.0 1.9 %collective-permute-start.2 = (bf16[264,128]{1,0:T(8,128)(2,1)S(1)}, bf16[264,128]{1,0:T(8,128)(2,1)S(1)}, u32[]{:S(2)}, u32[]{:S(2)}) collective-permute-start(bf16[264,128]{1,0:T(8,128)(2,1)S(1)} %get-tuple-element.15), channel_id=1, source_target_pairs={{0,8},{1,9},{2,10},{3,11},{4,12},{5,13},{6,14},{7,15},{8,0},{9,1},... | collective-permute-start | bytes 202760 | tf_op jit(solution)/shard_map/ppermute | solution.py:159
  24.0 1.7 %collective-permute-done.3 = bf16[264,128]{1,0:T(8,128)(2,1)S(1)} collective-permute-done((bf16[264,128]{1,0:T(8,128)(2,1)S(1)}, bf16[264,128]{1,0:T(8,128)(2,1)S(1)}, u32[]{:S(2)}, u32[]{:S(2)}) %collective-permute-start.3) | collective-permute-done | bytes 67616 | tf_op jit(solution)/shard_map/ppermute | solution.py:159
  25.7 0.0 collective-permute-done.2
  25.7 0.0 copy-done.4
  25.7 0.0 copy-done.1
  25.8 0.0 copy-done.2
  25.8 0.0 copy-done.3
  25.8 0.0 copy-start.5
  25.8 4.8 %shard_map.87 = (bf16[18,144,256]{2,1,0:T(8,128)(2,1)S(1)}, bf16[8,4,16,128]{3,2,1,0:T(8,128)(2,1)}) custom-call(s32[3]{0:T(128)S(1)} %pad_add_fusion.flags, bf16[16,128,128]{2,1,0:T(8,128)(2,1)S(1)} %get-tuple-element.6.cells, bf16[4,16,128]{2,1,0:T(8,128)(2,1)S(1)} %pad_maximum_fusion.2.sides, bf16[264,128]{1,0:T(8,128)(2,1)S(1)} %get-tuple-element.13.above, ...), custom_call_target="tpu_custom_call" | custom-call | flops 1528823808 | bytes 3000000 | tf_op jit(solution)/shard_map/pallas_call | solution.py:99
  30.5 4.1 %all-to-all-start = ((bf16[8,4,16,128]{3,2,1,0:T(8,128)(2,1)}), bf16[8,4,16,128]{3,2,1,0:T(8,128)(2,1)S(1)}, u32[]{:S(2)}, u32[]{:S(2)}) async-start(bf16[8,4,16,128]{3,2,1,0:T(8,128)(2,1)} %get-tuple-element.9), calls=%async_computation | async-start | bytes 262144 | tf_op jit(solution)/shard_map/all_to_all | solution.py:266
  34.6 0.1 compare_select_fusion.place
  34.7 9.5 %all-to-all-done.held = bf16[8,4,16,128]{3,2,1,0:T(8,128)(2,1)S(1)} async-done(((bf16[8,4,16,128]{3,2,1,0:T(8,128)(2,1)}), bf16[8,4,16,128]{3,2,1,0:T(8,128)(2,1)S(1)}, u32[]{:S(2)}, u32[]{:S(2)}) %all-to-all-start) | async-done | bytes 131104 | tf_op jit(solution)/shard_map/all_to_all | solution.py:266
  44.2 1.3 %shard_map.89 = bf16[16,4,16,128]{3,2,1,0:T(8,128)(2,1)} custom-call(s32[8]{0:T(128)S(1)} %compare_select_fusion.place, bf16[8,4,16,128]{3,2,1,0:T(8,128)(2,1)S(1)} %all-to-all-done.held), custom_call_target="tpu_custom_call" | custom-call | tf_op jit(solution)/shard_map/pallas_call | solution.py:192
  45.5 3.8 %all-to-all-start.1 = ((bf16[8,2,4,16,128]{4,3,2,1,0:T(8,128)(2,1)}), bf16[8,2,4,16,128]{4,3,2,1,0:T(8,128)(2,1)S(1)}, u32[]{:S(2)}, u32[]{:S(2)}) async-start(bf16[8,2,4,16,128]{4,3,2,1,0:T(8,128)(2,1)} %bitcast.16), calls=%async_computation.1 | async-start | bytes 524288 | tf_op jit(solution)/shard_map/all_to_all | solution.py:269
  49.3 0.0 copy-done.5
  49.3 2.4 %shard_map.88 = bf16[128,16,128]{2,1,0:T(8,128)(2,1)} custom-call(bf16[18,144,256]{2,1,0:T(8,128)(2,1)S(1)} %get-tuple-element.8.hidden, bf16[16,128,128]{2,1,0:T(8,128)(2,1)S(1)} %get-tuple-element.6.cells, bf16[5,128,256]{2,1,0:T(8,128)(2,1)S(1)} %copy-done.3, f32[1,128]{1,0:T(1,128)S(1)} %bitcast.35), custom_call_target="tpu_custom_call" | custom-call | flops 849346560 | bytes 2500000 | tf_op jit(solution)/shard_map/pallas_call | solution.py:138
  51.7 6.3 %all-to-all-done.1.got = bf16[8,2,4,16,128]{4,3,2,1,0:T(8,128)(2,1)S(1)} async-done(((bf16[8,2,4,16,128]{4,3,2,1,0:T(8,128)(2,1)}), bf16[8,2,4,16,128]{4,3,2,1,0:T(8,128)(2,1)S(1)}, u32[]{:S(2)}, u32[]{:S(2)}) %all-to-all-start.1) | async-done | bytes 262176 | tf_op jit(solution)/shard_map/all_to_all | solution.py:269
  58.0 0.7 %shard_map.90 = bf16[2,4,16,128]{3,2,1,0:T(8,128)(2,1)} custom-call(bf16[8,2,4,16,128]{4,3,2,1,0:T(8,128)(2,1)S(1)} %all-to-all-done.1.got), custom_call_target="tpu_custom_call" | custom-call | tf_op jit(solution)/shard_map/pallas_call | solution.py:209
  (11 shorter events, 0.1 us)
Async XLA Ops:
  0.6 25.1 %copy-start.4 = (f32[256]{0:T(256)S(1)}, f32[256]{0:T(256)}, u32[]{:S(2)}) copy-start(f32[256]{0:T(256)} %param.9) | copy-start | bytes 3076
  0.7 1.0 %copy-start = (bf16[1,128,16,128]{3,2,1,0:T(8,128)(2,1)S(1)}, bf16[1,128,16,128]{3,2,1,0:T(8,128)(2,1)}, u32[]{:S(2)}) copy-start(bf16[1,128,16,128]{3,2,1,0:T(8,128)(2,1)} %param.7) | copy-start | bytes 1572868
  1.7 24.0 %copy-start.1 = (bf16[1,128,16,128]{3,2,1,0:T(8,128)(2,1)S(1)}, bf16[1,128,16,128]{3,2,1,0:T(8,128)(2,1)}, u32[]{:S(2)}) copy-start(bf16[1,128,16,128]{3,2,1,0:T(8,128)(2,1)} %param.7) | copy-start | bytes 1572868
  1.7 24.1 %copy-start.2 = (bf16[5,256,128]{2,1,0:T(8,128)(2,1)S(1)}, bf16[5,256,128]{2,1,0:T(8,128)(2,1)}, u32[]{:S(2)}) copy-start(bf16[5,256,128]{2,1,0:T(8,128)(2,1)} %conv_in.1) | copy-start | bytes 983044
  1.7 24.1 %copy-start.3 = (bf16[5,128,256]{2,1,0:T(8,128)(2,1)S(1)}, bf16[5,128,256]{2,1,0:T(8,128)(2,1)}, u32[]{:S(2)}) copy-start(bf16[5,128,256]{2,1,0:T(8,128)(2,1)} %conv_out.3) | copy-start | bytes 983044
  2.2 17.8 %collective-permute-start.1 = (bf16[2,16,128]{2,1,0:T(8,128)(2,1)S(1)}, bf16[2,16,128]{2,1,0:T(8,128)(2,1)S(1)}, u32[]{:S(2)}, u32[]{:S(2)}) collective-permute-start(bf16[2,16,128]{2,1,0:T(8,128)(2,1)S(1)} %broadcast_select_fusion.4), channel_id=1, source_target_pairs={{0,184},{1,2},{2,1},{3,4},{4,3},{5,6},{6,5},{7,127},{8,176},{9,10}... | collective-permute-start | bytes 24584 | tf_op jit(solution)/shard_map/ppermute | solution.py:159
  13.7 6.3 %collective-permute-start = (bf16[2,16,128]{2,1,0:T(8,128)(2,1)S(1)}, bf16[2,16,128]{2,1,0:T(8,128)(2,1)S(1)}, u32[]{:S(2)}, u32[]{:S(2)}) collective-permute-start(bf16[2,16,128]{2,1,0:T(8,128)(2,1)S(1)} %get-tuple-element.20), channel_id=1, source_target_pairs={{0,1},{1,0},{2,3},{3,2},{4,5},{5,4},{6,7},{7,6},{8,9},{9,8},{10,11... | collective-permute-start | bytes 24584 | tf_op jit(solution)/shard_map/ppermute | solution.py:159
  20.1 5.6 %collective-permute-start.3 = (bf16[264,128]{1,0:T(8,128)(2,1)S(1)}, bf16[264,128]{1,0:T(8,128)(2,1)S(1)}, u32[]{:S(2)}, u32[]{:S(2)}) collective-permute-start(bf16[264,128]{1,0:T(8,128)(2,1)S(1)} %get-tuple-element.14), channel_id=1, source_target_pairs={{8,16},{9,17},{10,18},{11,19},{12,20},{13,21},{14,22},{15,23},{16,... | collective-permute-start | bytes 202760 | tf_op jit(solution)/shard_map/ppermute | solution.py:159
  22.0 3.7 %collective-permute-start.2 = (bf16[264,128]{1,0:T(8,128)(2,1)S(1)}, bf16[264,128]{1,0:T(8,128)(2,1)S(1)}, u32[]{:S(2)}, u32[]{:S(2)}) collective-permute-start(bf16[264,128]{1,0:T(8,128)(2,1)S(1)} %get-tuple-element.15), channel_id=1, source_target_pairs={{0,8},{1,9},{2,10},{3,11},{4,12},{5,13},{6,14},{7,15},{8,0},{9,1},... | collective-permute-start | bytes 202760 | tf_op jit(solution)/shard_map/ppermute | solution.py:159
  25.8 23.5 %copy-start.5 = (f32[128]{0:T(128)S(1)}, f32[128]{0:T(128)}, u32[]{:S(2)}) copy-start(f32[128]{0:T(128)} %param.11) | copy-start | bytes 1540
  30.5 13.7 %all-to-all-start = ((bf16[8,4,16,128]{3,2,1,0:T(8,128)(2,1)}), bf16[8,4,16,128]{3,2,1,0:T(8,128)(2,1)S(1)}, u32[]{:S(2)}, u32[]{:S(2)}) async-start(bf16[8,4,16,128]{3,2,1,0:T(8,128)(2,1)} %get-tuple-element.9), calls=%async_computation | async-start | bytes 262144 | tf_op jit(solution)/shard_map/all_to_all | solution.py:266
  45.5 12.5 %all-to-all-start.1 = ((bf16[8,2,4,16,128]{4,3,2,1,0:T(8,128)(2,1)}), bf16[8,2,4,16,128]{4,3,2,1,0:T(8,128)(2,1)S(1)}, u32[]{:S(2)}, u32[]{:S(2)}) async-start(bf16[8,2,4,16,128]{4,3,2,1,0:T(8,128)(2,1)} %bitcast.16), calls=%async_computation.1 | async-start | bytes 524288 | tf_op jit(solution)/shard_map/all_to_all | solution.py:269

commit v3 on v1

v3 whole, which is shorter than its diff:
```python
import jax
import jax.numpy as jnp
from jax import lax
from jax.experimental import pallas as pl
from jax.experimental.pallas import tpu as pltpu
from jax.sharding import PartitionSpec as P

OC = 4
CAP = 2
ALL = ("face", "row", "col")
BORDER = 2
LONG = 32
TAPS = (3, 2, 4, 1, 0, 1, 4, 2, 3)
NT = (((1,), (1,)), ((), ()))
VM = pl.BlockSpec(memory_space=pltpu.VMEM)
PARAMS = pltpu.CompilerParams(vmem_limit_bytes=24 * 2**20)
F32 = jnp.float32
BF16 = jnp.bfloat16


def call(kernel, out_shape, scratch, cost, *operands):
    many = isinstance(out_shape, list)
    return pl.pallas_call(
        kernel,
        out_shape=out_shape,
        in_specs=[VM] * len(operands),
        out_specs=[VM] * len(out_shape) if many else VM,
        scratch_shapes=[pltpu.VMEM(s, d) for s, d in scratch],
        compiler_params=PARAMS,
        cost_estimate=pl.CostEstimate(flops=cost[0], bytes_accessed=cost[1], transcendentals=cost[2]),
    )(*operands)


def turn_kernel(state, cells, edges, flat, turned):
    chans, rows, cols = state.shape
    flat[...] = state[...].reshape(chans * rows, cols).astype(F32)
    for r in range(rows):
        turned[r] = flat[pl.ds(r, chans, stride=rows), :].T
        cells[r] = turned[r].astype(BF16)
    for k, w in enumerate((0, 1, cols - 2, cols - 1)):
        edges[k] = turned.reshape(rows * cols, chans)[pl.ds(w, rows, stride=cols), :].astype(BF16)


def turn(state):
    chans, rows, cols = state.shape
    return call(
        turn_kernel,
        [jax.ShapeDtypeStruct((rows, cols, chans), BF16), jax.ShapeDtypeStruct((4, rows, chans), BF16)],
        [((chans * rows, cols), F32), ((rows, cols, chans), F32)],
        (0, 4 * state.size, 0),
        state,
    )


def route_kernel(owner, land, here, target, place):
    count = owner.shape[1]
    cols = rows = 8
    wide = lambda v: jnp.broadcast_to(v, (count, count))
    i = lax.broadcasted_iota(jnp.int32, (count, count), 0)
    j = lax.broadcasted_iota(jnp.int32, (count, count), 1)
    own, wet = wide(owner[...]), wide(1 - land[...])
    down = lambda v: jnp.sum(jnp.where(i == j, v, 0).astype(F32), axis=1, keepdims=True)
    own_i, wet_i = down(own), down(wet)
    same = (own.astype(F32) == own_i) & (wet == 1) & (j < i)
    slot = jnp.sum(jnp.where(same, 1.0, 0.0), axis=1, keepdims=True)
    lanes = here.shape[1]
    spread = lambda v: jnp.broadcast_to(v, (count, lanes))
    own_i, wet_i, slot = spread(own_i).astype(jnp.int32), spread(wet_i), spread(slot).astype(jnp.int32)
    tile = lax.broadcasted_iota(jnp.int32, (count, lanes), 0)
    r, c = here[2:3], here[3:4]
    mine = (tile == r * cols + c) & (wet_i > 0)
    to_col = jnp.sum(jnp.where(mine, (own_i & (cols - 1)) + 1, 0).astype(F32), axis=0, keepdims=True) - 1.0
    target[...] = jnp.broadcast_to(to_col, target.shape)
    spot = jnp.where((wet_i > 0) & ((own_i & (cols - 1)) == c), (own_i >> 3) * 2 + slot, -1).astype(F32)
    total = jnp.full((cols, lanes), 0.0, F32)
    for k in range(rows):
        total = jnp.where(r == k, spot[k * cols : (k + 1) * cols], total)
    place[...] = total


def routes(owner, land, here):
    shape = jax.ShapeDtypeStruct((8, here.shape[1]), F32)
    return call(route_kernel, [shape, shape], [], (100000, 20000, 0), owner, land, here)


def inner_kernel(here, cells, above, below, conv_in, bias_in, conv_out, bias_sea, state, hidden, sea, field, taps):
    rows, cols, chans = cells.shape
    hid = bias_in.shape[1]
    for start, part in ((0, above), (BORDER, cells), (BORDER + rows, below)):
        for r in range(part.shape[0]):
            field[start + r, 8 : 8 + cols] = part[r].astype(F32)
    for r in range(rows + 2 * BORDER):
        for k in range(3):
            taps[r, :, k * chans : (k + 1) * chans] = field[r, 7 + k : 7 + k + cols].astype(BF16)
    weights = jnp.concatenate([conv_in[t] for t in TAPS], axis=1)
    col = lax.broadcasted_iota(jnp.int32, (cols, hid), 0)
    inside = (col > 0) & (col < cols - 1)
    keep = jnp.concatenate([here[0:2]] * (hid // here.shape[1]), axis=1) > 0
    step = 3
    for j in range(0, rows + 2, step):
        data = jnp.concatenate([taps[j + d : j + d + step].reshape(step * cols, 3 * chans) for d in range(3)], axis=1)
        x = lax.dot_general(data, weights, NT, preferred_element_type=F32) + bias_in[...]
        x = jax.nn.gelu(x).reshape(step, cols, hid)
        for d in range(step):
            here_in = inside
            if j + d == 0:
                here_in = inside & keep[0:1]
            if j + d == rows + 1:
                here_in = inside & keep[1:2]
            hidden[j + d] = jnp.where(here_in, x[d], 0.0).astype(BF16)
    sea_weights = conv_out[:, 0:16].reshape(5 * 16, hid)
    z = []
    for j in range(0, rows + 2, 2):
        two = lax.dot_general(sea_weights, hidden[j : j + 2].reshape(2 * cols, hid), NT, preferred_element_type=F32)
        z += [two[:, :cols], two[:, cols:]]
    cut = lambda j, t: z[j][16 * t : 16 * t + 8]
    for r in range(rows):
        j = r + 1
        mid = cut(j, 0) + cut(j - 1, 2) + cut(j + 1, 2)
        plus = cut(j, 1) + cut(j + 1, 3) + cut(j - 1, 4)
        minus = cut(j, 1) + cut(j - 1, 3) + cut(j + 1, 4)
        total = mid + pltpu.roll(plus, cols - 1, 1) + pltpu.roll(minus, 1, 1) + bias_sea[...]
        sea[:, r] = total
    sea[...] += state[0:8].astype(F32)


def inner_part(here, cells, above, below, conv_in, bias_in, conv_out, bias_sea, state):
    rows, cols, chans = cells.shape
    hid = conv_in.shape[1]
    return call(
        inner_kernel,
        [jax.ShapeDtypeStruct((rows + 2, cols, hid), BF16), jax.ShapeDtypeStruct((8, rows, cols), F32)],
        [((rows + 4, cols + 16, chans), F32), ((rows + 4, cols, 3 * chans), BF16)],
        (2 * 18 * 128 * (1152 + 80) * 256, 3000000, 18 * 128 * 256),
        here, cells, above, below, conv_in, bias_in, conv_out, bias_sea, state,
    )


def rim_kernel(here, target, edges, sides, conv_in, bias_in, conv_out, sea, rim, blocks, field, tall):
    hid = bias_in.shape[1]
    n_blocks, n_sea, rows, cols = blocks.shape
    for k, (part, at) in enumerate(((sides, 0), (sides, 1), (edges, 0), (edges, 1), (edges, 2), (edges, 3), (sides, 2), (sides, 3))):
        field[k, 0:LONG] = part[at].astype(F32)
        field[k, LONG : LONG + 8] = jnp.zeros((8, field.shape[2]), F32)
    weights = jnp.concatenate([conv_in[t] for t in TAPS], axis=1)
    data = []
    for k in (1, 2, 5, 6):
        data.append(jnp.concatenate([field[k + dc, dr : dr + LONG].astype(BF16) for dr in range(3) for dc in (-1, 0, 1)], axis=1))
    x = lax.dot_general(jnp.concatenate(data, axis=0), weights, NT, preferred_element_type=F32) + bias_in[...]
    x = jax.nn.gelu(x)
    keep = jnp.concatenate([here[0:2]] * (hid // here.shape[1]), axis=1) > 0
    row = lax.broadcasted_iota(jnp.int32, (LONG, hid), 0)
    inside = ((row > 0) | keep[0:1]) & ((row < rows + 1) | keep[1:2]) & (row < rows + 2)
    for k in range(4):
        tall[k] = jnp.where(inside, x[k * LONG : (k + 1) * LONG], 0.0).astype(BF16).astype(F32)
        rim[k] = tall[k].astype(BF16)
    data = [jnp.concatenate([tall[k, d : d + rows].astype(BF16) for d in range(3)], axis=1) for k in range(4)]
    part = lambda dc: jnp.concatenate([conv_out[TAPS[3 * dr + dc], 0:16] for dr in range(3)], axis=1)
    sea_weights = jnp.concatenate([part(dc) for dc in range(3)], axis=0)
    z = lax.dot_general(jnp.concatenate(data, axis=0), sea_weights, NT, preferred_element_type=F32)
    lane = lax.broadcasted_iota(jnp.int32, (rows, cols), 1)
    for o in range(n_sea):
        piece = lambda k, dc: z[k * rows : (k + 1) * rows, 16 * (dc + 1) + o : 16 * (dc + 1) + o + 1]
        extra = jnp.where(lane == 0, piece(0, -1) + piece(1, 0), 0.0)
        extra = jnp.where(lane == 1, piece(1, -1), extra)
        extra = jnp.where(lane == cols - 2, piece(2, 1), extra)
        extra = jnp.where(lane == cols - 1, piece(2, 0) + piece(3, 1), extra)
        v = (sea[o] + extra).astype(BF16).astype(F32)
        for b in range(n_blocks):
            blocks[b, o] = jnp.where(target[0:1] == b, v, 0.0).astype(BF16)


def rim_part(here, target, edges, sides, conv_in, bias_in, conv_out, sea, n_blocks, n_sea):
    rows, cols = sea.shape[1:]
    chans = edges.shape[2]
    hid = conv_in.shape[1]
    return call(
        rim_kernel,
        [jax.ShapeDtypeStruct((4, LONG, hid), BF16), jax.ShapeDtypeStruct((n_blocks, n_sea, rows, cols), BF16)],
        [((8, LONG + 8, chans), F32), ((4, LONG, hid), F32)],
        (2 * 128 * 1152 * 256, 1500000, 128 * 256),
        here, target, edges, sides, conv_in, bias_in, conv_out, sea,
    )


def out_kernel(hidden, rim, cells, conv_out, bias_out, new_state, z, flat):
    rows, cols, chans = cells.shape
    hid = hidden.shape[2]
    weights = conv_out[...].reshape(5 * chans, hid)
    step = 3
    for j in range(0, rows + 2, step):
        data = hidden[j : j + step].reshape(step * cols, hid)
        got = lax.dot_general(data, weights, NT, preferred_element_type=F32)
        z[j : j + step, 8 : 8 + cols] = got.reshape(step, cols, 5 * chans)
    got = lax.dot_general(rim[...].reshape(4 * LONG, hid), weights, NT, preferred_element_type=F32)
    for k, s in enumerate((7, 8, 7 + cols, 8 + cols)):
        for j in range(rows + 2):
            z[j, s : s + 1] = got[k * LONG + j : k * LONG + j + 1]
    cut = lambda j, t, s: z[j, 8 + s : 8 + s + cols, t * chans : (t + 1) * chans]
    for r in range(rows):
        j = r + 1
        total = cut(j, 0, 0) + cut(j - 1, 2, 0) + cut(j + 1, 2, 0)
        total += cut(j, 1, 1) + cut(j + 1, 3, 1) + cut(j - 1, 4, 1)
        total += cut(j, 1, -1) + cut(j - 1, 3, -1) + cut(j + 1, 4, -1)
        total += bias_out[...] + cells[r].astype(F32)
        flat[pl.ds(r, chans, stride=rows), :] = total.T
    new_state[...] = flat[...].reshape(chans, rows, cols).astype(BF16)


def out_part(hidden, rim, cells, conv_out, bias_out):
    rows, cols, chans = cells.shape
    return call(
        out_kernel,
        jax.ShapeDtypeStruct((chans, rows, cols), BF16),
        [((rows + 2, cols + 16, 5 * chans), F32), ((chans * rows, cols), F32)],
        (2 * 18 * 128 * 640 * 256, 3000000, 0),
        hidden, rim, cells, conv_out, bias_out,
    )


def sort_kernel(place, held, sent):
    half = sent.shape[0] // 2
    parts = [held[k].astype(F32) for k in range(held.shape[0])]
    for p in range(half):
        total = jnp.zeros_like(parts[0])
        for k, v in enumerate(parts):
            total = jnp.where((place[k : k + 1] == p)[None], v, total)
        sent[p] = total.astype(BF16)
    sent[half:] = jnp.zeros((half,) + sent.shape[1:], BF16)


def sort_tiles(place, held, count):
    shape = jax.ShapeDtypeStruct((count,) + held.shape[1:], BF16)
    return call(sort_kernel, shape, [], (100000, 6 * held.size, 0), place, held)


def merge_kernel(got, ocean):
    total = got[0].astype(F32)
    for k in range(1, got.shape[0]):
        total += got[k].astype(F32)
    ocean[...] = total.astype(BF16)


def merge(got):
    return call(merge_kernel, jax.ShapeDtypeStruct(got.shape[1:], BF16), [], (100000, 2 * got.size, 0), got)


def exchange(values, partner):
    shape = tuple(lax.axis_size(a) for a in ALL)
    number = lambda f, r, c: (f * shape[1] + r) * shape[2] + c
    pairs = []
    for f in range(shape[0]):
        for r in range(shape[1]):
            for c in range(shape[2]):
                other = partner(f, r, c, shape)
                if other is not None:
                    pairs.append((number(f, r, c), number(*other)))
    return lax.ppermute(values, ALL, pairs)


def col_near(f, r, c, shape):
    return (f, r, c ^ 1)


def col_far(f, r, c, shape):
    if c == 0:
        return (f ^ 2, shape[1] - 1 - r, c)
    if c == shape[2] - 1:
        return (f ^ 1, shape[1] - 1 - r, c)
    return (f, r, ((c + 1) ^ 1) - 1)


def row_near(f, r, c, shape):
    return (f, r ^ 1, c)


def row_far(f, r, c, shape):
    return None if r in (0, shape[1] - 1) else (f, ((r + 1) ^ 1) - 1, c)


def local(state, conv_in, bias_in, conv_out, bias_out, land, owner):
    state = state[0]
    chans, height, width = state.shape
    rows, cols = lax.axis_size("row"), lax.axis_size("col")
    r, c = lax.axis_index("row"), lax.axis_index("col")
    lines = (r > 0, r < rows - 1, r, c, 0, 0, 0, 0)
    here = jnp.concatenate([jnp.full((1, 128), v, jnp.int32) for v in lines])
    cells, edges = turn(state)

    odd = r % 2 == 1
    top, bottom = cells[:BORDER], cells[height - BORDER :]
    got_far = exchange(jnp.where(odd, bottom, top), row_far)
    got_near = exchange(jnp.where(odd, top, bottom), row_near)
    above, below = jnp.where(odd, got_near, got_far), jnp.where(odd, got_far, got_near)

    odd = c % 2 == 1
    pick = lambda v: jnp.stack([v[:, 0], v[:, 1], v[:, width - 2], v[:, width - 1]])
    tall = jnp.concatenate([pick(above), edges, pick(below)], axis=1)
    full = lambda v: jnp.pad(v, ((0, 0), (0, LONG - v.shape[1]), (0, 0)))
    west, east = tall[:BORDER], tall[BORDER:]
    far = jnp.where(odd, east, west)
    far = jnp.where((c == 0) | (c == cols - 1), far[::-1, ::-1], far)
    got_far = exchange(full(far), col_far)
    got_near = exchange(full(jnp.where(odd, west, east)), col_near)
    sides = jnp.concatenate([jnp.where(odd, got_near, got_far), jnp.where(odd, got_far, got_near)])

    target, place = routes(owner, land, here)
    bias_in = bias_in[None]
    hidden, sea = inner_part(here, cells, above, below, conv_in, bias_in, conv_out, bias_out[:8, None], state)
    rim, blocks = rim_part(here, target, full(tall), sides, conv_in, bias_in, conv_out, sea, cols, OC)
    held = lax.all_to_all(blocks, "col", 0, 0, tiled=True)
    new_state = out_part(hidden, rim, cells, conv_out, bias_out[None])
    sent = sort_tiles(place, held, rows * CAP).reshape((rows, CAP, OC, height, width))
    got = lax.all_to_all(sent, "row", 0, 0, tiled=True)
    return (new_state[None], merge(got)[None, None])


def solution(mesh):
    in_specs = (P("face", None, "row", "col"), P(), P(), P(), P(), P("face", None), P("face", None))
    out_specs = (P("face", None, "row", "col"), P("face", ("row", "col"), None, None, None, None))
    return jax.shard_map(local, mesh=mesh, in_specs=in_specs, out_specs=out_specs, check_vma=False)
```

time: 63.4 us -> 53.1 us (0.84)
  blocking collectives: 0 us -> 12.3 us
  waiting for transfers between devices: 17.5 us -> 6.71 us
  Pallas kernels: 0 us -> 8.1 us
  local copies, waits for them, and re-layouts: 8.71 us -> 1.63 us
  matrix products: 5.77 us -> 0 us
  other arithmetic: 2.99 us -> 0.22 us
  starting transfers between devices: 25.1 us -> 22.8 us
  between operations: 2.93 us -> 0.99 us
    all_to_all x0 -> x1, blocking collectives: none -> 12.3 us  [local(): held = lax.all_to_all(blocks, 'col', 0, 0, tiled=True)]
    all_to_all x2 -> x1, waiting for transfers between devices: 16.4 us -> 5.99 us  [local(): got = lax.all_to_all(sent, 'row', 0, 0, tiled=True)]
    pallas_call x0 -> x7, Pallas kernels: none -> 8.1 us  [call(): pl.pallas_call(kernel, out_shape=out_shape, in_specs=[VM] * len(operands)...]
    conv_general_dilated x2 -> x0, matrix products: 5.42 us -> none  [conv(): lax.conv_general_dilated(padded[None], kernel, (1, 1), 'VALID', dimension...]
    unnamed x17 -> x16, local copies, waits for them, and re-layouts: 5.49 us -> 1.07 us
    all_to_all x2 -> x1, starting transfers between devices: 7.88 us -> 4.76 us  [local(): got = lax.all_to_all(sent, 'row', 0, 0, tiled=True)]
    dynamic_slice x2 -> x0, local copies, waits for them, and re-layouts: 1.17 us -> none  [relay(): to_col = wet[mine] & (owner[mine] % cols == jnp.arange(cols))]
    reshape x1 -> x0, local copies, waits for them, and re-layouts: 0.92 us -> none  [relay(): sent = sent.astype(jnp.bfloat16).reshape((rows, CAP) + sea.shape)]
  transfers between devices with their start and end apart: 6 -> 5, of which waited for: 3 -> 3; matrix products, arithmetic and copies ran while one was open for 6% -> 0% of each run, Pallas kernels for 0% -> 10%
where the time goes in v3:
time: 53.1 us; the launch traced here: 52.7 us
  starting transfers between devices  22.8 us (43%)
  blocking collectives  12.3 us (23%)
  Pallas kernels  8.1 us (15%)
  waiting for transfers between devices  6.71 us (13%)
  local copies, waits for them, and re-layouts  1.63 us (3%)
  between operations  0.99 us (2%)
    ppermute x4, starting transfers between devices, exchange(): return lax.ppermute(values, ALL, pairs)  18.1 us
    all_to_all x1, blocking collectives, local(): held = lax.all_to_all(blocks, 'col', 0, 0, tiled=True)  12.3 us
    pallas_call x7, Pallas kernels, call(): pl.pallas_call(kernel, out_shape=out_shape, in_specs=[VM] * len(operands)...  8.1 us
    all_to_all x1, waiting for transfers between devices, local(): got = lax.all_to_all(sent, 'row', 0, 0, tiled=True)  5.99 us
    all_to_all x1, starting transfers between devices, local(): got = lax.all_to_all(sent, 'row', 0, 0, tiled=True)  4.76 us
    unnamed x16, local copies, waits for them, and re-layouts  1.07 us
  transfers between devices with their start and end apart: 5, of which 3 were waited for; matrix products, arithmetic and copies ran while one was open for 0% of the time, Pallas kernels for 10%

profile of v3, /device:TPU:1, one launch (start us, length us, event | category | flops | bytes accessed | tf_op | source)
XLA Modules:
  0.0 52.7 jit_solution(11061034036060824388)
XLA Ops:
  0.6 0.0 copy-start.7
  0.6 0.0 copy-start.5
  0.7 0.0 copy-start.6
  0.7 0.0 copy-start
  0.7 1.0 %copy-done = bf16[1,128,16,128]{3,2,1,0:T(8,128)(2,1)S(1)} copy-done((bf16[1,128,16,128]{3,2,1,0:T(8,128)(2,1)S(1)}, bf16[1,128,16,128]{3,2,1,0:T(8,128)(2,1)}, u32[]{:S(2)}) %copy-start) | copy-done | bytes 524312
  1.7 0.4 shard_map.86
  2.2 0.0 copy-start.1
  2.2 0.0 copy-start.2
  2.2 0.0 copy-start.3
  2.2 0.0 copy-start.4
  2.2 0.3 copy.9
  2.5 0.1 broadcast_select_fusion.2
  2.7 5.4 %collective-permute-start.1 = (bf16[2,128,128]{2,0,1:T(2,128)(2,1)S(1)}, bf16[2,128,128]{2,0,1:T(2,128)(2,1)S(1)}, u32[]{:S(2)}, u32[]{:S(2)}) collective-permute-start(bf16[2,128,128]{2,0,1:T(2,128)(2,1)S(1)} %get-tuple-element.18), channel_id=1, source_target_pairs={{8,16},{9,17},{10,18},{11,19},{12,20},{13,21},{14,22},{15,23},{16,... | collective-permute-start | bytes 196616 | tf_op jit(solution)/shard_map/ppermute | solution.py:258
  8.1 4.1 %collective-permute-start = (bf16[2,128,128]{2,0,1:T(2,128)(2,1)S(1)}, bf16[2,128,128]{2,0,1:T(2,128)(2,1)S(1)}, u32[]{:S(2)}, u32[]{:S(2)}) collective-permute-start(bf16[2,128,128]{2,0,1:T(2,128)(2,1)S(1)} %get-tuple-element.19), channel_id=1, source_target_pairs={{0,8},{1,9},{2,10},{3,11},{4,12},{5,13},{6,14},{7,15},{8,0},{9,1},... | collective-permute-start | bytes 196616 | tf_op jit(solution)/shard_map/ppermute | solution.py:258
  12.2 0.0 copy-done.7
  12.3 0.0 copy-done.5
  12.3 0.0 copy-done.6
  12.3 0.2 shard_map.88
  12.5 0.1 copy.13.bias_sea
  12.6 0.0 collective-permute-done.1
  12.6 0.5 collective-permute-done
  13.2 6.7 %collective-permute-start.3 = (bf16[2,32,128]{2,1,0:T(8,128)(2,1)S(1)}, bf16[2,32,128]{2,1,0:T(8,128)(2,1)S(1)}, u32[]{:S(2)}, u32[]{:S(2)}) collective-permute-start(bf16[2,32,128]{2,1,0:T(8,128)(2,1)S(1)} %pad.13), channel_id=1, source_target_pairs={{0,184},{1,2},{2,1},{3,4},{4,3},{5,6},{6,5},{7,127},{8,176},{9,10}... | collective-permute-start | bytes 49160 | tf_op jit(solution)/shard_map/ppermute | solution.py:258
  20.0 1.9 %collective-permute-start.2 = (bf16[2,32,128]{2,1,0:T(8,128)(2,1)S(1)}, bf16[2,32,128]{2,1,0:T(8,128)(2,1)S(1)}, u32[]{:S(2)}, u32[]{:S(2)}) collective-permute-start(bf16[2,32,128]{2,1,0:T(8,128)(2,1)S(1)} %pad.12), channel_id=1, source_target_pairs={{0,1},{1,0},{2,3},{3,2},{4,5},{5,4},{6,7},{7,6},{8,9},{9,8},{10,11... | collective-permute-start | bytes 49160 | tf_op jit(solution)/shard_map/ppermute | solution.py:258
  21.9 0.0 copy-done.1
  21.9 0.0 copy-done.2
  21.9 0.0 copy-done.3
  21.9 0.0 copy-done.4
  21.9 2.6 %shard_map.87 = (bf16[18,128,256]{2,1,0:T(8,128)(2,1)S(1)}, f32[8,16,128]{2,1,0:T(8,128)S(1)}) custom-call(s32[8,128]{1,0:T(8,128)S(1)} %concatenate.13.here, bf16[16,128,128]{2,1,0:T(8,128)(2,1)S(1)} %get-tuple-element.10.cells, bf16[2,128,128]{2,1,0:T(8,128)(2,1)S(1)} %copy.11.above, bf16[2,128,128]{2,1,0:T(8,128)(2,1)S(1)} %copy.12.below, ...), custom_call_target="tpu_custom_call" | custom-call | flops 1453326336 | bytes 3000000 | tf_op jit(solution)/shard_map/pallas_call | solution.py:23
  24.6 0.0 collective-permute-done.3
  24.6 0.2 collective-permute-done.2
  24.8 0.7 %shard_map.89 = (bf16[4,32,256]{2,1,0:T(8,128)(2,1)S(1)}, bf16[8,4,16,128]{3,2,1,0:T(8,128)(2,1)S(1)}) custom-call(s32[8,128]{1,0:T(8,128)S(1)} %concatenate.13.here, f32[8,128]{1,0:T(8,128)S(1)} %get-tuple-element.12.target, bf16[4,32,128]{2,1,0:T(8,128)(2,1)S(1)} %pad.11.edges, bf16[4,32,128]{2,1,0:T(8,128)(2,1)S(1)} %pad_maximum_fusion.sides, ...), custom_call_target="tpu_custom_call" | custom-call | flops 75497472 | bytes 1500000 | tf_op jit(solution)/shard_map/pallas_call | solution.py:23
  25.5 12.3 %all_to_all.10.held = bf16[8,4,16,128]{3,2,1,0:T(8,128)(2,1)S(1)} all-to-all(bf16[8,4,16,128]{3,2,1,0:T(8,128)(2,1)S(1)} %get-tuple-element.17), channel_id=1, replica_groups=mesh['face'=8,'row'=8,'col'=8] {'col'}, dimensions={0} | all-to-all | bytes 262144 | tf_op jit(solution)/shard_map/all_to_all | solution.py:311
  37.8 0.8 %shard_map.91 = bf16[16,4,16,128]{3,2,1,0:T(8,128)(2,1)} custom-call(f32[8,128]{1,0:T(8,128)S(1)} %get-tuple-element.16.place, bf16[8,4,16,128]{3,2,1,0:T(8,128)(2,1)S(1)} %all_to_all.10.held), custom_call_target="tpu_custom_call" | custom-call | flops 100000 | bytes 393216 | tf_op jit(solution)/shard_map/pallas_call | solution.py:23
  38.6 4.8 %all-to-all-start.1 = ((bf16[8,2,4,16,128]{4,3,2,1,0:T(8,128)(2,1)}), bf16[8,2,4,16,128]{4,3,2,1,0:T(8,128)(2,1)S(1)}, u32[]{:S(2)}, u32[]{:S(2)}) async-start(bf16[8,2,4,16,128]{4,3,2,1,0:T(8,128)(2,1)} %bitcast.13), calls=%async_computation.1 | async-start | bytes 524288 | tf_op jit(solution)/shard_map/all_to_all | solution.py:314
  43.4 2.7 %shard_map.90 = bf16[128,16,128]{2,1,0:T(8,128)(2,1)} custom-call(bf16[18,128,256]{2,1,0:T(8,128)(2,1)S(1)} %get-tuple-element.11.hidden, bf16[4,32,256]{2,1,0:T(8,128)(2,1)S(1)} %get-tuple-element.15.rim, bf16[16,128,128]{2,1,0:T(8,128)(2,1)S(1)} %get-tuple-element.10.cells, bf16[5,128,256]{2,1,0:T(8,128)(2,1)S(1)} %copy-done.3, f32[1,128]{1,0:T(1,128)S(1)} %bitcast.32), custom_call_target="tpu_custom_call" | custom-call | flops 754974720 | bytes 3000000 | tf_op jit(solution)/shard_map/pallas_call | solution.py:23
  46.1 6.0 %all-to-all-done.1.got = bf16[8,2,4,16,128]{4,3,2,1,0:T(8,128)(2,1)S(1)} async-done(((bf16[8,2,4,16,128]{4,3,2,1,0:T(8,128)(2,1)}), bf16[8,2,4,16,128]{4,3,2,1,0:T(8,128)(2,1)S(1)}, u32[]{:S(2)}, u32[]{:S(2)}) %all-to-all-start.1) | async-done | bytes 262176 | tf_op jit(solution)/shard_map/all_to_all | solution.py:314
  52.1 0.7 %shard_map.92 = bf16[2,4,16,128]{3,2,1,0:T(8,128)(2,1)} custom-call(bf16[8,2,4,16,128]{4,3,2,1,0:T(8,128)(2,1)S(1)} %all-to-all-done.1.got), custom_call_target="tpu_custom_call" | custom-call | flops 100000 | bytes 262144 | tf_op jit(solution)/shard_map/pallas_call | solution.py:23
  (20 shorter events, 0.2 us)
Async XLA Ops:
  0.6 11.5 %copy-start.7 = (f32[128]{0:T(128)S(1)}, f32[128]{0:T(128)}, u32[]{:S(2)}) copy-start(f32[128]{0:T(128)} %param.11) | copy-start | bytes 1540
  0.6 11.7 %copy-start.5 = (s32[1,64]{1,0:T(1,128)S(1)}, s32[1,64]{1,0:T(1,128)}, u32[]{:S(2)}) copy-start(s32[1,64]{1,0:T(1,128)} %owner.1) | copy-start | bytes 772
  0.7 11.6 %copy-start.6 = (s32[1,64]{1,0:T(1,128)S(1)}, s32[1,64]{1,0:T(1,128)}, u32[]{:S(2)}) copy-start(s32[1,64]{1,0:T(1,128)} %land.1) | copy-start | bytes 772
  0.7 1.0 %copy-start = (bf16[1,128,16,128]{3,2,1,0:T(8,128)(2,1)S(1)}, bf16[1,128,16,128]{3,2,1,0:T(8,128)(2,1)}, u32[]{:S(2)}) copy-start(bf16[1,128,16,128]{3,2,1,0:T(8,128)(2,1)} %param.7) | copy-start | bytes 1572868
  2.2 19.7 %copy-start.1 = (bf16[1,128,16,128]{3,2,1,0:T(8,128)(2,1)S(1)}, bf16[1,128,16,128]{3,2,1,0:T(8,128)(2,1)}, u32[]{:S(2)}) copy-start(bf16[1,128,16,128]{3,2,1,0:T(8,128)(2,1)} %param.7) | copy-start | bytes 1572868
  2.2 19.7 %copy-start.2 = (bf16[5,256,128]{2,1,0:T(8,128)(2,1)S(1)}, bf16[5,256,128]{2,1,0:T(8,128)(2,1)}, u32[]{:S(2)}) copy-start(bf16[5,256,128]{2,1,0:T(8,128)(2,1)} %conv_in.3) | copy-start | bytes 983044
  2.2 19.7 %copy-start.3 = (bf16[5,128,256]{2,1,0:T(8,128)(2,1)S(1)}, bf16[5,128,256]{2,1,0:T(8,128)(2,1)}, u32[]{:S(2)}) copy-start(bf16[5,128,256]{2,1,0:T(8,128)(2,1)} %conv_out.5) | copy-start | bytes 983044
  2.2 19.7 %copy-start.4 = (f32[256]{0:T(256)S(1)}, f32[256]{0:T(256)}, u32[]{:S(2)}) copy-start(f32[256]{0:T(256)} %param.9) | copy-start | bytes 3076
  2.7 9.9 %collective-permute-start.1 = (bf16[2,128,128]{2,0,1:T(2,128)(2,1)S(1)}, bf16[2,128,128]{2,0,1:T(2,128)(2,1)S(1)}, u32[]{:S(2)}, u32[]{:S(2)}) collective-permute-start(bf16[2,128,128]{2,0,1:T(2,128)(2,1)S(1)} %get-tuple-element.18), channel_id=1, source_target_pairs={{8,16},{9,17},{10,18},{11,19},{12,20},{13,21},{14,22},{15,23},{16,... | collective-permute-start | bytes 196616 | tf_op jit(solution)/shard_map/ppermute | solution.py:258
  8.1 4.9 %collective-permute-start = (bf16[2,128,128]{2,0,1:T(2,128)(2,1)S(1)}, bf16[2,128,128]{2,0,1:T(2,128)(2,1)S(1)}, u32[]{:S(2)}, u32[]{:S(2)}) collective-permute-start(bf16[2,128,128]{2,0,1:T(2,128)(2,1)S(1)} %get-tuple-element.19), channel_id=1, source_target_pairs={{0,8},{1,9},{2,10},{3,11},{4,12},{5,13},{6,14},{7,15},{8,0},{9,1},... | collective-permute-start | bytes 196616 | tf_op jit(solution)/shard_map/ppermute | solution.py:258
  13.2 11.3 %collective-permute-start.3 = (bf16[2,32,128]{2,1,0:T(8,128)(2,1)S(1)}, bf16[2,32,128]{2,1,0:T(8,128)(2,1)S(1)}, u32[]{:S(2)}, u32[]{:S(2)}) collective-permute-start(bf16[2,32,128]{2,1,0:T(8,128)(2,1)S(1)} %pad.13), channel_id=1, source_target_pairs={{0,184},{1,2},{2,1},{3,4},{4,3},{5,6},{6,5},{7,127},{8,176},{9,10}... | collective-permute-start | bytes 49160 | tf_op jit(solution)/shard_map/ppermute | solution.py:258
  20.0 4.8 %collective-permute-start.2 = (bf16[2,32,128]{2,1,0:T(8,128)(2,1)S(1)}, bf16[2,32,128]{2,1,0:T(8,128)(2,1)S(1)}, u32[]{:S(2)}, u32[]{:S(2)}) collective-permute-start(bf16[2,32,128]{2,1,0:T(8,128)(2,1)S(1)} %pad.12), channel_id=1, source_target_pairs={{0,1},{1,0},{2,3},{3,2},{4,5},{5,4},{6,7},{7,6},{8,9},{9,8},{10,11... | collective-permute-start | bytes 49160 | tf_op jit(solution)/shard_map/ppermute | solution.py:258
  38.6 13.5 %all-to-all-start.1 = ((bf16[8,2,4,16,128]{4,3,2,1,0:T(8,128)(2,1)}), bf16[8,2,4,16,128]{4,3,2,1,0:T(8,128)(2,1)S(1)}, u32[]{:S(2)}, u32[]{:S(2)}) async-start(bf16[8,2,4,16,128]{4,3,2,1,0:T(8,128)(2,1)} %bitcast.13), calls=%async_computation.1 | async-start | bytes 524288 | tf_op jit(solution)/shard_map/all_to_all | solution.py:314

commit v4 on v3

--- a/solution.py
+++ b/solution.py
@@ -13,12 +13,11 @@
 TAPS = (3, 2, 4, 1, 0, 1, 4, 2, 3)
 NT = (((1,), (1,)), ((), ()))
 VM = pl.BlockSpec(memory_space=pltpu.VMEM)
-PARAMS = pltpu.CompilerParams(vmem_limit_bytes=24 * 2**20)
 F32 = jnp.float32
 BF16 = jnp.bfloat16
 
 
-def call(kernel, out_shape, scratch, cost, *operands):
+def call(kernel, out_shape, scratch, cost, room, *operands):
     many = isinstance(out_shape, list)
     return pl.pallas_call(
         kernel,
@@ -26,12 +25,12 @@
         in_specs=[VM] * len(operands),
         out_specs=[VM] * len(out_shape) if many else VM,
         scratch_shapes=[pltpu.VMEM(s, d) for s, d in scratch],
-        compiler_params=PARAMS,
+        compiler_params=pltpu.CompilerParams(vmem_limit_bytes=room * 2**20),
         cost_estimate=pl.CostEstimate(flops=cost[0], bytes_accessed=cost[1], transcendentals=cost[2]),
     )(*operands)
 
 
-def turn_kernel(state, cells, edges, flat, turned):
+def turn_kernel(here, state, cells, edges, far, near, first, flat, turned):
     chans, rows, cols = state.shape
     flat[...] = state[...].reshape(chans * rows, cols).astype(F32)
     for r in range(rows):
@@ -39,26 +38,42 @@
         cells[r] = turned[r].astype(BF16)
     for k, w in enumerate((0, 1, cols - 2, cols - 1)):
         edges[k] = turned.reshape(rows * cols, chans)[pl.ds(w, rows, stride=cols), :].astype(BF16)
-
-
-def turn(state):
+    odd = jnp.broadcast_to((here[2:3] & 1) == 1, (cols, chans))
+    ends = (0, 1, cols - 2, cols - 1)
+    lines = lambda r: [turned[r + k, w : w + 1] for w in ends for k in range(BORDER)]
+    rest = jnp.zeros((8, chans), F32)
+    top, bottom = (jnp.concatenate(lines(r) + [rest]) for r in (0, rows - BORDER))
+    far[BORDER * cols :] = jnp.where(odd[:16], bottom, top).astype(BF16)
+    near[BORDER * cols :] = jnp.where(odd[:16], top, bottom).astype(BF16)
+    for k in range(BORDER):
+        top, bottom = turned[k], turned[rows - BORDER + k]
+        far[k * cols : (k + 1) * cols] = jnp.where(odd, bottom, top).astype(BF16)
+        near[k * cols : (k + 1) * cols] = jnp.where(odd, top, bottom).astype(BF16)
+    first[...] = state[0:8].astype(F32)
+
+
+def turn(here, state):
     chans, rows, cols = state.shape
+    strip = jax.ShapeDtypeStruct((BORDER * cols + 16, chans), BF16)
     return call(
         turn_kernel,
-        [jax.ShapeDtypeStruct((rows, cols, chans), BF16), jax.ShapeDtypeStruct((4, rows, chans), BF16)],
+        [jax.ShapeDtypeStruct((rows, cols, chans), BF16), jax.ShapeDtypeStruct((4, rows, chans), BF16), strip, strip]
+        + [jax.ShapeDtypeStruct((8, rows, cols), F32)],
         [((chans * rows, cols), F32), ((rows, cols, chans), F32)],
         (0, 4 * state.size, 0),
+        10,
+        here,
         state,
     )
 
 
-def route_kernel(owner, land, here, target, place):
-    count = owner.shape[1]
+def route_kernel(table, here, target, place):
+    count = table.shape[1]
     cols = rows = 8
     wide = lambda v: jnp.broadcast_to(v, (count, count))
     i = lax.broadcasted_iota(jnp.int32, (count, count), 0)
     j = lax.broadcasted_iota(jnp.int32, (count, count), 1)
-    own, wet = wide(owner[...]), wide(1 - land[...])
+    own, wet = wide(table[0:1]), wide(1 - table[1:2])
     down = lambda v: jnp.sum(jnp.where(i == j, v, 0).astype(F32), axis=1, keepdims=True)
     own_i, wet_i = down(own), down(wet)
     same = (own.astype(F32) == own_i) & (wet == 1) & (j < i)
@@ -75,20 +90,66 @@
     total = jnp.full((cols, lanes), 0.0, F32)
     for k in range(rows):
         total = jnp.where(r == k, spot[k * cols : (k + 1) * cols], total)
-    place[...] = total
-
-
-def routes(owner, land, here):
-    shape = jax.ShapeDtypeStruct((8, here.shape[1]), F32)
-    return call(route_kernel, [shape, shape], [], (100000, 20000, 0), owner, land, here)
-
-
-def inner_kernel(here, cells, above, below, conv_in, bias_in, conv_out, bias_sea, state, hidden, sea, field, taps):
+    for k in range(cols):
+        place[k] = jnp.broadcast_to(total[k : k + 1], place.shape[1:])
+
+
+def routes(table, here):
+    lanes = here.shape[1]
+    shapes = [jax.ShapeDtypeStruct((8, lanes), F32), jax.ShapeDtypeStruct((8, 8, lanes), F32)]
+    return call(route_kernel, shapes, [], (100000, 50000, 0), 4, table, here)
+
+
+def strip_kernel(here, edges, got_far, got_near, tall, far, near, field, picked):
+    count, rows, chans = edges.shape
+    length = rows + 2 * BORDER
+    odd_row = jnp.broadcast_to((here[2:3] & 1) == 1, (16, chans))
+    tail = got_far.shape[0] - 16
+    a, b = got_far[tail:].astype(F32), got_near[tail:].astype(F32)
+    above, below = jnp.where(odd_row, b, a), jnp.where(odd_row, a, b)
+    for k in range(count):
+        field[k, 0:BORDER] = above[BORDER * k : BORDER * (k + 1)]
+        field[k, BORDER : BORDER + rows] = edges[k].astype(F32)
+        field[k, BORDER + rows : length] = below[BORDER * k : BORDER * (k + 1)]
+        field[k, length:] = jnp.zeros((field.shape[1] - length, chans), F32)
+        tall[k] = field[k].astype(BF16)
+    col = jnp.broadcast_to(here[3:4], (LONG, chans))
+    odd = (col & 1) == 1
+    seam = (col == 0) | (col == here[4:5])
+    for k in range(BORDER):
+        west, east = field[k], field[BORDER + k]
+        near[k] = jnp.where(odd, west, east).astype(BF16)
+        picked[k] = jnp.where(odd, east, west)
+    for k in range(BORDER):
+        for r in range(length):
+            field[k, r : r + 1] = picked[BORDER - 1 - k, length - 1 - r : length - r]
+    for k in range(BORDER):
+        far[k] = jnp.where(seam, field[k], picked[k]).astype(BF16)
+
+
+def strips(here, edges, got_far, got_near):
+    count, rows, chans = edges.shape
+    two = jax.ShapeDtypeStruct((BORDER, LONG, chans), BF16)
+    return call(
+        strip_kernel,
+        [jax.ShapeDtypeStruct((count, LONG, chans), BF16), two, two],
+        [((count, LONG, chans), F32), ((BORDER, LONG, chans), F32)],
+        (0, 200000, 0),
+        4,
+        here, edges, got_far, got_near,
+    )
+
+
+def inner_kernel(here, cells, got_far, got_near, conv_in, bias_in, conv_out, bias_out, first, hidden, sea, field, taps):
     rows, cols, chans = cells.shape
     hid = bias_in.shape[1]
-    for start, part in ((0, above), (BORDER, cells), (BORDER + rows, below)):
-        for r in range(part.shape[0]):
-            field[start + r, 8 : 8 + cols] = part[r].astype(F32)
+    for r in range(rows):
+        field[BORDER + r, 8 : 8 + cols] = cells[r].astype(F32)
+    odd = jnp.broadcast_to((here[2:3] & 1) == 1, (cols, chans))
+    for k in range(BORDER):
+        far, near = (v[k * cols : (k + 1) * cols].astype(F32) for v in (got_far, got_near))
+        field[k, 8 : 8 + cols] = jnp.where(odd, near, far)
+        field[BORDER + rows + k, 8 : 8 + cols] = jnp.where(odd, far, near)
     for r in range(rows + 2 * BORDER):
         for k in range(3):
             taps[r, :, k * chans : (k + 1) * chans] = field[r, 7 + k : 7 + k + cols].astype(BF16)
@@ -114,17 +175,21 @@
         two = lax.dot_general(sea_weights, hidden[j : j + 2].reshape(2 * cols, hid), NT, preferred_element_type=F32)
         z += [two[:, :cols], two[:, cols:]]
     cut = lambda j, t: z[j][16 * t : 16 * t + 8]
+    upper = bias_out[:, :128]
+    lane = lax.broadcasted_iota(jnp.int32, (8, upper.shape[1]), 1)
+    channel = lax.broadcasted_iota(jnp.int32, (8, upper.shape[1]), 0)
+    bias_sea = jnp.sum(jnp.where(lane == channel, upper, 0.0), axis=1, keepdims=True)
     for r in range(rows):
         j = r + 1
         mid = cut(j, 0) + cut(j - 1, 2) + cut(j + 1, 2)
         plus = cut(j, 1) + cut(j + 1, 3) + cut(j - 1, 4)
         minus = cut(j, 1) + cut(j - 1, 3) + cut(j + 1, 4)
-        total = mid + pltpu.roll(plus, cols - 1, 1) + pltpu.roll(minus, 1, 1) + bias_sea[...]
+        total = mid + pltpu.roll(plus, cols - 1, 1) + pltpu.roll(minus, 1, 1) + bias_sea
         sea[:, r] = total
-    sea[...] += state[0:8].astype(F32)
-
-
-def inner_part(here, cells, above, below, conv_in, bias_in, conv_out, bias_sea, state):
+    sea[...] += first[...]
+
+
+def inner_part(here, cells, got_far, got_near, conv_in, bias_in, conv_out, bias_out, first):
     rows, cols, chans = cells.shape
     hid = conv_in.shape[1]
     return call(
@@ -132,15 +197,22 @@
         [jax.ShapeDtypeStruct((rows + 2, cols, hid), BF16), jax.ShapeDtypeStruct((8, rows, cols), F32)],
         [((rows + 4, cols + 16, chans), F32), ((rows + 4, cols, 3 * chans), BF16)],
         (2 * 18 * 128 * (1152 + 80) * 256, 3000000, 18 * 128 * 256),
-        here, cells, above, below, conv_in, bias_in, conv_out, bias_sea, state,
-    )
-
-
-def rim_kernel(here, target, edges, sides, conv_in, bias_in, conv_out, sea, rim, blocks, field, tall):
+        14,
+        here, cells, got_far, got_near, conv_in, bias_in, conv_out, bias_out, first,
+    )
+
+
+def rim_kernel(here, target, edges, far, near, conv_in, bias_in, conv_out, sea, rim, blocks, field, tall):
     hid = bias_in.shape[1]
     n_blocks, n_sea, rows, cols = blocks.shape
-    for k, (part, at) in enumerate(((sides, 0), (sides, 1), (edges, 0), (edges, 1), (edges, 2), (edges, 3), (sides, 2), (sides, 3))):
-        field[k, 0:LONG] = part[at].astype(F32)
+    odd = jnp.broadcast_to((here[3:4] & 1) == 1, (LONG, field.shape[2]))
+    for k, w in enumerate((-1, -1, 0, 1, 2, 3, -1, -1)):
+        if w >= 0:
+            field[k, 0:LONG] = edges[w].astype(F32)
+        else:
+            i, j = (k, k) if k < 2 else (k - 6, k - 4)
+            one, two = far[i].astype(F32), near[j].astype(F32)
+            field[k, 0:LONG] = jnp.where(odd, two, one) if k < 2 else jnp.where(odd, one, two)
         field[k, LONG : LONG + 8] = jnp.zeros((8, field.shape[2]), F32)
     weights = jnp.concatenate([conv_in[t] for t in TAPS], axis=1)
     data = []
@@ -170,7 +242,7 @@
             blocks[b, o] = jnp.where(target[0:1] == b, v, 0.0).astype(BF16)
 
 
-def rim_part(here, target, edges, sides, conv_in, bias_in, conv_out, sea, n_blocks, n_sea):
+def rim_part(here, target, edges, far, near, conv_in, bias_in, conv_out, sea, n_blocks, n_sea):
     rows, cols = sea.shape[1:]
     chans = edges.shape[2]
     hid = conv_in.shape[1]
@@ -179,7 +251,8 @@
         [jax.ShapeDtypeStruct((4, LONG, hid), BF16), jax.ShapeDtypeStruct((n_blocks, n_sea, rows, cols), BF16)],
         [((8, LONG + 8, chans), F32), ((4, LONG, hid), F32)],
         (2 * 128 * 1152 * 256, 1500000, 128 * 256),
-        here, target, edges, sides, conv_in, bias_in, conv_out, sea,
+        10,
+        here, target, edges, far, near, conv_in, bias_in, conv_out, sea,
     )
 
 
@@ -214,35 +287,31 @@
         jax.ShapeDtypeStruct((chans, rows, cols), BF16),
         [((rows + 2, cols + 16, 5 * chans), F32), ((chans * rows, cols), F32)],
         (2 * 18 * 128 * 640 * 256, 3000000, 0),
+        18,
         hidden, rim, cells, conv_out, bias_out,
     )
 
 
 def sort_kernel(place, held, sent):
+    count, chans, rows, cols = held.shape
     half = sent.shape[0] // 2
-    parts = [held[k].astype(F32) for k in range(held.shape[0])]
-    for p in range(half):
-        total = jnp.zeros_like(parts[0])
-        for k, v in enumerate(parts):
-            total = jnp.where((place[k : k + 1] == p)[None], v, total)
-        sent[p] = total.astype(BF16)
+    named = [place[k] for k in range(count)]
+    chosen = [[v == p for v in named] for p in range(half)]
+    for o in range(chans):
+        for i in range(0, rows, 16):
+            parts = [held[k, o, i : i + 16].astype(F32) for k in range(count)]
+            parts = [(v[:8], v[8:]) for v in parts]
+            for p in range(half):
+                total = [jnp.zeros((8, cols), F32)] * 2
+                for k, v in enumerate(parts):
+                    total = [jnp.where(chosen[p][k], x, t) for x, t in zip(v, total)]
+                sent[p, o, i : i + 16] = jnp.concatenate(total).astype(BF16)
     sent[half:] = jnp.zeros((half,) + sent.shape[1:], BF16)
 
 
 def sort_tiles(place, held, count):
     shape = jax.ShapeDtypeStruct((count,) + held.shape[1:], BF16)
-    return call(sort_kernel, shape, [], (100000, 6 * held.size, 0), place, held)
-
-
-def merge_kernel(got, ocean):
-    total = got[0].astype(F32)
-    for k in range(1, got.shape[0]):
-        total += got[k].astype(F32)
-    ocean[...] = total.astype(BF16)
-
-
-def merge(got):
-    return call(merge_kernel, jax.ShapeDtypeStruct(got.shape[1:], BF16), [], (100000, 2 * got.size, 0), got)
+    return call(sort_kernel, shape, [], (100000, 6 * held.size, 0), 6, place, held)
 
 
 def exchange(values, partner):
@@ -283,36 +352,29 @@
     chans, height, width = state.shape
     rows, cols = lax.axis_size("row"), lax.axis_size("col")
     r, c = lax.axis_index("row"), lax.axis_index("col")
-    lines = (r > 0, r < rows - 1, r, c, 0, 0, 0, 0)
+    lines = (r > 0, r < rows - 1, r, c, cols - 1, 0, 0, 0)
     here = jnp.concatenate([jnp.full((1, 128), v, jnp.int32) for v in lines])
-    cells, edges = turn(state)
-
-    odd = r % 2 == 1
-    top, bottom = cells[:BORDER], cells[height - BORDER :]
-    got_far = exchange(jnp.where(odd, bottom, top), row_far)
-    got_near = exchange(jnp.where(odd, top, bottom), row_near)
-    above, below = jnp.where(odd, got_near, got_far), jnp.where(odd, got_far, got_near)
-
+    cells, edges, far, near, first = turn(here, state)
+
+    far_rows, near_rows = exchange(far, row_far), exchange(near, row_near)
+
+    tall, far, near = strips(here, edges, far_rows, near_rows)
+    got_far = exchange(far, col_far)
+    got_near = exchange(near, col_near)
     odd = c % 2 == 1
-    pick = lambda v: jnp.stack([v[:, 0], v[:, 1], v[:, width - 2], v[:, width - 1]])
-    tall = jnp.concatenate([pick(above), edges, pick(below)], axis=1)
-    full = lambda v: jnp.pad(v, ((0, 0), (0, LONG - v.shape[1]), (0, 0)))
-    west, east = tall[:BORDER], tall[BORDER:]
-    far = jnp.where(odd, east, west)
-    far = jnp.where((c == 0) | (c == cols - 1), far[::-1, ::-1], far)
-    got_far = exchange(full(far), col_far)
-    got_near = exchange(full(jnp.where(odd, west, east)), col_near)
-    sides = jnp.concatenate([jnp.where(odd, got_near, got_far), jnp.where(odd, got_far, got_near)])
-
-    target, place = routes(owner, land, here)
-    bias_in = bias_in[None]
-    hidden, sea = inner_part(here, cells, above, below, conv_in, bias_in, conv_out, bias_out[:8, None], state)
-    rim, blocks = rim_part(here, target, full(tall), sides, conv_in, bias_in, conv_out, sea, cols, OC)
+    got_near = jnp.concatenate([jnp.where(odd, got_near, 0), jnp.where(odd, 0, got_near)])
+
+    target, place = routes(jnp.concatenate([owner, land]), here)
+    bias_in, bias_out = bias_in[None], bias_out[None]
+    wide = cells.astype(F32)
+    hidden, sea = inner_part(here, wide, far_rows, near_rows, conv_in, bias_in, conv_out, bias_out, first)
+    rim, blocks = rim_part(here, target, tall, got_far, got_near, conv_in, bias_in, conv_out, sea, cols, OC)
     held = lax.all_to_all(blocks, "col", 0, 0, tiled=True)
-    new_state = out_part(hidden, rim, cells, conv_out, bias_out[None])
+    new_state = out_part(hidden, rim, cells, conv_out, bias_out)
     sent = sort_tiles(place, held, rows * CAP).reshape((rows, CAP, OC, height, width))
     got = lax.all_to_all(sent, "row", 0, 0, tiled=True)
-    return (new_state[None], merge(got)[None, None])
+    ocean = jnp.sum(got.astype(F32), axis=0).astype(BF16)
+    return (new_state[None], ocean[None, None])
 
 
 def solution(mesh):

time: 53.1 us -> 52.6 us (level)
  waiting for transfers between devices: 6.71 us -> 4.75 us
  other arithmetic: 0.22 us -> 1.45 us
  local copies, waits for them, and re-layouts: 1.63 us -> 2.37 us
  Pallas kernels: 8.1 us -> 7.49 us
    unnamed x16 -> x14, local copies, waits for them, and re-layouts: 1.07 us -> 2.33 us
    all_to_all x1, waiting for transfers between devices: 5.99 us -> 4.74 us  [local(): got = lax.all_to_all(sent, 'row', 0, 0, tiled=True)]
    ppermute x4, waiting for transfers between devices: 0.71 us -> 0.01 us  [exchange(): return lax.ppermute(values, ALL, pairs)]
    concatenate x2, other arithmetic: 0.03 us -> 0.69 us  [the longest x1 0.68 us: local(): target, place = routes(jnp.concatenate([owner, land]), here)]
    reduce_sum x0 -> x1, other arithmetic: none -> 0.65 us  [local(): ocean = jnp.sum(got.astype(F32), axis=0).astype(BF16)]
    pallas_call x7, Pallas kernels: 8.1 us -> 7.49 us  [call(): pl.pallas_call(kernel, out_shape=out_shape, in_specs=[VM] * len(operands)...]
  transfers between devices with their start and end apart: 5 -> 5, of which waited for: 3 -> 1; matrix products, arithmetic and copies ran while one was open for 0% -> 2% of each run, Pallas kernels for 10% -> 10%
where the time goes in v4:
time: 52.6 us; the launch traced here: 52.2 us
  starting transfers between devices  22.8 us (43%)
  blocking collectives  12.4 us (24%)
  Pallas kernels  7.49 us (14%)
  waiting for transfers between devices  4.75 us (9%)
  local copies, waits for them, and re-layouts  2.37 us (5%)
  other arithmetic  1.45 us (3%)
  between operations  0.9 us (2%)
    ppermute x4, starting transfers between devices, exchange(): return lax.ppermute(values, ALL, pairs)  18 us
    all_to_all x1, blocking collectives, local(): held = lax.all_to_all(blocks, 'col', 0, 0, tiled=True)  12.4 us
    pallas_call x7, Pallas kernels, call(): pl.pallas_call(kernel, out_shape=out_shape, in_specs=[VM] * len(operands)...  7.49 us
    all_to_all x1, starting transfers between devices, local(): got = lax.all_to_all(sent, 'row', 0, 0, tiled=True)  4.82 us
    all_to_all x1, waiting for transfers between devices, local(): got = lax.all_to_all(sent, 'row', 0, 0, tiled=True)  4.74 us
    unnamed x14, local copies, waits for them, and re-layouts  2.33 us
  transfers between devices with their start and end apart: 5, of which 1 were waited for; matrix products, arithmetic and copies ran while one was open for 2% of the time, Pallas kernels for 10%

profile of v4, /device:TPU:1, one launch (start us, length us, event | category | flops | bytes accessed | tf_op | source)
XLA Modules:
  0.0 52.2 jit_solution(9005541011156201654)
XLA Ops:
  0.6 0.0 copy-start.3
  0.6 0.0 copy-start.4
  0.8 0.0 copy-start
  0.8 1.0 %copy-done = bf16[1,128,16,128]{3,2,1,0:T(8,128)(2,1)S(1)} copy-done((bf16[1,128,16,128]{3,2,1,0:T(8,128)(2,1)S(1)}, bf16[1,128,16,128]{3,2,1,0:T(8,128)(2,1)}, u32[]{:S(2)}) %copy-start) | copy-done | bytes 524312
  1.8 0.0 copy-start.1
  1.8 0.0 copy-start.2
  1.8 0.5 shard_map.86
  2.3 5.4 %collective-permute-start = (bf16[272,128]{1,0:T(8,128)(2,1)S(1)}, bf16[272,128]{1,0:T(8,128)(2,1)S(1)}, u32[]{:S(2)}, u32[]{:S(2)}) collective-permute-start(bf16[272,128]{1,0:T(8,128)(2,1)S(1)} %get-tuple-element.17), channel_id=1, source_target_pairs={{8,16},{9,17},{10,18},{11,19},{12,20},{13,21},{14,22},{15,23},{16,... | collective-permute-start | bytes 208904 | tf_op jit(solution)/shard_map/ppermute | solution.py:327
  7.7 4.1 %collective-permute-start.1 = (bf16[272,128]{1,0:T(8,128)(2,1)S(1)}, bf16[272,128]{1,0:T(8,128)(2,1)S(1)}, u32[]{:S(2)}, u32[]{:S(2)}) collective-permute-start(bf16[272,128]{1,0:T(8,128)(2,1)S(1)} %get-tuple-element.18), channel_id=1, source_target_pairs={{0,8},{1,9},{2,10},{3,11},{4,12},{5,13},{6,14},{7,15},{8,0},{9,1},... | collective-permute-start | bytes 208904 | tf_op jit(solution)/shard_map/ppermute | solution.py:327
  11.7 0.7 %pad_add_fusion.table = s32[2,64]{1,0:T(2,128)S(1)} fusion(s32[1,64]{1,0:T(1,128)} %param.12, s32[1,64]{1,0:T(1,128)} %param.13), kind=kLoop, calls=%fused_computation.3 | loop fusion | flops 128 | bytes 1024 | tf_op jit(solution)/shard_map/concatenate | solution.py:367
  12.4 0.2 shard_map.88
  12.6 0.1 convert_element_type.17.cells
  12.7 0.0 collective-permute-done.got_far
  12.7 0.0 collective-permute-done.1.got_near
  12.8 6.6 %collective-permute-start.2 = (bf16[2,32,128]{2,1,0:T(8,128)(2,1)S(1)}, bf16[2,32,128]{2,1,0:T(8,128)(2,1)S(1)}, u32[]{:S(2)}, u32[]{:S(2)}) collective-permute-start(bf16[2,32,128]{2,1,0:T(8,128)(2,1)S(1)} %get-tuple-element.24), channel_id=1, source_target_pairs={{0,184},{1,2},{2,1},{3,4},{4,3},{5,6},{6,5},{7,127},{8,176},{9,10}... | collective-permute-start | bytes 49160 | tf_op jit(solution)/shard_map/ppermute | solution.py:327
  19.4 1.9 %collective-permute-start.3 = (bf16[2,32,128]{2,1,0:T(8,128)(2,1)S(1)}, bf16[2,32,128]{2,1,0:T(8,128)(2,1)S(1)}, u32[]{:S(2)}, u32[]{:S(2)}) collective-permute-start(bf16[2,32,128]{2,1,0:T(8,128)(2,1)S(1)} %get-tuple-element.25), channel_id=1, source_target_pairs={{0,1},{1,0},{2,3},{3,2},{4,5},{5,4},{6,7},{7,6},{8,9},{9,8},{10,11... | collective-permute-start | bytes 49160 | tf_op jit(solution)/shard_map/ppermute | solution.py:327
  21.4 0.0 copy-done.3
  21.4 0.0 copy-done.4
  21.4 0.0 copy-done.1
  21.4 0.0 copy-done.2
  21.4 2.6 %shard_map.87 = (bf16[18,128,256]{2,1,0:T(8,128)(2,1)S(1)}, f32[8,16,128]{2,1,0:T(8,128)S(1)}) custom-call(s32[8,128]{1,0:T(8,128)S(1)} %concatenate.13.here, f32[16,128,128]{2,1,0:T(8,128)S(1)} %convert_element_type.17.cells, bf16[272,128]{1,0:T(8,128)(2,1)S(1)} %collective-permute-done.got_far, bf16[272,128]{1,0:T(8,128)(2,1)S(1)} %collective-permute-done.1.got_near, ...), custom_call_target="tpu_custom_call" | custom-call | flops 1453326336 | bytes 3000000 | tf_op jit(solution)/shard_map/pallas_call | solution.py:22
  24.0 0.0 copy-start.5
  24.0 0.0 collective-permute-done.3
  24.0 0.0 collective-permute-done.2.far
  24.1 0.7 %shard_map.90 = (bf16[4,32,256]{2,1,0:T(8,128)(2,1)S(1)}, bf16[8,4,16,128]{3,2,1,0:T(8,128)(2,1)S(1)}) custom-call(s32[8,128]{1,0:T(8,128)S(1)} %concatenate.13.here, f32[8,128]{1,0:T(8,128)S(1)} %get-tuple-element.21.target, bf16[4,32,128]{2,1,0:T(8,128)(2,1)S(1)} %get-tuple-element.23.edges, bf16[2,32,128]{2,1,0:T(8,128)(2,1)S(1)} %collective-permute-done.2.far, ...), custom_call_target="tpu_custom_call" | custom-call | flops 75497472 | bytes 1500000 | tf_op jit(solution)/shard_map/pallas_call | solution.py:22
  24.7 12.4 %all_to_all.10.held = bf16[8,4,16,128]{3,2,1,0:T(8,128)(2,1)S(1)} all-to-all(bf16[8,4,16,128]{3,2,1,0:T(8,128)(2,1)S(1)} %get-tuple-element.29), channel_id=1, replica_groups=mesh['face'=8,'row'=8,'col'=8] {'col'}, dimensions={0} | all-to-all | bytes 262144 | tf_op jit(solution)/shard_map/all_to_all | solution.py:372
  37.2 0.8 %shard_map.92 = bf16[16,4,16,128]{3,2,1,0:T(8,128)(2,1)} custom-call(f32[8,8,128]{2,1,0:T(8,128)S(1)} %get-tuple-element.28.place, bf16[8,4,16,128]{3,2,1,0:T(8,128)(2,1)S(1)} %all_to_all.10.held), custom_call_target="tpu_custom_call" | custom-call | flops 100000 | bytes 393216 | tf_op jit(solution)/shard_map/pallas_call | solution.py:22
  38.0 0.0 copy-done.5
  38.0 4.8 %all-to-all-start.1 = ((bf16[8,2,4,16,128]{4,3,2,1,0:T(8,128)(2,1)}), bf16[8,2,4,16,128]{4,3,2,1,0:T(8,128)(2,1)S(1)}, u32[]{:S(2)}, u32[]{:S(2)}) async-start(bf16[8,2,4,16,128]{4,3,2,1,0:T(8,128)(2,1)} %bitcast.4), calls=%async_computation.1 | async-start | bytes 524288 | tf_op jit(solution)/shard_map/all_to_all | solution.py:375
  42.8 0.0 copy-start.6
  42.8 1.3 %copy-done.6 = bf16[18,128,256]{2,1,0:T(8,128)(2,1)S(1)} copy-done((bf16[18,128,256]{2,1,0:T(8,128)(2,1)S(1)}, bf16[18,128,256]{2,1,0:T(8,128)(2,1)}, u32[]{:S(2)}) %copy-start.6) | copy-done | bytes 1179672
  44.1 2.7 %shard_map.91 = bf16[128,16,128]{2,1,0:T(8,128)(2,1)} custom-call(bf16[18,128,256]{2,1,0:T(8,128)(2,1)S(1)} %copy-done.6, bf16[4,32,256]{2,1,0:T(8,128)(2,1)S(1)} %get-tuple-element.27.rim, bf16[16,128,128]{2,1,0:T(8,128)(2,1)S(1)} %get-tuple-element.16.cells, bf16[5,128,256]{2,1,0:T(8,128)(2,1)S(1)} %copy-done.2, f32[1,128]{1,0:T(1,128)S(1)} %bitcast.10), custom_call_target="tpu_custom_call" | custom-call | flops 754974720 | bytes 3000000 | tf_op jit(solution)/shard_map/pallas_call | solution.py:22
  46.8 4.7 %all-to-all-done.1 = bf16[8,2,4,16,128]{4,3,2,1,0:T(8,128)(2,1)S(1)} async-done(((bf16[8,2,4,16,128]{4,3,2,1,0:T(8,128)(2,1)}), bf16[8,2,4,16,128]{4,3,2,1,0:T(8,128)(2,1)S(1)}, u32[]{:S(2)}, u32[]{:S(2)}) %all-to-all-start.1) | async-done | bytes 262176 | tf_op jit(solution)/shard_map/all_to_all | solution.py:375
  51.5 0.7 %reduce_sum.12 = bf16[2,4,16,128]{3,2,1,0:T(8,128)(2,1)} reduce(bf16[8,2,4,16,128]{4,3,2,1,0:T(8,128)(2,1)S(1)} %all-to-all-done.1, bf16[]{:T(256)} %constant.30.clone.1), dimensions={0}, to_apply=%region_0.1 | reduce | flops 114688 | bytes 294914 | tf_op jit(solution)/shard_map/reduce_sum | solution.py:376
  (11 shorter events, 0.1 us)
Async XLA Ops:
  0.6 20.7 %copy-start.3 = (f32[256]{0:T(256)S(1)}, f32[256]{0:T(256)}, u32[]{:S(2)}) copy-start(f32[256]{0:T(256)} %param.9) | copy-start | bytes 3076
  0.6 20.7 %copy-start.4 = (f32[128]{0:T(128)S(1)}, f32[128]{0:T(128)}, u32[]{:S(2)}) copy-start(f32[128]{0:T(128)} %param.11) | copy-start | bytes 1540
  0.8 1.0 %copy-start = (bf16[1,128,16,128]{3,2,1,0:T(8,128)(2,1)S(1)}, bf16[1,128,16,128]{3,2,1,0:T(8,128)(2,1)}, u32[]{:S(2)}) copy-start(bf16[1,128,16,128]{3,2,1,0:T(8,128)(2,1)} %param.7) | copy-start | bytes 1572868
  1.8 19.6 %copy-start.1 = (bf16[5,256,128]{2,1,0:T(8,128)(2,1)S(1)}, bf16[5,256,128]{2,1,0:T(8,128)(2,1)}, u32[]{:S(2)}) copy-start(bf16[5,256,128]{2,1,0:T(8,128)(2,1)} %conv_in.3) | copy-start | bytes 983044
  1.8 19.6 %copy-start.2 = (bf16[5,128,256]{2,1,0:T(8,128)(2,1)S(1)}, bf16[5,128,256]{2,1,0:T(8,128)(2,1)}, u32[]{:S(2)}) copy-start(bf16[5,128,256]{2,1,0:T(8,128)(2,1)} %conv_out.5) | copy-start | bytes 983044
  2.3 10.5 %collective-permute-start = (bf16[272,128]{1,0:T(8,128)(2,1)S(1)}, bf16[272,128]{1,0:T(8,128)(2,1)S(1)}, u32[]{:S(2)}, u32[]{:S(2)}) collective-permute-start(bf16[272,128]{1,0:T(8,128)(2,1)S(1)} %get-tuple-element.17), channel_id=1, source_target_pairs={{8,16},{9,17},{10,18},{11,19},{12,20},{13,21},{14,22},{15,23},{16,... | collective-permute-start | bytes 208904 | tf_op jit(solution)/shard_map/ppermute | solution.py:327
  7.7 5.1 %collective-permute-start.1 = (bf16[272,128]{1,0:T(8,128)(2,1)S(1)}, bf16[272,128]{1,0:T(8,128)(2,1)S(1)}, u32[]{:S(2)}, u32[]{:S(2)}) collective-permute-start(bf16[272,128]{1,0:T(8,128)(2,1)S(1)} %get-tuple-element.18), channel_id=1, source_target_pairs={{0,8},{1,9},{2,10},{3,11},{4,12},{5,13},{6,14},{7,15},{8,0},{9,1},... | collective-permute-start | bytes 208904 | tf_op jit(solution)/shard_map/ppermute | solution.py:327
  12.8 11.2 %collective-permute-start.2 = (bf16[2,32,128]{2,1,0:T(8,128)(2,1)S(1)}, bf16[2,32,128]{2,1,0:T(8,128)(2,1)S(1)}, u32[]{:S(2)}, u32[]{:S(2)}) collective-permute-start(bf16[2,32,128]{2,1,0:T(8,128)(2,1)S(1)} %get-tuple-element.24), channel_id=1, source_target_pairs={{0,184},{1,2},{2,1},{3,4},{4,3},{5,6},{6,5},{7,127},{8,176},{9,10}... | collective-permute-start | bytes 49160 | tf_op jit(solution)/shard_map/ppermute | solution.py:327
  19.4 4.6 %collective-permute-start.3 = (bf16[2,32,128]{2,1,0:T(8,128)(2,1)S(1)}, bf16[2,32,128]{2,1,0:T(8,128)(2,1)S(1)}, u32[]{:S(2)}, u32[]{:S(2)}) collective-permute-start(bf16[2,32,128]{2,1,0:T(8,128)(2,1)S(1)} %get-tuple-element.25), channel_id=1, source_target_pairs={{0,1},{1,0},{2,3},{3,2},{4,5},{5,4},{6,7},{7,6},{8,9},{9,8},{10,11... | collective-permute-start | bytes 49160 | tf_op jit(solution)/shard_map/ppermute | solution.py:327
  24.0 14.0 %copy-start.5 = (bf16[18,128,256]{2,1,0:T(8,128)(2,1)}, bf16[18,128,256]{2,1,0:T(8,128)(2,1)S(1)}, u32[]{:S(2)}) copy-start(bf16[18,128,256]{2,1,0:T(8,128)(2,1)S(1)} %get-tuple-element.20.hidden) | copy-start | bytes 3538948
  38.0 13.5 %all-to-all-start.1 = ((bf16[8,2,4,16,128]{4,3,2,1,0:T(8,128)(2,1)}), bf16[8,2,4,16,128]{4,3,2,1,0:T(8,128)(2,1)S(1)}, u32[]{:S(2)}, u32[]{:S(2)}) async-start(bf16[8,2,4,16,128]{4,3,2,1,0:T(8,128)(2,1)} %bitcast.4), calls=%async_computation.1 | async-start | bytes 524288 | tf_op jit(solution)/shard_map/all_to_all | solution.py:375
  42.8 1.3 %copy-start.6 = (bf16[18,128,256]{2,1,0:T(8,128)(2,1)S(1)}, bf16[18,128,256]{2,1,0:T(8,128)(2,1)}, u32[]{:S(2)}) copy-start(bf16[18,128,256]{2,1,0:T(8,128)(2,1)} %copy-done.5) | copy-start | bytes 3538948

commit v5 on v4

--- a/solution.py
+++ b/solution.py
@@ -10,6 +10,8 @@
 ALL = ("face", "row", "col")
 BORDER = 2
 LONG = 32
+SHARE = 6
+OWNER_AT, LAND_AT, IN_AT, OUT_AT = 0, 128, 256, 512
 TAPS = (3, 2, 4, 1, 0, 1, 4, 2, 3)
 NT = (((1,), (1,)), ((), ()))
 VM = pl.BlockSpec(memory_space=pltpu.VMEM)
@@ -30,12 +32,11 @@
     )(*operands)
 
 
-def turn_kernel(here, state, cells, edges, far, near, first, flat, turned):
+def turn_kernel(here, state, turned, edges, far, near, first, flat):
     chans, rows, cols = state.shape
     flat[...] = state[...].reshape(chans * rows, cols).astype(F32)
     for r in range(rows):
         turned[r] = flat[pl.ds(r, chans, stride=rows), :].T
-        cells[r] = turned[r].astype(BF16)
     for k, w in enumerate((0, 1, cols - 2, cols - 1)):
         edges[k] = turned.reshape(rows * cols, chans)[pl.ds(w, rows, stride=cols), :].astype(BF16)
     odd = jnp.broadcast_to((here[2:3] & 1) == 1, (cols, chans))
@@ -57,9 +58,9 @@
     strip = jax.ShapeDtypeStruct((BORDER * cols + 16, chans), BF16)
     return call(
         turn_kernel,
-        [jax.ShapeDtypeStruct((rows, cols, chans), BF16), jax.ShapeDtypeStruct((4, rows, chans), BF16), strip, strip]
+        [jax.ShapeDtypeStruct((rows, cols, chans), F32), jax.ShapeDtypeStruct((4, rows, chans), BF16), strip, strip]
         + [jax.ShapeDtypeStruct((8, rows, cols), F32)],
-        [((chans * rows, cols), F32), ((rows, cols, chans), F32)],
+        [((chans * rows, cols), F32)],
         (0, 4 * state.size, 0),
         10,
         here,
@@ -67,13 +68,14 @@
     )
 
 
-def route_kernel(table, here, target, place):
-    count = table.shape[1]
+def route_kernel(pack, here, target, place):
+    count = 64
     cols = rows = 8
     wide = lambda v: jnp.broadcast_to(v, (count, count))
     i = lax.broadcasted_iota(jnp.int32, (count, count), 0)
     j = lax.broadcasted_iota(jnp.int32, (count, count), 1)
-    own, wet = wide(table[0:1]), wide(1 - table[1:2])
+    own, land = (pack[:, at : at + count].astype(jnp.int32) for at in (OWNER_AT, LAND_AT))
+    own, wet = wide(own), wide(1 - land)
     down = lambda v: jnp.sum(jnp.where(i == j, v, 0).astype(F32), axis=1, keepdims=True)
     own_i, wet_i = down(own), down(wet)
     same = (own.astype(F32) == own_i) & (wet == 1) & (j < i)
@@ -94,10 +96,10 @@
         place[k] = jnp.broadcast_to(total[k : k + 1], place.shape[1:])
 
 
-def routes(table, here):
+def routes(pack, here):
     lanes = here.shape[1]
     shapes = [jax.ShapeDtypeStruct((8, lanes), F32), jax.ShapeDtypeStruct((8, 8, lanes), F32)]
-    return call(route_kernel, shapes, [], (100000, 50000, 0), 4, table, here)
+    return call(route_kernel, shapes, [], (100000, 50000, 0), 4, pack, here)
 
 
 def strip_kernel(here, edges, got_far, got_near, tall, far, near, field, picked):
@@ -140,9 +142,11 @@
     )
 
 
-def inner_kernel(here, cells, got_far, got_near, conv_in, bias_in, conv_out, bias_out, first, hidden, sea, field, taps):
+def inner_kernel(here, cells, got_far, got_near, conv_in, pack, conv_out, first, *refs):
+    *hidden, sea, field, taps = refs
     rows, cols, chans = cells.shape
-    hid = bias_in.shape[1]
+    hid = conv_in.shape[1]
+    bias_in = pack[:, IN_AT : IN_AT + hid]
     for r in range(rows):
         field[BORDER + r, 8 : 8 + cols] = cells[r].astype(F32)
     odd = jnp.broadcast_to((here[2:3] & 1) == 1, (cols, chans))
@@ -160,7 +164,7 @@
     step = 3
     for j in range(0, rows + 2, step):
         data = jnp.concatenate([taps[j + d : j + d + step].reshape(step * cols, 3 * chans) for d in range(3)], axis=1)
-        x = lax.dot_general(data, weights, NT, preferred_element_type=F32) + bias_in[...]
+        x = lax.dot_general(data, weights, NT, preferred_element_type=F32) + bias_in
         x = jax.nn.gelu(x).reshape(step, cols, hid)
         for d in range(step):
             here_in = inside
@@ -168,14 +172,14 @@
                 here_in = inside & keep[0:1]
             if j + d == rows + 1:
                 here_in = inside & keep[1:2]
-            hidden[j + d] = jnp.where(here_in, x[d], 0.0).astype(BF16)
+            hidden[(j + d) // SHARE][(j + d) % SHARE] = jnp.where(here_in, x[d], 0.0).astype(BF16)
     sea_weights = conv_out[:, 0:16].reshape(5 * 16, hid)
     z = []
     for j in range(0, rows + 2, 2):
-        two = lax.dot_general(sea_weights, hidden[j : j + 2].reshape(2 * cols, hid), NT, preferred_element_type=F32)
+        two = lax.dot_general(sea_weights, hidden[j // SHARE][j % SHARE : j % SHARE + 2].reshape(2 * cols, hid), NT, preferred_element_type=F32)
         z += [two[:, :cols], two[:, cols:]]
     cut = lambda j, t: z[j][16 * t : 16 * t + 8]
-    upper = bias_out[:, :128]
+    upper = pack[:, OUT_AT : OUT_AT + chans]
     lane = lax.broadcasted_iota(jnp.int32, (8, upper.shape[1]), 1)
     channel = lax.broadcasted_iota(jnp.int32, (8, upper.shape[1]), 0)
     bias_sea = jnp.sum(jnp.where(lane == channel, upper, 0.0), axis=1, keepdims=True)
@@ -189,21 +193,23 @@
     sea[...] += first[...]
 
 
-def inner_part(here, cells, got_far, got_near, conv_in, bias_in, conv_out, bias_out, first):
+def inner_part(here, cells, got_far, got_near, conv_in, pack, conv_out, first):
     rows, cols, chans = cells.shape
     hid = conv_in.shape[1]
     return call(
         inner_kernel,
-        [jax.ShapeDtypeStruct((rows + 2, cols, hid), BF16), jax.ShapeDtypeStruct((8, rows, cols), F32)],
+        [jax.ShapeDtypeStruct((SHARE, cols, hid), BF16)] * ((rows + 2) // SHARE)
+        + [jax.ShapeDtypeStruct((8, rows, cols), F32)],
         [((rows + 4, cols + 16, chans), F32), ((rows + 4, cols, 3 * chans), BF16)],
         (2 * 18 * 128 * (1152 + 80) * 256, 3000000, 18 * 128 * 256),
         14,
-        here, cells, got_far, got_near, conv_in, bias_in, conv_out, bias_out, first,
-    )
-
-
-def rim_kernel(here, target, edges, far, near, conv_in, bias_in, conv_out, sea, rim, blocks, field, tall):
-    hid = bias_in.shape[1]
+        here, cells, got_far, got_near, conv_in, pack, conv_out, first,
+    )
+
+
+def rim_kernel(here, target, edges, far, near, conv_in, pack, conv_out, sea, rim, blocks, field, tall):
+    hid = conv_in.shape[1]
+    bias_in = pack[:, IN_AT : IN_AT + hid]
     n_blocks, n_sea, rows, cols = blocks.shape
     odd = jnp.broadcast_to((here[3:4] & 1) == 1, (LONG, field.shape[2]))
     for k, w in enumerate((-1, -1, 0, 1, 2, 3, -1, -1)):
@@ -218,7 +224,7 @@
     data = []
     for k in (1, 2, 5, 6):
         data.append(jnp.concatenate([field[k + dc, dr : dr + LONG].astype(BF16) for dr in range(3) for dc in (-1, 0, 1)], axis=1))
-    x = lax.dot_general(jnp.concatenate(data, axis=0), weights, NT, preferred_element_type=F32) + bias_in[...]
+    x = lax.dot_general(jnp.concatenate(data, axis=0), weights, NT, preferred_element_type=F32) + bias_in
     x = jax.nn.gelu(x)
     keep = jnp.concatenate([here[0:2]] * (hid // here.shape[1]), axis=1) > 0
     row = lax.broadcasted_iota(jnp.int32, (LONG, hid), 0)
@@ -242,7 +248,7 @@
             blocks[b, o] = jnp.where(target[0:1] == b, v, 0.0).astype(BF16)
 
 
-def rim_part(here, target, edges, far, near, conv_in, bias_in, conv_out, sea, n_blocks, n_sea):
+def rim_part(here, target, edges, far, near, conv_in, pack, conv_out, sea, n_blocks, n_sea):
     rows, cols = sea.shape[1:]
     chans = edges.shape[2]
     hid = conv_in.shape[1]
@@ -252,17 +258,18 @@
         [((8, LONG + 8, chans), F32), ((4, LONG, hid), F32)],
         (2 * 128 * 1152 * 256, 1500000, 128 * 256),
         10,
-        here, target, edges, far, near, conv_in, bias_in, conv_out, sea,
-    )
-
-
-def out_kernel(hidden, rim, cells, conv_out, bias_out, new_state, z, flat):
+        here, target, edges, far, near, conv_in, pack, conv_out, sea,
+    )
+
+
+def out_kernel(*refs):
+    *hidden, rim, cells, conv_out, pack, new_state, done, z, flat = refs
     rows, cols, chans = cells.shape
-    hid = hidden.shape[2]
+    hid = rim.shape[2]
     weights = conv_out[...].reshape(5 * chans, hid)
     step = 3
     for j in range(0, rows + 2, step):
-        data = hidden[j : j + step].reshape(step * cols, hid)
+        data = hidden[j // SHARE][j % SHARE : j % SHARE + step].reshape(step * cols, hid)
         got = lax.dot_general(data, weights, NT, preferred_element_type=F32)
         z[j : j + step, 8 : 8 + cols] = got.reshape(step, cols, 5 * chans)
     got = lax.dot_general(rim[...].reshape(4 * LONG, hid), weights, NT, preferred_element_type=F32)
@@ -275,24 +282,25 @@
         total = cut(j, 0, 0) + cut(j - 1, 2, 0) + cut(j + 1, 2, 0)
         total += cut(j, 1, 1) + cut(j + 1, 3, 1) + cut(j - 1, 4, 1)
         total += cut(j, 1, -1) + cut(j - 1, 3, -1) + cut(j + 1, 4, -1)
-        total += bias_out[...] + cells[r].astype(F32)
+        total += pack[:, OUT_AT : OUT_AT + chans] + cells[r].astype(F32)
         flat[pl.ds(r, chans, stride=rows), :] = total.T
     new_state[...] = flat[...].reshape(chans, rows, cols).astype(BF16)
-
-
-def out_part(hidden, rim, cells, conv_out, bias_out):
+    done[...] = jnp.zeros_like(done)
+
+
+def out_part(hidden, rim, cells, conv_out, pack):
     rows, cols, chans = cells.shape
     return call(
         out_kernel,
-        jax.ShapeDtypeStruct((chans, rows, cols), BF16),
+        [jax.ShapeDtypeStruct((chans, rows, cols), BF16), jax.ShapeDtypeStruct((8, cols), F32)],
         [((rows + 2, cols + 16, 5 * chans), F32), ((chans * rows, cols), F32)],
         (2 * 18 * 128 * 640 * 256, 3000000, 0),
         18,
-        hidden, rim, cells, conv_out, bias_out,
-    )
-
-
-def sort_kernel(place, held, sent):
+        *hidden, rim, cells, conv_out, pack,
+    )
+
+
+def sort_kernel(place, held, done, sent):
     count, chans, rows, cols = held.shape
     half = sent.shape[0] // 2
     named = [place[k] for k in range(count)]
@@ -309,9 +317,9 @@
     sent[half:] = jnp.zeros((half,) + sent.shape[1:], BF16)
 
 
-def sort_tiles(place, held, count):
+def sort_tiles(place, held, done, count):
     shape = jax.ShapeDtypeStruct((count,) + held.shape[1:], BF16)
-    return call(sort_kernel, shape, [], (100000, 6 * held.size, 0), 6, place, held)
+    return call(sort_kernel, shape, [], (100000, 6 * held.size, 0), 6, place, held, done)
 
 
 def exchange(values, partner):
@@ -364,14 +372,15 @@
     odd = c % 2 == 1
     got_near = jnp.concatenate([jnp.where(odd, got_near, 0), jnp.where(odd, 0, got_near)])
 
-    target, place = routes(jnp.concatenate([owner, land]), here)
-    bias_in, bias_out = bias_in[None], bias_out[None]
-    wide = cells.astype(F32)
-    hidden, sea = inner_part(here, wide, far_rows, near_rows, conv_in, bias_in, conv_out, bias_out, first)
-    rim, blocks = rim_part(here, target, tall, got_far, got_near, conv_in, bias_in, conv_out, sea, cols, OC)
+    lane = lambda v: jnp.pad(v.astype(F32), ((0, 0), (0, 128 - v.shape[1])))
+    pack = jnp.concatenate([lane(owner), lane(land), bias_in[None], bias_out[None]], axis=1)
+    target, place = routes(pack, here)
+    cells = cells.astype(BF16)
+    *hidden, sea = inner_part(here, cells, far_rows, near_rows, conv_in, pack, conv_out, first)
+    rim, blocks = rim_part(here, target, tall, got_far, got_near, conv_in, pack, conv_out, sea, cols, OC)
     held = lax.all_to_all(blocks, "col", 0, 0, tiled=True)
-    new_state = out_part(hidden, rim, cells, conv_out, bias_out)
-    sent = sort_tiles(place, held, rows * CAP).reshape((rows, CAP, OC, height, width))
+    new_state, done = out_part(hidden, rim, cells, conv_out, pack)
+    sent = sort_tiles(place, held, done, rows * CAP).reshape((rows, CAP, OC, height, width))
     got = lax.all_to_all(sent, "row", 0, 0, tiled=True)
     ocean = jnp.sum(got.astype(F32), axis=0).astype(BF16)
     return (new_state[None], ocean[None, None])

time: 52.6 us -> 52.1 us (level)
  starting transfers between devices: 22.8 us -> 22 us
  blocking collectives: 12.4 us -> 13.2 us
  waiting for transfers between devices: 4.75 us -> 5.52 us
  other arithmetic: 1.45 us -> 0.77 us
  local copies, waits for them, and re-layouts: 2.37 us -> 1.78 us
    all_to_all x1, blocking collectives: 12.4 us -> 13.2 us  [local(): got = lax.all_to_all(sent, 'row', 0, 0, tiled=True)]
    all_to_all x1, waiting for transfers between devices: 4.74 us -> 5.51 us  [local(): held = lax.all_to_all(blocks, 'col', 0, 0, tiled=True)]
    all_to_all x1, starting transfers between devices: 4.82 us -> 4.1 us  [local(): held = lax.all_to_all(blocks, 'col', 0, 0, tiled=True)]
    concatenate x1, other arithmetic: 0.68 us -> 0.01 us  [local(): jnp.concatenate([lane(owner), lane(land), bias_in[None], bias_out[None]],...]
    unnamed x14, local copies, waits for them, and re-layouts: 2.33 us -> 1.73 us
  transfers between devices with their start and end apart: 5 -> 5, of which waited for: 1 -> 1; matrix products, arithmetic and copies ran while one was open for 2% -> 0% of each run, Pallas kernels for 10% -> 11%
where the time goes in v5:
time: 52.1 us; the launch traced here: 51.8 us
  starting transfers between devices  22 us (42%)
  blocking collectives  13.2 us (25%)
  Pallas kernels  7.54 us (14%)
  waiting for transfers between devices  5.52 us (11%)
  local copies, waits for them, and re-layouts  1.78 us (3%)
  between operations  0.92 us (2%)
  other arithmetic  0.77 us (1%)
    ppermute x4, starting transfers between devices, exchange(): return lax.ppermute(values, ALL, pairs)  17.9 us
    all_to_all x1, blocking collectives, local(): got = lax.all_to_all(sent, 'row', 0, 0, tiled=True)  13.2 us
    pallas_call x7, Pallas kernels, call(): pl.pallas_call(kernel, out_shape=out_shape, in_specs=[VM] * len(operands)...  7.54 us
    all_to_all x1, waiting for transfers between devices, local(): held = lax.all_to_all(blocks, 'col', 0, 0, tiled=True)  5.51 us
    all_to_all x1, starting transfers between devices, local(): held = lax.all_to_all(blocks, 'col', 0, 0, tiled=True)  4.1 us
    unnamed x14, local copies, waits for them, and re-layouts  1.73 us
  transfers between devices with their start and end apart: 5, of which 1 were waited for; matrix products, arithmetic and copies ran while one was open for 0% of the time, Pallas kernels for 11%

profile of v5, /device:TPU:1, one launch (start us, length us, event | category | flops | bytes accessed | tf_op | source)
XLA Modules:
  0.0 51.8 jit_solution(721196137419449838)
XLA Ops:
  0.7 0.0 copy-start
  0.8 1.0 %copy-done = bf16[1,128,16,128]{3,2,1,0:T(8,128)(2,1)S(1)} copy-done((bf16[1,128,16,128]{3,2,1,0:T(8,128)(2,1)S(1)}, bf16[1,128,16,128]{3,2,1,0:T(8,128)(2,1)}, u32[]{:S(2)}) %copy-start) | copy-done | bytes 524312
  1.8 0.5 shard_map.86
  2.3 0.0 copy-start.5
  2.3 5.4 %collective-permute-start = (bf16[272,128]{1,0:T(8,128)(2,1)S(1)}, bf16[272,128]{1,0:T(8,128)(2,1)S(1)}, u32[]{:S(2)}, u32[]{:S(2)}) collective-permute-start(bf16[272,128]{1,0:T(8,128)(2,1)S(1)} %get-tuple-element.21), channel_id=1, source_target_pairs={{8,16},{9,17},{10,18},{11,19},{12,20},{13,21},{14,22},{15,23},{16,... | collective-permute-start | bytes 208904 | tf_op jit(solution)/shard_map/ppermute | solution.py:335
  7.7 0.0 copy-start.6
  7.7 4.1 %collective-permute-start.1 = (bf16[272,128]{1,0:T(8,128)(2,1)S(1)}, bf16[272,128]{1,0:T(8,128)(2,1)S(1)}, u32[]{:S(2)}, u32[]{:S(2)}) collective-permute-start(bf16[272,128]{1,0:T(8,128)(2,1)S(1)} %get-tuple-element.22), channel_id=1, source_target_pairs={{0,8},{1,9},{2,10},{3,11},{4,12},{5,13},{6,14},{7,15},{8,0},{9,1},... | collective-permute-start | bytes 208904 | tf_op jit(solution)/shard_map/ppermute | solution.py:335
  11.7 0.0 copy-done.5
  11.8 0.0 copy-done.6
  11.8 0.0 copy-start.3
  11.8 0.0 copy-start.4
  11.8 0.7 %copy-done.3 = f32[256]{0:T(256)S(1)} copy-done((f32[256]{0:T(256)S(1)}, f32[256]{0:T(256)}, u32[]{:S(2)}) %copy-start.3) | copy-done | bytes 1048
  12.5 0.0 copy-done.4
  12.5 0.2 shard_map.88
  12.7 0.0 copy-start.1
  12.7 0.0 copy-start.2
  12.7 0.1 convert_element_type.26.cells.refs_4_
  12.8 0.0 collective-permute-done.got_far
  12.8 0.0 collective-permute-done.1.got_near
  12.9 6.6 %collective-permute-start.2 = (bf16[2,32,128]{2,1,0:T(8,128)(2,1)S(1)}, bf16[2,32,128]{2,1,0:T(8,128)(2,1)S(1)}, u32[]{:S(2)}, u32[]{:S(2)}) collective-permute-start(bf16[2,32,128]{2,1,0:T(8,128)(2,1)S(1)} %get-tuple-element.30), channel_id=1, source_target_pairs={{0,184},{1,2},{2,1},{3,4},{4,3},{5,6},{6,5},{7,127},{8,176},{9,10}... | collective-permute-start | bytes 49160 | tf_op jit(solution)/shard_map/ppermute | solution.py:335
  19.4 1.9 %collective-permute-start.3 = (bf16[2,32,128]{2,1,0:T(8,128)(2,1)S(1)}, bf16[2,32,128]{2,1,0:T(8,128)(2,1)S(1)}, u32[]{:S(2)}, u32[]{:S(2)}) collective-permute-start(bf16[2,32,128]{2,1,0:T(8,128)(2,1)S(1)} %get-tuple-element.31), channel_id=1, source_target_pairs={{0,1},{1,0},{2,3},{3,2},{4,5},{5,4},{6,7},{7,6},{8,9},{9,8},{10,11... | collective-permute-start | bytes 49160 | tf_op jit(solution)/shard_map/ppermute | solution.py:335
  21.3 0.0 copy-done.1
  21.4 0.0 copy-done.2
  21.4 2.6 %shard_map.87 = (bf16[6,128,256]{2,1,0:T(8,128)(2,1)S(1)}, bf16[6,128,256]{2,1,0:T(8,128)(2,1)S(1)}, bf16[6,128,256]{2,1,0:T(8,128)(2,1)S(1)}, f32[8,16,128]{2,1,0:T(8,128)S(1)}) custom-call(s32[8,128]{1,0:T(8,128)S(1)} %concatenate.13.here, bf16[16,128,128]{2,1,0:T(8,128)(2,1)S(1)} %convert_element_type.26.cells.refs_4_, ...), custom_call_target="tpu_custom_call" | custom-call | flops 1453326336 | bytes 3000000 | tf_op jit(solution)/shard_map/pallas_call | solution.py:24
  24.0 0.0 collective-permute-done.3
  24.1 0.0 collective-permute-done.2.far
  24.1 1.3 %shard_map.90 = (bf16[4,32,256]{2,1,0:T(8,128)(2,1)S(1)}, bf16[8,4,16,128]{3,2,1,0:T(8,128)(2,1)}) custom-call(s32[8,128]{1,0:T(8,128)S(1)} %concatenate.13.here, f32[8,128]{1,0:T(8,128)S(1)} %get-tuple-element.27.target, bf16[4,32,128]{2,1,0:T(8,128)(2,1)S(1)} %get-tuple-element.29.edges, bf16[2,32,128]{2,1,0:T(8,128)(2,1)S(1)} %collective-permute-done.2.far, ...), custom_call_target="tpu_custom_call" | custom-call | flops 75497472 | bytes 1500000 | tf_op jit(solution)/shard_map/pallas_call | solution.py:24
  25.4 4.1 %all-to-all-start = ((bf16[8,4,16,128]{3,2,1,0:T(8,128)(2,1)}), bf16[8,4,16,128]{3,2,1,0:T(8,128)(2,1)S(1)}, u32[]{:S(2)}, u32[]{:S(2)}) async-start(bf16[8,4,16,128]{3,2,1,0:T(8,128)(2,1)} %get-tuple-element.36), calls=%async_computation | async-start | bytes 262144 | tf_op jit(solution)/shard_map/all_to_all | solution.py:381
  29.5 2.7 %shard_map.91 = (bf16[128,16,128]{2,1,0:T(8,128)(2,1)}, f32[8,128]{1,0:T(8,128)S(1)}) custom-call(bf16[6,128,256]{2,1,0:T(8,128)(2,1)S(1)} %get-tuple-element.24.refs_0_, bf16[6,128,256]{2,1,0:T(8,128)(2,1)S(1)} %get-tuple-element.25.refs_1_, bf16[6,128,256]{2,1,0:T(8,128)(2,1)S(1)} %get-tuple-element.26.refs_2_, ...), custom_call_target="tpu_custom_call" | custom-call | flops 754974720 | bytes 3000000 | tf_op jit(solution)/shard_map/pallas_call | solution.py:24
  32.2 5.5 %all-to-all-done.held = bf16[8,4,16,128]{3,2,1,0:T(8,128)(2,1)S(1)} async-done(((bf16[8,4,16,128]{3,2,1,0:T(8,128)(2,1)}), bf16[8,4,16,128]{3,2,1,0:T(8,128)(2,1)S(1)}, u32[]{:S(2)}, u32[]{:S(2)}) %all-to-all-start) | async-done | bytes 131104 | tf_op jit(solution)/shard_map/all_to_all | solution.py:381
  37.8 0.1 shard_map.92
  37.9 13.2 %all_to_all.10 = bf16[8,2,4,16,128]{4,3,2,1,0:T(8,128)(2,1)S(1)} all-to-all(bf16[8,2,4,16,128]{4,3,2,1,0:T(8,128)(2,1)S(1)} %bitcast.6), channel_id=1, replica_groups=mesh['face'=8,'row'=8,'col'=8] {'row'}, dimensions={0} | all-to-all | bytes 524288 | tf_op jit(solution)/shard_map/all_to_all | solution.py:384
  51.1 0.7 %reduce_sum.12 = bf16[2,4,16,128]{3,2,1,0:T(8,128)(2,1)} reduce(bf16[8,2,4,16,128]{4,3,2,1,0:T(8,128)(2,1)S(1)} %all_to_all.10, bf16[]{:T(256)} %constant.32.clone.1), dimensions={0}, to_apply=%region_0.1 | reduce | flops 114688 | bytes 294914 | tf_op jit(solution)/shard_map/reduce_sum | solution.py:385
  (14 shorter events, 0.1 us)
Async XLA Ops:
  0.7 1.0 %copy-start = (bf16[1,128,16,128]{3,2,1,0:T(8,128)(2,1)S(1)}, bf16[1,128,16,128]{3,2,1,0:T(8,128)(2,1)}, u32[]{:S(2)}) copy-start(bf16[1,128,16,128]{3,2,1,0:T(8,128)(2,1)} %param.7) | copy-start | bytes 1572868
  2.3 9.5 %copy-start.5 = (s32[1,64]{1,0:T(1,128)S(1)}, s32[1,64]{1,0:T(1,128)}, u32[]{:S(2)}) copy-start(s32[1,64]{1,0:T(1,128)} %param.12) | copy-start | bytes 772
  2.3 10.5 %collective-permute-start = (bf16[272,128]{1,0:T(8,128)(2,1)S(1)}, bf16[272,128]{1,0:T(8,128)(2,1)S(1)}, u32[]{:S(2)}, u32[]{:S(2)}) collective-permute-start(bf16[272,128]{1,0:T(8,128)(2,1)S(1)} %get-tuple-element.21), channel_id=1, source_target_pairs={{8,16},{9,17},{10,18},{11,19},{12,20},{13,21},{14,22},{15,23},{16,... | collective-permute-start | bytes 208904 | tf_op jit(solution)/shard_map/ppermute | solution.py:335
  7.7 4.1 %copy-start.6 = (s32[1,64]{1,0:T(1,128)S(1)}, s32[1,64]{1,0:T(1,128)}, u32[]{:S(2)}) copy-start(s32[1,64]{1,0:T(1,128)} %param.13) | copy-start | bytes 772
  7.7 5.1 %collective-permute-start.1 = (bf16[272,128]{1,0:T(8,128)(2,1)S(1)}, bf16[272,128]{1,0:T(8,128)(2,1)S(1)}, u32[]{:S(2)}, u32[]{:S(2)}) collective-permute-start(bf16[272,128]{1,0:T(8,128)(2,1)S(1)} %get-tuple-element.22), channel_id=1, source_target_pairs={{0,8},{1,9},{2,10},{3,11},{4,12},{5,13},{6,14},{7,15},{8,0},{9,1},... | collective-permute-start | bytes 208904 | tf_op jit(solution)/shard_map/ppermute | solution.py:335
  11.8 0.7 %copy-start.3 = (f32[256]{0:T(256)S(1)}, f32[256]{0:T(256)}, u32[]{:S(2)}) copy-start(f32[256]{0:T(256)} %param.9) | copy-start | bytes 3076
  11.8 0.7 %copy-start.4 = (f32[128]{0:T(128)S(1)}, f32[128]{0:T(128)}, u32[]{:S(2)}) copy-start(f32[128]{0:T(128)} %param.11) | copy-start | bytes 1540
  12.7 8.7 %copy-start.1 = (bf16[5,256,128]{2,1,0:T(8,128)(2,1)S(1)}, bf16[5,256,128]{2,1,0:T(8,128)(2,1)}, u32[]{:S(2)}) copy-start(bf16[5,256,128]{2,1,0:T(8,128)(2,1)} %conv_in.3) | copy-start | bytes 983044
  12.7 8.7 %copy-start.2 = (bf16[5,128,256]{2,1,0:T(8,128)(2,1)S(1)}, bf16[5,128,256]{2,1,0:T(8,128)(2,1)}, u32[]{:S(2)}) copy-start(bf16[5,128,256]{2,1,0:T(8,128)(2,1)} %refs_5_.1) | copy-start | bytes 983044
  12.9 11.2 %collective-permute-start.2 = (bf16[2,32,128]{2,1,0:T(8,128)(2,1)S(1)}, bf16[2,32,128]{2,1,0:T(8,128)(2,1)S(1)}, u32[]{:S(2)}, u32[]{:S(2)}) collective-permute-start(bf16[2,32,128]{2,1,0:T(8,128)(2,1)S(1)} %get-tuple-element.30), channel_id=1, source_target_pairs={{0,184},{1,2},{2,1},{3,4},{4,3},{5,6},{6,5},{7,127},{8,176},{9,10}... | collective-permute-start | bytes 49160 | tf_op jit(solution)/shard_map/ppermute | solution.py:335
  19.4 4.6 %collective-permute-start.3 = (bf16[2,32,128]{2,1,0:T(8,128)(2,1)S(1)}, bf16[2,32,128]{2,1,0:T(8,128)(2,1)S(1)}, u32[]{:S(2)}, u32[]{:S(2)}) collective-permute-start(bf16[2,32,128]{2,1,0:T(8,128)(2,1)S(1)} %get-tuple-element.31), channel_id=1, source_target_pairs={{0,1},{1,0},{2,3},{3,2},{4,5},{5,4},{6,7},{7,6},{8,9},{9,8},{10,11... | collective-permute-start | bytes 49160 | tf_op jit(solution)/shard_map/ppermute | solution.py:335
  25.4 12.3 %all-to-all-start = ((bf16[8,4,16,128]{3,2,1,0:T(8,128)(2,1)}), bf16[8,4,16,128]{3,2,1,0:T(8,128)(2,1)S(1)}, u32[]{:S(2)}, u32[]{:S(2)}) async-start(bf16[8,4,16,128]{3,2,1,0:T(8,128)(2,1)} %get-tuple-element.36), calls=%async_computation | async-start | bytes 262144 | tf_op jit(solution)/shard_map/all_to_all | solution.py:381

commit v6 on v5

--- a/solution.py
+++ b/solution.py
@@ -86,12 +86,11 @@
     tile = lax.broadcasted_iota(jnp.int32, (count, lanes), 0)
     r, c = here[2:3], here[3:4]
     mine = (tile == r * cols + c) & (wet_i > 0)
-    to_col = jnp.sum(jnp.where(mine, (own_i & (cols - 1)) + 1, 0).astype(F32), axis=0, keepdims=True) - 1.0
-    target[...] = jnp.broadcast_to(to_col, target.shape)
-    spot = jnp.where((wet_i > 0) & ((own_i & (cols - 1)) == c), (own_i >> 3) * 2 + slot, -1).astype(F32)
-    total = jnp.full((cols, lanes), 0.0, F32)
-    for k in range(rows):
-        total = jnp.where(r == k, spot[k * cols : (k + 1) * cols], total)
+    to_row = jnp.sum(jnp.where(mine, (own_i >> 3) + 1, 0).astype(F32), axis=0, keepdims=True) - 1.0
+    target[...] = jnp.broadcast_to(to_row, target.shape)
+    held = (wet_i > 0) & ((own_i >> 3) == r) & ((tile & (cols - 1)) == c)
+    spot = jnp.where(held, (own_i & (cols - 1)) * 2 + slot + 1, 0).astype(F32)
+    total = jnp.sum(spot.reshape(rows, cols, lanes), axis=1) - 1.0
     for k in range(cols):
         place[k] = jnp.broadcast_to(total[k : k + 1], place.shape[1:])
 
@@ -302,19 +301,17 @@
 
 def sort_kernel(place, held, done, sent):
     count, chans, rows, cols = held.shape
-    half = sent.shape[0] // 2
     named = [place[k] for k in range(count)]
-    chosen = [[v == p for v in named] for p in range(half)]
+    chosen = [[v == p for v in named] for p in range(sent.shape[0])]
     for o in range(chans):
         for i in range(0, rows, 16):
             parts = [held[k, o, i : i + 16].astype(F32) for k in range(count)]
             parts = [(v[:8], v[8:]) for v in parts]
-            for p in range(half):
+            for p in range(sent.shape[0]):
                 total = [jnp.zeros((8, cols), F32)] * 2
                 for k, v in enumerate(parts):
                     total = [jnp.where(chosen[p][k], x, t) for x, t in zip(v, total)]
                 sent[p, o, i : i + 16] = jnp.concatenate(total).astype(BF16)
-    sent[half:] = jnp.zeros((half,) + sent.shape[1:], BF16)
 
 
 def sort_tiles(place, held, done, count):
@@ -377,11 +374,11 @@
     target, place = routes(pack, here)
     cells = cells.astype(BF16)
     *hidden, sea = inner_part(here, cells, far_rows, near_rows, conv_in, pack, conv_out, first)
-    rim, blocks = rim_part(here, target, tall, got_far, got_near, conv_in, pack, conv_out, sea, cols, OC)
-    held = lax.all_to_all(blocks, "col", 0, 0, tiled=True)
+    rim, blocks = rim_part(here, target, tall, got_far, got_near, conv_in, pack, conv_out, sea, rows, OC)
+    held = lax.all_to_all(blocks, "row", 0, 0, tiled=True)
     new_state, done = out_part(hidden, rim, cells, conv_out, pack)
-    sent = sort_tiles(place, held, done, rows * CAP).reshape((rows, CAP, OC, height, width))
-    got = lax.all_to_all(sent, "row", 0, 0, tiled=True)
+    sent = sort_tiles(place, held, done, cols * CAP).reshape((cols, CAP, OC, height, width))
+    got = lax.all_to_all(sent, "col", 0, 0, tiled=True)
     ocean = jnp.sum(got.astype(F32), axis=0).astype(BF16)
     return (new_state[None], ocean[None, None])
 

time: 52.1 us -> 51.3 us (0.985)
  the two profiles are of different devices: /device:TPU:1 before, /device:TPU:6 now
where the time goes in v6:
time: 51.3 us; the launch traced here: 51 us
  starting transfers between devices  18.1 us (35%)
  blocking collectives  16.7 us (33%)
  Pallas kernels  7.67 us (15%)
  waiting for transfers between devices  5.01 us (10%)
  local copies, waits for them, and re-layouts  1.78 us (3%)
  between operations  0.91 us (2%)
  other arithmetic  0.77 us (2%)
    all_to_all x1, blocking collectives, local(): got = lax.all_to_all(sent, 'col', 0, 0, tiled=True)  16.7 us
    ppermute x4, starting transfers between devices, exchange(): return lax.ppermute(values, ALL, pairs)  14.7 us
    pallas_call x7, Pallas kernels, call(): pl.pallas_call(kernel, out_shape=out_shape, in_specs=[VM] * len(operands)...  7.67 us
    all_to_all x1, waiting for transfers between devices, local(): held = lax.all_to_all(blocks, 'row', 0, 0, tiled=True)  3.97 us
    all_to_all x1, starting transfers between devices, local(): held = lax.all_to_all(blocks, 'row', 0, 0, tiled=True)  3.37 us
    unnamed x14, local copies, waits for them, and re-layouts  1.73 us
    ppermute x4, waiting for transfers between devices, exchange(): return lax.ppermute(values, ALL, pairs)  1.04 us
  transfers between devices with their start and end apart: 5, of which 2 were waited for; matrix products, arithmetic and copies ran while one was open for 0% of the time, Pallas kernels for 11%

profile of v6, /device:TPU:6, one launch (start us, length us, event | category | flops | bytes accessed | tf_op | source)
XLA Modules:
  0.0 51.0 jit_solution(1006164645861988780)
XLA Ops:
  0.7 0.0 copy-start
  0.8 1.0 %copy-done = bf16[1,128,16,128]{3,2,1,0:T(8,128)(2,1)S(1)} copy-done((bf16[1,128,16,128]{3,2,1,0:T(8,128)(2,1)S(1)}, bf16[1,128,16,128]{3,2,1,0:T(8,128)(2,1)}, u32[]{:S(2)}) %copy-start) | copy-done | bytes 524312
  1.8 0.5 shard_map.86
  2.3 0.0 copy-start.5
  2.3 0.7 %collective-permute-start = (bf16[272,128]{1,0:T(8,128)(2,1)S(1)}, bf16[272,128]{1,0:T(8,128)(2,1)S(1)}, u32[]{:S(2)}, u32[]{:S(2)}) collective-permute-start(bf16[272,128]{1,0:T(8,128)(2,1)S(1)} %get-tuple-element.21), channel_id=1, source_target_pairs={{8,16},{9,17},{10,18},{11,19},{12,20},{13,21},{14,22},{15,23},{16,... | collective-permute-start | bytes 208904 | tf_op jit(solution)/shard_map/ppermute | solution.py:332
  2.9 0.0 copy-start.6
  3.0 5.6 %collective-permute-start.1 = (bf16[272,128]{1,0:T(8,128)(2,1)S(1)}, bf16[272,128]{1,0:T(8,128)(2,1)S(1)}, u32[]{:S(2)}, u32[]{:S(2)}) collective-permute-start(bf16[272,128]{1,0:T(8,128)(2,1)S(1)} %get-tuple-element.22), channel_id=1, source_target_pairs={{0,8},{1,9},{2,10},{3,11},{4,12},{5,13},{6,14},{7,15},{8,0},{9,1},... | collective-permute-start | bytes 208904 | tf_op jit(solution)/shard_map/ppermute | solution.py:332
  8.6 0.0 copy-done.5
  8.6 0.0 copy-done.6
  8.6 0.0 copy-start.3
  8.7 0.0 copy-start.4
  8.7 0.7 %copy-done.3 = f32[256]{0:T(256)S(1)} copy-done((f32[256]{0:T(256)S(1)}, f32[256]{0:T(256)}, u32[]{:S(2)}) %copy-start.3) | copy-done | bytes 1048
  9.3 0.0 copy-done.4
  9.3 0.2 shard_map.88
  9.5 0.0 copy-start.1
  9.6 0.0 copy-start.2
  9.6 0.1 convert_element_type.26.cells.refs_4_
  9.7 0.0 collective-permute-done.got_far
  9.7 0.0 collective-permute-done.1.got_near
  9.7 6.5 %collective-permute-start.2 = (bf16[2,32,128]{2,1,0:T(8,128)(2,1)S(1)}, bf16[2,32,128]{2,1,0:T(8,128)(2,1)S(1)}, u32[]{:S(2)}, u32[]{:S(2)}) collective-permute-start(bf16[2,32,128]{2,1,0:T(8,128)(2,1)S(1)} %get-tuple-element.30), channel_id=1, source_target_pairs={{0,184},{1,2},{2,1},{3,4},{4,3},{5,6},{6,5},{7,127},{8,176},{9,10}... | collective-permute-start | bytes 49160 | tf_op jit(solution)/shard_map/ppermute | solution.py:332
  16.2 1.9 %collective-permute-start.3 = (bf16[2,32,128]{2,1,0:T(8,128)(2,1)S(1)}, bf16[2,32,128]{2,1,0:T(8,128)(2,1)S(1)}, u32[]{:S(2)}, u32[]{:S(2)}) collective-permute-start(bf16[2,32,128]{2,1,0:T(8,128)(2,1)S(1)} %get-tuple-element.31), channel_id=1, source_target_pairs={{0,1},{1,0},{2,3},{3,2},{4,5},{5,4},{6,7},{7,6},{8,9},{9,8},{10,11... | collective-permute-start | bytes 49160 | tf_op jit(solution)/shard_map/ppermute | solution.py:332
  18.2 0.0 copy-done.1
  18.2 0.0 copy-done.2
  18.2 2.6 %shard_map.87 = (bf16[6,128,256]{2,1,0:T(8,128)(2,1)S(1)}, bf16[6,128,256]{2,1,0:T(8,128)(2,1)S(1)}, bf16[6,128,256]{2,1,0:T(8,128)(2,1)S(1)}, f32[8,16,128]{2,1,0:T(8,128)S(1)}) custom-call(s32[8,128]{1,0:T(8,128)S(1)} %concatenate.13.here, bf16[16,128,128]{2,1,0:T(8,128)(2,1)S(1)} %convert_element_type.26.cells.refs_4_, ...), custom_call_target="tpu_custom_call" | custom-call | flops 1453326336 | bytes 3000000 | tf_op jit(solution)/shard_map/pallas_call | solution.py:24
  20.8 1.0 %collective-permute-done.3 = bf16[2,32,128]{2,1,0:T(8,128)(2,1)S(1)} collective-permute-done((bf16[2,32,128]{2,1,0:T(8,128)(2,1)S(1)}, bf16[2,32,128]{2,1,0:T(8,128)(2,1)S(1)}, u32[]{:S(2)}, u32[]{:S(2)}) %collective-permute-start.3) | collective-permute-done | bytes 16416 | tf_op jit(solution)/shard_map/ppermute | solution.py:332
  21.9 0.0 collective-permute-done.2.far
  21.9 1.3 %shard_map.90 = (bf16[4,32,256]{2,1,0:T(8,128)(2,1)S(1)}, bf16[8,4,16,128]{3,2,1,0:T(8,128)(2,1)}) custom-call(s32[8,128]{1,0:T(8,128)S(1)} %concatenate.13.here, f32[8,128]{1,0:T(8,128)S(1)} %get-tuple-element.27.target, bf16[4,32,128]{2,1,0:T(8,128)(2,1)S(1)} %get-tuple-element.29.edges, bf16[2,32,128]{2,1,0:T(8,128)(2,1)S(1)} %collective-permute-done.2.far, ...), custom_call_target="tpu_custom_call" | custom-call | flops 75497472 | bytes 1500000 | tf_op jit(solution)/shard_map/pallas_call | solution.py:24
  23.2 3.4 %all-to-all-start = ((bf16[8,4,16,128]{3,2,1,0:T(8,128)(2,1)}), bf16[8,4,16,128]{3,2,1,0:T(8,128)(2,1)S(1)}, u32[]{:S(2)}, u32[]{:S(2)}) async-start(bf16[8,4,16,128]{3,2,1,0:T(8,128)(2,1)} %get-tuple-element.36), calls=%async_computation | async-start | bytes 262144 | tf_op jit(solution)/shard_map/all_to_all | solution.py:378
  26.6 2.7 %shard_map.91 = (bf16[128,16,128]{2,1,0:T(8,128)(2,1)}, f32[8,128]{1,0:T(8,128)S(1)}) custom-call(bf16[6,128,256]{2,1,0:T(8,128)(2,1)S(1)} %get-tuple-element.24.refs_0_, bf16[6,128,256]{2,1,0:T(8,128)(2,1)S(1)} %get-tuple-element.25.refs_1_, bf16[6,128,256]{2,1,0:T(8,128)(2,1)S(1)} %get-tuple-element.26.refs_2_, ...), custom_call_target="tpu_custom_call" | custom-call | flops 754974720 | bytes 3000000 | tf_op jit(solution)/shard_map/pallas_call | solution.py:24
  29.4 4.0 %all-to-all-done.held = bf16[8,4,16,128]{3,2,1,0:T(8,128)(2,1)S(1)} async-done(((bf16[8,4,16,128]{3,2,1,0:T(8,128)(2,1)}), bf16[8,4,16,128]{3,2,1,0:T(8,128)(2,1)S(1)}, u32[]{:S(2)}, u32[]{:S(2)}) %all-to-all-start) | async-done | bytes 131104 | tf_op jit(solution)/shard_map/all_to_all | solution.py:378
  33.3 0.3 shard_map.92
  33.6 16.7 %all_to_all.10 = bf16[8,2,4,16,128]{4,3,2,1,0:T(8,128)(2,1)S(1)} all-to-all(bf16[8,2,4,16,128]{4,3,2,1,0:T(8,128)(2,1)S(1)} %bitcast.6), channel_id=1, replica_groups=mesh['face'=8,'row'=8,'col'=8] {'col'}, dimensions={0} | all-to-all | bytes 524288 | tf_op jit(solution)/shard_map/all_to_all | solution.py:381
  50.3 0.7 %reduce_sum.12 = bf16[2,4,16,128]{3,2,1,0:T(8,128)(2,1)} reduce(bf16[8,2,4,16,128]{4,3,2,1,0:T(8,128)(2,1)S(1)} %all_to_all.10, bf16[]{:T(256)} %constant.32.clone.1), dimensions={0}, to_apply=%region_0.1 | reduce | flops 114688 | bytes 294914 | tf_op jit(solution)/shard_map/reduce_sum | solution.py:382
  (14 shorter events, 0.1 us)
Async XLA Ops:
  0.7 1.0 %copy-start = (bf16[1,128,16,128]{3,2,1,0:T(8,128)(2,1)S(1)}, bf16[1,128,16,128]{3,2,1,0:T(8,128)(2,1)}, u32[]{:S(2)}) copy-start(bf16[1,128,16,128]{3,2,1,0:T(8,128)(2,1)} %param.7) | copy-start | bytes 1572868
  2.3 6.3 %copy-start.5 = (s32[1,64]{1,0:T(1,128)S(1)}, s32[1,64]{1,0:T(1,128)}, u32[]{:S(2)}) copy-start(s32[1,64]{1,0:T(1,128)} %param.12) | copy-start | bytes 772
  2.3 7.4 %collective-permute-start = (bf16[272,128]{1,0:T(8,128)(2,1)S(1)}, bf16[272,128]{1,0:T(8,128)(2,1)S(1)}, u32[]{:S(2)}, u32[]{:S(2)}) collective-permute-start(bf16[272,128]{1,0:T(8,128)(2,1)S(1)} %get-tuple-element.21), channel_id=1, source_target_pairs={{8,16},{9,17},{10,18},{11,19},{12,20},{13,21},{14,22},{15,23},{16,... | collective-permute-start | bytes 208904 | tf_op jit(solution)/shard_map/ppermute | solution.py:332
  2.9 5.7 %copy-start.6 = (s32[1,64]{1,0:T(1,128)S(1)}, s32[1,64]{1,0:T(1,128)}, u32[]{:S(2)}) copy-start(s32[1,64]{1,0:T(1,128)} %param.13) | copy-start | bytes 772
  3.0 6.7 %collective-permute-start.1 = (bf16[272,128]{1,0:T(8,128)(2,1)S(1)}, bf16[272,128]{1,0:T(8,128)(2,1)S(1)}, u32[]{:S(2)}, u32[]{:S(2)}) collective-permute-start(bf16[272,128]{1,0:T(8,128)(2,1)S(1)} %get-tuple-element.22), channel_id=1, source_target_pairs={{0,8},{1,9},{2,10},{3,11},{4,12},{5,13},{6,14},{7,15},{8,0},{9,1},... | collective-permute-start | bytes 208904 | tf_op jit(solution)/shard_map/ppermute | solution.py:332
  8.6 0.7 %copy-start.3 = (f32[256]{0:T(256)S(1)}, f32[256]{0:T(256)}, u32[]{:S(2)}) copy-start(f32[256]{0:T(256)} %param.9) | copy-start | bytes 3076
  8.7 0.7 %copy-start.4 = (f32[128]{0:T(128)S(1)}, f32[128]{0:T(128)}, u32[]{:S(2)}) copy-start(f32[128]{0:T(128)} %param.11) | copy-start | bytes 1540
  9.5 8.6 %copy-start.1 = (bf16[5,256,128]{2,1,0:T(8,128)(2,1)S(1)}, bf16[5,256,128]{2,1,0:T(8,128)(2,1)}, u32[]{:S(2)}) copy-start(bf16[5,256,128]{2,1,0:T(8,128)(2,1)} %conv_in.3) | copy-start | bytes 983044
  9.6 8.6 %copy-start.2 = (bf16[5,128,256]{2,1,0:T(8,128)(2,1)S(1)}, bf16[5,128,256]{2,1,0:T(8,128)(2,1)}, u32[]{:S(2)}) copy-start(bf16[5,128,256]{2,1,0:T(8,128)(2,1)} %refs_5_.1) | copy-start | bytes 983044
  9.7 12.2 %collective-permute-start.2 = (bf16[2,32,128]{2,1,0:T(8,128)(2,1)S(1)}, bf16[2,32,128]{2,1,0:T(8,128)(2,1)S(1)}, u32[]{:S(2)}, u32[]{:S(2)}) collective-permute-start(bf16[2,32,128]{2,1,0:T(8,128)(2,1)S(1)} %get-tuple-element.30), channel_id=1, source_target_pairs={{0,184},{1,2},{2,1},{3,4},{4,3},{5,6},{6,5},{7,127},{8,176},{9,10}... | collective-permute-start | bytes 49160 | tf_op jit(solution)/shard_map/ppermute | solution.py:332
  16.2 5.6 %collective-permute-start.3 = (bf16[2,32,128]{2,1,0:T(8,128)(2,1)S(1)}, bf16[2,32,128]{2,1,0:T(8,128)(2,1)S(1)}, u32[]{:S(2)}, u32[]{:S(2)}) collective-permute-start(bf16[2,32,128]{2,1,0:T(8,128)(2,1)S(1)} %get-tuple-element.31), channel_id=1, source_target_pairs={{0,1},{1,0},{2,3},{3,2},{4,5},{5,4},{6,7},{7,6},{8,9},{9,8},{10,11... | collective-permute-start | bytes 49160 | tf_op jit(solution)/shard_map/ppermute | solution.py:332
  23.2 10.1 %all-to-all-start = ((bf16[8,4,16,128]{3,2,1,0:T(8,128)(2,1)}), bf16[8,4,16,128]{3,2,1,0:T(8,128)(2,1)S(1)}, u32[]{:S(2)}, u32[]{:S(2)}) async-start(bf16[8,4,16,128]{3,2,1,0:T(8,128)(2,1)} %get-tuple-element.36), calls=%async_computation | async-start | bytes 262144 | tf_op jit(solution)/shard_map/all_to_all | solution.py:378
